TPU v7x, 256 devices: a whole 4x4x8 slice. The times are simulated.
256 devices in a mesh: comp: 4 (over z_hi, core), lon: 16 (over x, y), lat: 4 (over z_lo).
Axes of the slice: x: 4, y: 4, z: 8 (z_hi: 2, z_lo: 4; z = z_hi * 4 + z_lo), core: 2. Of those that a mesh axis runs over, the one named last changes fastest.
Arguments:
- component_snapshots: bfloat16 [4, 16, 1440, 512], P('comp', 'lat', 'lon'), may hold values from -6 to 6
- cotangent: bfloat16 [4, 16, 1440, 512], P('comp', 'lat', 'lon'), may hold values from -0.15625 to 0.15625
- land: int32 [16, 1440], P('lat', 'lon'), may hold values 0 or 1
- atmosphere_kernel: float32 [49, 512], replicated, may hold values from -0.875 to 0.875
- atmosphere_gain: float32 [512], replicated, may hold values from 0.1 to 1.9
- atmosphere_expand_weight: bfloat16 [512, 2048], replicated, may hold values from -0.25 to 0.25
- atmosphere_contract_weight: bfloat16 [2048, 512], replicated, may hold values from -0.125 to 0.125
- ocean_kernel: float32 [49, 512], replicated, may hold values from -0.875 to 0.875
- ocean_gain: float32 [512], replicated, may hold values from 0.1 to 1.9
- ocean_expand_weight: bfloat16 [512, 2048], replicated, may hold values from -0.25 to 0.25
- ocean_contract_weight: bfloat16 [2048, 512], replicated, may hold values from -0.125 to 0.125
- marine_to_air_map: bfloat16 [512, 512], replicated, may hold values from -0.25 to 0.25
- flux_weight: bfloat16 [512, 512], replicated, may hold values from -0.25 to 0.25
Outputs:
- outputs: bfloat16 [4, 16, 1440, 512], P('comp', 'lat', 'lon')
- grad_kern_atm: float32 [49, 512], replicated
- grad_gain_atm: float32 [512], replicated
- grad_w_in_atm: float32 [512, 2048], P(('lon', 'lat'))
- grad_w_out_atm: float32 [2048, 512], P(('lon', 'lat'))
- grad_kern_ocn: float32 [49, 512], replicated
- grad_gain_ocn: float32 [512], replicated
- grad_w_in_ocn: float32 [512, 2048], P(('lon', 'lat'))
- grad_w_out_ocn: float32 [2048, 512], P(('lon', 'lat'))
- seasurface_weight_gradient: float32 [512, 512], P(('lon', 'lat'))
- flux_weight_gradient: float32 [512, 512], P(('lon', 'lat'))
Inputs may be any that keep to these rules, and one draw needn't show every extreme that they name: 1 marks land, 0 sea.
All inputs are finite; a program needn't handle non-finite values. No bound on the sum of `land` on one device may be relied on, other than what follows from the above.
Results may differ from a plain program's by a relative error of at most 0.009.
Values may be sent and summed in bfloat16 or wider, within the bound.
No kernel may reach another device: no remote copies, remote signals or barrier semaphores. Data moves between devices by JAX's collectives and lax.ppermute only.
A program may use at most 128 MiB of HBM per device.

v0:
```python
import math

import jax
import jax.numpy as jnp
from jax import lax
from jax.experimental import pallas as pl
from jax.experimental.pallas import tpu as pltpu
from jax.sharding import Mesh
from jax.sharding import PartitionSpec as P

tanh_scale = math.sqrt(2.0 / math.pi)
cubic_term = 0.044715
eps_norm = 1e-06
bf16 = jnp.bfloat16
f32 = jnp.float32

COMP = ("zh", "core")
LON = ("x", "y")


def ring(count, step):
    return [(i, (i + step) % count) for i in range(count)]


def scatter_sum(parts, axis, dim):
    me = lax.axis_index(axis)
    total = lax.dynamic_index_in_dim(parts, me, dim, keepdims=False).astype(f32)
    for step in (1, 2, 3):
        out = lax.dynamic_index_in_dim(parts, lax.rem(me + step, 4), dim, keepdims=False)
        total = total + lax.ppermute(out, axis, ring(4, step)).astype(f32)
    return total


def all_sum(block, axis):
    one, two, three = (lax.ppermute(block, axis, ring(4, step)).astype(f32) for step in (1, 2, 3))
    return (block.astype(f32) + two) + (one + three)


def lat_halo(tile):
    north = lax.ppermute(tile[1:4], "lat", [(i, i + 1) for i in range(3)])
    south = lax.ppermute(tile[0:3], "lat", [(i + 1, i) for i in range(3)])
    return north, south


def picker(rows, cols, group, stride):
    row = lax.broadcasted_iota(jnp.int32, (rows, cols), 0)
    col = lax.broadcasted_iota(jnp.int32, (rows, cols), 1)
    pick = lax.rem(row, group) * stride + lax.div(row, group)
    return (pick == col).astype(f32).astype(bf16)


def mm(a, b, dims=((1,), (0,))):
    return lax.dot_general(a, b, (dims, ((), ())), preferred_element_type=f32)


def block_kernel(
    ocean_ref,
    north_ref,
    own_ref,
    south_ref,
    cot_ref,
    mask_ref,
    kern_ref,
    gain_ref,
    w_in_air,
    w_out_air,
    w_in_sea,
    w_out_sea,
    result_ref,
    gwi_ref,
    gwo_ref,
    small_ref,
    gct_ref,
    w_in,
    w_out,
    taps_in,
    conv,
    normed,
    norm_in,
    norm_in_t,
    gb,
    branch,
    gnorm,
    sems,
):
    @pl.when(ocean_ref[0] == 1)
    def _():
        pltpu.make_async_copy(w_in_sea, w_in, sems.at[0]).start()
        pltpu.make_async_copy(w_out_sea, w_out, sems.at[1]).start()

    @pl.when(ocean_ref[0] == 0)
    def _():
        pltpu.make_async_copy(w_in_air, w_in, sems.at[0]).start()
        pltpu.make_async_copy(w_out_air, w_out, sems.at[1]).start()

    spread = picker(144, 96, 8, 12)
    for r in range(10):
        src = north_ref[r] if r < 3 else own_ref[r - 3] if r < 7 else south_ref[r - 7]
        q = mm(spread, src)
        for lb in range(4):
            taps_in[lb, r] = q[:, lb * 128 : lb * 128 + 128].reshape(18, 8, 128)
    order = picker(96, 96, 8, 12)
    for i in range(4):
        gb[i * 96 : i * 96 + 96, :] = mm(order, cot_ref[i]).astype(bf16)

    def conv_step(n, carry):
        lb, i = lax.div(n, 4), lax.rem(n, 4)
        acc = [None] * 12
        for u in range(7):
            q = [taps_in[lb, i + u, t] for t in range(18)]
            for v in range(7):
                k = kern_ref[lb, pl.ds(u * 7 + v, 1), :]
                for t in range(12):
                    term = k * q[t + v]
                    acc[t] = term if acc[t] is None else acc[t] + term
        lanes = pl.ds(pl.multiple_of(lb * 128, 128), 128)
        for t in range(12):
            conv[pl.ds(pl.multiple_of(i * 96 + t * 8, 8), 8), lanes] = acc[t]
        return carry

    lax.fori_loop(0, 16, conv_step, 0)

    gain = gain_ref[...]
    scales = []
    for i in range(4):
        rows = slice(i * 96, i * 96 + 96)
        c = conv[rows, :]
        centred = c - jnp.mean(c, axis=1, keepdims=True)
        scale = lax.rsqrt(jnp.mean(centred * centred, axis=1, keepdims=True) + eps_norm)
        z = centred * scale
        scales.append(scale)
        normed[rows, :] = z
        norm_in[rows, :] = (z * gain).astype(bf16)
    norm_in_t[...] = norm_in[...].T
    branch[...] = jnp.zeros_like(branch)
    gnorm[...] = jnp.zeros_like(gnorm)
    pltpu.make_async_copy(w_in_air, w_in, sems.at[0]).wait()
    pltpu.make_async_copy(w_out_air, w_out, sems.at[1]).wait()

    def mlp_step(n, carry):
        cols = pl.ds(pl.multiple_of(n * 256, 256), 256)
        wi, wo = w_in[:, cols], w_out[cols, :]
        pre = mm(norm_in[...], wi)
        square = pre * pre
        tangent = jnp.tanh(tanh_scale * (pre + cubic_term * square * pre))
        half = 0.5 * (1.0 + tangent)
        hidden = (pre * half).astype(bf16)
        slope = half + 0.5 * pre * (1.0 - tangent * tangent) * (
            tanh_scale * (1.0 + 3.0 * cubic_term * square)
        )
        gpre = (mm(gb[...], wo, ((1,), (1,))) * slope).astype(bf16)
        branch[...] += mm(hidden, wo)
        gnorm[...] += mm(gpre, wi, ((1,), (1,)))
        gwi_ref[:, cols] = mm(norm_in_t[...], gpre).astype(bf16)
        gwo_ref[cols, :] = mm(hidden, gb[...], ((0,), (0,))).astype(bf16)
        return carry

    lax.fori_loop(0, 8, mlp_step, 0)

    back = picker(96, 96, 12, 8)
    ggain = jnp.zeros((1, 512), f32)
    for i in range(4):
        rows = slice(i * 96, i * 96 + 96)
        field = jnp.concatenate(
            [taps_in[lb, 3 + i, 3:15].reshape(96, 128) for lb in range(4)], axis=1
        )
        m = mask_ref[rows, :]
        res = (field + jnp.concatenate([m] * 4, axis=1) * branch[rows, :]).astype(bf16)
        result_ref[i] = mm(back, res).astype(bf16)[:90]
        g, z = gnorm[rows, :], normed[rows, :]
        ggain = ggain + jnp.sum(g * z, axis=0, keepdims=True)
        g = g * gain
        conv[rows, :] = scales[i] * (
            g - jnp.mean(g, axis=1, keepdims=True) - z * jnp.mean(g * z, axis=1, keepdims=True)
        )

    to_nat = picker(96, 96, 12, 8)
    to_16 = picker(96, 96, 16, 6)
    shuffle = mm(to_16, to_nat).astype(bf16)
    for i in range(4):
        rows = slice(i * 96, i * 96 + 96)
        moved = mm(shuffle, conv[rows, :].astype(bf16)).astype(bf16)
        norm_in[rows, :] = moved
    gct_ref[...] = norm_in[...].T

    def kern_step(n, carry):
        lb, u = lax.div(n, 7), lax.rem(n, 7)
        lanes = pl.ds(pl.multiple_of(lb * 128, 128), 128)
        acc = [jnp.zeros((8, 128), f32)] * 7
        for i in range(4):
            q = [taps_in[lb, i + u, t] for t in range(18)]
            for t in range(12):
                g = conv[i * 96 + t * 8 : i * 96 + t * 8 + 8, lanes]
                for v in range(7):
                    acc[v] = acc[v] + g * q[t + v]
        rows = [jnp.sum(a, axis=0, keepdims=True) for a in acc] + [jnp.zeros((1, 128), f32)]
        small_ref[pl.ds(pl.multiple_of(u * 8, 8), 8), lanes] = jnp.concatenate(rows, axis=0)
        return carry

    lax.fori_loop(0, 28, kern_step, 0)
    small_ref[56:64, :] = jnp.concatenate([ggain, jnp.zeros((7, 512), f32)], axis=0)


def block(ocean, north, own, south, cot, mask, kern, gain, wia, woa, wis, wos):
    vmem = pl.BlockSpec(memory_space=pltpu.VMEM)
    hbm = pl.BlockSpec(memory_space=pl.ANY)
    flops = 2 * 6 * 384 * 512 * 2048
    return pl.pallas_call(
        block_kernel,
        out_shape=(
            jax.ShapeDtypeStruct((4, 90, 512), bf16),
            jax.ShapeDtypeStruct((512, 2048), bf16),
            jax.ShapeDtypeStruct((2048, 512), bf16),
            jax.ShapeDtypeStruct((64, 512), f32),
            jax.ShapeDtypeStruct((512, 384), bf16),
        ),
        in_specs=[pl.BlockSpec(memory_space=pltpu.SMEM)] + [vmem] * 7 + [hbm] * 4,
        out_specs=(vmem,) * 5,
        scratch_shapes=[
            pltpu.VMEM((512, 2048), bf16),
            pltpu.VMEM((2048, 512), bf16),
            pltpu.VMEM((4, 10, 18, 8, 128), f32),
            pltpu.VMEM((384, 512), f32),
            pltpu.VMEM((384, 512), f32),
            pltpu.VMEM((384, 512), bf16),
            pltpu.VMEM((512, 384), bf16),
            pltpu.VMEM((384, 512), bf16),
            pltpu.VMEM((384, 512), f32),
            pltpu.VMEM((384, 512), f32),
            pltpu.SemaphoreType.DMA((2,)),
        ],
        compiler_params=pltpu.CompilerParams(vmem_limit_bytes=40 * 1024 * 1024),
        cost_estimate=pl.CostEstimate(
            flops=flops, bytes_accessed=12 * 1024 * 1024, transcendentals=384 * 2048
        ),
        name="block_kernel",
    )(ocean, north, own, south, cot, mask, kern, gain, wia, woa, wis, wos)


def couple_kernel(north_ref, own_ref, south_ref, gct_ref, cot_ref, kern_ref, scale_ref, out_ref, rows16, acc, cot_t):
    spread = picker(192, 96, 16, 6)
    for r in range(10):
        src = north_ref[r] if r < 3 else own_ref[r - 3] if r < 7 else south_ref[r - 7]
        rows16[r] = mm(spread, src).astype(bf16)
    order = picker(96, 96, 16, 6)
    moved = [mm(order, cot_ref[i]).astype(bf16) for i in range(4)]
    cot_t[...] = jnp.concatenate(moved, axis=0).T
    acc[...] = mm(cot_t[...], rows16[3:7, 48:144, :].reshape(384, 512))

    def step(u, carry):
        for v in range(7):
            part = rows16[pl.ds(u, 4), v * 16 : v * 16 + 96, :].reshape(384, 512)
            k = kern_ref[u, :, v : v + 1]
            acc[...] += k * mm(gct_ref[...], part)
        return carry

    lax.fori_loop(0, 7, step, 0)
    out_ref[...] = (acc[...] * scale_ref[0]).T.astype(bf16)


def couple(north, own, south, gct, cot, kern_t, scale):
    vmem = pl.BlockSpec(memory_space=pltpu.VMEM)
    return pl.pallas_call(
        couple_kernel,
        out_shape=jax.ShapeDtypeStruct((512, 512), bf16),
        in_specs=[vmem] * 6 + [pl.BlockSpec(memory_space=pltpu.SMEM)],
        out_specs=vmem,
        scratch_shapes=[
            pltpu.VMEM((10, 192, 512), bf16),
            pltpu.VMEM((512, 512), f32),
            pltpu.VMEM((512, 384), bf16),
        ],
        compiler_params=pltpu.CompilerParams(vmem_limit_bytes=40 * 1024 * 1024),
        cost_estimate=pl.CostEstimate(
            flops=2 * 50 * 384 * 512 * 512, bytes_accessed=4 * 1024 * 1024, transcendentals=0
        ),
        name="couple_kernel",
    )(north, own, south, gct, cot, kern_t, scale)


def on_device(
    component_snapshots,
    cotangent,
    land,
    atmosphere_kernel,
    atmosphere_gain,
    atmosphere_expand_weight,
    atmosphere_contract_weight,
    ocean_kernel,
    ocean_gain,
    ocean_expand_weight,
    ocean_contract_weight,
    marine_to_air_map,
    flux_weight,
):
    zh, core = lax.axis_index("zh"), lax.axis_index("core")
    is_ocean = (zh == 1) & (core == 1)
    copies = 3.0
    sea = (1 - land).astype(f32)
    local = component_snapshots[0]

    marked = jnp.concatenate(
        [local, jnp.broadcast_to(sea.astype(bf16)[:, :, None], (4, 90, 128))], axis=2
    )
    west = lax.ppermute(marked[:, 87:], LON, ring(16, 1))
    east = lax.ppermute(marked[:, :3], LON, ring(16, -1))
    local = jnp.concatenate([west[:, :, :512], local, east[:, :, :512]], axis=1)
    sea_wide = jnp.concatenate(
        [west[:, :, 512].astype(f32), sea, east[:, :, 512].astype(f32)], axis=1
    )

    beside = lax.ppermute(local, "core", ring(2, 1))
    pair_sum = (local.astype(f32) + beside.astype(f32)).astype(bf16)
    payload = jnp.where(zh == 0, pair_sum, jnp.where(core == 0, beside, local))
    half = lax.dynamic_slice_in_dim(payload, core * 2, 2, axis=0)
    got = lax.ppermute(half, "zh", ring(2, 1))
    got_beside = lax.ppermute(got, "core", ring(2, 1))
    full = jnp.where(
        core == 0,
        jnp.concatenate([got, got_beside], axis=0),
        jnp.concatenate([got_beside, got], axis=0),
    )
    ocean_sum = (full.astype(f32) + beside.astype(f32)).astype(bf16)
    partner = jnp.where(zh == 0, full, jnp.where(core == 0, beside, ocean_sum))

    coupling = jnp.where(is_ocean, flux_weight, marine_to_air_map)
    kernel = jnp.where(is_ocean, ocean_kernel, atmosphere_kernel)
    gain = jnp.where(is_ocean, ocean_gain, atmosphere_gain)
    mask = jnp.where(is_ocean, sea, jnp.ones_like(sea))
    grad_branch = (mask[:, :, None] * cotangent[0].astype(f32)).astype(bf16)
    grad_branch = jnp.pad(grad_branch, ((0, 0), (0, 6), (0, 0)))
    mask = jnp.pad(mask, ((0, 0), (0, 6))).reshape(4, 8, 12).transpose(0, 2, 1).reshape(384, 1)
    mask = jnp.broadcast_to(mask, (384, 128))
    kernel_lanes = kernel.reshape(49, 4, 128).transpose(1, 0, 2)
    kernel_rows = jnp.pad(
        kernel.reshape(7, 7, 512).transpose(0, 2, 1), ((0, 0), (0, 0), (0, 1))
    )

    projected = jnp.dot(partner.reshape(384, 512), coupling, preferred_element_type=f32)
    forcing = jnp.where(is_ocean, projected / copies, projected.astype(bf16).astype(f32))
    field = local.astype(f32) + sea_wide[:, :, None] * forcing.reshape(4, 96, 512)
    field = field.astype(bf16)
    north, south = lat_halo(field)
    masked = (sea_wide[:, :, None] * partner.astype(f32)).astype(bf16)
    masked, north = lax.optimization_barrier((masked, north))
    masked_north, masked_south = lat_halo(masked)

    result, grad_w_in, grad_w_out, small, grad_conv_t = block(
        is_ocean.astype(jnp.int32).reshape(1),
        north,
        field,
        south,
        grad_branch,
        mask,
        kernel_lanes,
        gain[None],
        atmosphere_expand_weight,
        atmosphere_contract_weight,
        ocean_expand_weight,
        ocean_contract_weight,
    )

    in_x = scatter_sum(grad_w_in.reshape(4, 128, 2048), "x", 0).astype(bf16)
    out_y = scatter_sum(grad_w_out.reshape(4, 4, 128, 512), "y", 1).astype(bf16)
    small = all_sum(small.astype(bf16), "x").astype(bf16)

    grad_couple = couple(
        masked_north,
        masked,
        masked_south,
        grad_conv_t,
        grad_branch,
        kernel_rows,
        jnp.where(is_ocean, 1.0 / copies, 1.0).astype(f32).reshape(1),
    )
    gathered = lax.all_to_all(grad_couple.reshape(16, 32, 512), LON, 0, 0, tiled=True)
    in_xy = scatter_sum(in_x.reshape(4, 32, 2048), "y", 0).astype(bf16)
    out_xy = scatter_sum(out_y, "x", 0).astype(bf16)
    small = all_sum(small, "y").astype(bf16)
    gathered = jnp.sum(gathered.astype(f32), axis=0).astype(bf16)

    pieces = jnp.concatenate(
        [
            in_xy.reshape(4, 32, 512),
            out_xy.reshape(4, 32, 512),
            gathered.reshape(4, 8, 512),
            jnp.broadcast_to(small[None], (4, 64, 512)),
        ],
        axis=1,
    )
    column = lax.all_to_all(
        jnp.concatenate([pieces, pieces], axis=0), ("zh", "lat"), 0, 0, tiled=True
    ).astype(f32)
    sums = jnp.stack([jnp.sum(column[:4], axis=0), jnp.sum(column[4:], axis=0)])
    sums_beside = lax.ppermute(sums, "core", ring(2, 1))
    first = jnp.where(core == 0, sums, sums_beside)
    second = jnp.where(core == 0, sums_beside, sums)
    air = (first[0] + first[1]) + second[0]
    sea_part = second[1]

    def split(total):
        return (
            total[72:128].reshape(7, 8, 512)[:, :7].reshape(49, 512),
            total[128],
            total[:32].reshape(8, 2048),
            total[32:64],
        )

    return (
        (result[None],)
        + split(air)
        + split(sea_part)
        + (air[64:72], sea_part[64:72])
    )


def solution(mesh):
    fine = Mesh(mesh.devices.reshape(2, 2, 4, 4, 4), ("zh", "core", "x", "y", "lat"))
    state = P(COMP, "lat", LON, None)
    rows = P(("x", "y", "lat"), None)
    in_specs = (state, state, P("lat", LON)) + (P(),) * 10
    out_specs = (state, P(), P(), rows, rows, P(), P(), rows, rows, rows, rows)
    return jax.shard_map(
        on_device, mesh=fine, in_specs=in_specs, out_specs=out_specs, check_vma=False
    )
```

profile of v0, /device:TPU:1, one launch (start us, length us, event | category | flops | bytes accessed | tf_op | source)
XLA Modules:
  0.0 187.9 jit_solution(1795820659927253776)
XLA Ops:
  2.6 2.2 %collective-permute-start = (bf16[4,3,640]{2,1,0:T(4,128)(2,1)S(1)}, bf16[4,3,640]{2,1,0:T(4,128)(2,1)S(1)}, u32[]{:S(2)}, u32[]{:S(2)}) collective-permute-start(bf16[4,3,640]{2,1,0:T(4,128)(2,1)S(1)} %get-tuple-element.80), channel_id=1, source_target_pairs={{0,4},{4,8},{8,12},{12,16},{16,20},{20,24},{24,28},{28,32},{32,36}... | collective-permute-start | bytes 46088 | tf_op jit(solution)/shard_map/ppermute | solution.py:305
  4.8 3.7 %collective-permute-start.1 = (bf16[4,3,640]{2,1,0:T(4,128)(2,1)S(1)}, bf16[4,3,640]{2,1,0:T(4,128)(2,1)S(1)}, u32[]{:S(2)}, u32[]{:S(2)}) collective-permute-start(bf16[4,3,640]{2,1,0:T(4,128)(2,1)S(1)} %get-tuple-element.81), channel_id=1, source_target_pairs={{0,60},{4,0},{8,4},{12,8},{16,12},{20,16},{24,20},{28,24},{32,28},... | collective-permute-start | bytes 46088 | tf_op jit(solution)/shard_map/ppermute | solution.py:306
  9.8 3.5 %collective-permute-start.2 = (bf16[4,96,512]{2,1,0:T(8,128)(2,1)S(1)}, bf16[4,96,512]{2,1,0:T(8,128)(2,1)S(1)}, u32[]{:S(2)}, u32[]{:S(2)}) collective-permute-start(bf16[4,96,512]{2,1,0:T(8,128)(2,1)S(1)} %get-tuple-element.63), channel_id=1, source_target_pairs={{0,64},{64,0},{1,65},{65,1},{2,66},{66,2},{3,67},{67,3},{4,68},{68... | collective-permute-start | bytes 1179656 | tf_op jit(solution)/shard_map/ppermute | solution.py:312
  13.3 1.3 collective-permute-done.2
  14.8 5.3 %collective-permute-start.3 = (bf16[2,96,512]{2,1,0:T(8,128)(2,1)S(1)}, bf16[2,96,512]{2,1,0:T(8,128)(2,1)S(1)}, u32[]{:S(2)}, u32[]{:S(2)}) collective-permute-start(bf16[2,96,512]{2,1,0:T(8,128)(2,1)S(1)} %fusion.21), channel_id=1, source_target_pairs={{0,128},{128,0},{1,129},{129,1},{2,130},{130,2},{3,131},{131,3},{4... | collective-permute-start | bytes 589832 | tf_op jit(solution)/shard_map/ppermute | solution.py:316
  21.0 3.9 %collective-permute-done.3 = bf16[2,96,512]{2,1,0:T(8,128)(2,1)S(1)} collective-permute-done((bf16[2,96,512]{2,1,0:T(8,128)(2,1)S(1)}, bf16[2,96,512]{2,1,0:T(8,128)(2,1)S(1)}, u32[]{:S(2)}, u32[]{:S(2)}) %collective-permute-start.3) | collective-permute-done | bytes 196640 | tf_op jit(solution)/shard_map/ppermute | solution.py:316
  24.9 2.4 %collective-permute-start.4 = (bf16[2,96,512]{2,1,0:T(8,128)(2,1)S(1)}, bf16[2,96,512]{2,1,0:T(8,128)(2,1)S(1)}, u32[]{:S(2)}, u32[]{:S(2)}) collective-permute-start(bf16[2,96,512]{2,1,0:T(8,128)(2,1)S(1)} %collective-permute-done.3), channel_id=1, source_target_pairs={{0,64},{64,0},{1,65},{65,1},{2,66},{66,2},{3,67},{67,3},{4,68},{68... | collective-permute-start | bytes 589832 | tf_op jit(solution)/shard_map/ppermute | solution.py:317
  30.1 5.5 %collective-permute-start.5 = (bf16[3,96,512]{2,1,0:T(8,128)(2,1)}, bf16[3,96,512]{2,1,0:T(8,128)(2,1)S(1)}, u32[]{:S(2)}, u32[]{:S(2)}) collective-permute-start(bf16[3,96,512]{2,1,0:T(8,128)(2,1)} %get-tuple-element.85), channel_id=1, source_target_pairs={{0,1},{1,2},{2,3},{4,5},{5,6},{6,7},{8,9},{9,10},{10,11},{12,13},{... | collective-permute-start | bytes 884744 | tf_op jit(solution)/shard_map/ppermute | solution.py:40
  38.0 1.4 pad.14.kern_ref
  40.2 1.8 collective-permute-done.5.north_ref
  42.7 3.0 %collective-permute-done.6.south_ref = bf16[3,96,512]{2,1,0:T(8,128)(2,1)S(1)} collective-permute-done((bf16[3,96,512]{2,1,0:T(8,128)(2,1)}, bf16[3,96,512]{2,1,0:T(8,128)(2,1)S(1)}, u32[]{:S(2)}, u32[]{:S(2)}) %collective-permute-start.6) | collective-permute-done | bytes 294944 | tf_op jit(solution)/shard_map/ppermute | solution.py:41
  47.5 1.6 copy-done.3
  49.1 1.6 copy-done.4
  50.7 1.6 copy-done.5
  54.2 16.5 %block_kernel.1 = (bf16[4,90,512]{2,1,0:T(8,128)(2,1)S(1)}, bf16[512,2048]{1,0:T(8,128)(2,1)S(1)}, bf16[2048,512]{1,0:T(8,128)(2,1)S(1)}, f32[64,512]{1,0:T(8,128)S(1)}, bf16[512,384]{1,0:T(8,128)(2,1)S(1)}) custom-call(s32[1]{0:T(128)} %bitcast.ocean_ref, bf16[3,96,512]{2,1,0:T(8,128)(2,1)S(1)} %copy-done.7, ...), custom_call_target="tpu_custom_call" | custom-call | flops 4831838208 | bytes 12582912 | tf_op jit(solution)/shard_map/block_kernel/pallas_call | solution.py:208
  70.7 1.6 collective-permute-start.21
  72.7 2.4 %collective-permute-start.23 = (bf16[64,512]{1,0:T(8,128)(2,1)S(1)}, bf16[64,512]{1,0:T(8,128)(2,1)S(1)}, u32[]{:S(2)}, u32[]{:S(2)}) collective-permute-start(bf16[64,512]{1,0:T(8,128)(2,1)S(1)} %convert_element_type.219), channel_id=1, source_target_pairs={{0,48},{16,0},{32,16},{48,32},{1,49},{17,1},{33,17},{49,33},{2,50}... | collective-permute-start | bytes 196616 | tf_op jit(solution)/shard_map/ppermute | solution.py:35
  75.1 3.0 %collective-permute-start.19 = (bf16[3,96,512]{2,1,0:T(8,128)(2,1)S(1)}, bf16[3,96,512]{2,1,0:T(8,128)(2,1)S(1)}, u32[]{:S(2)}, u32[]{:S(2)}) collective-permute-start(bf16[3,96,512]{2,1,0:T(8,128)(2,1)S(1)} %get-tuple-element.83), channel_id=1, source_target_pairs={{0,1},{1,2},{2,3},{4,5},{5,6},{6,7},{8,9},{9,10},{10,11},{12,13},{... | collective-permute-start | bytes 884744 | tf_op jit(solution)/shard_map/ppermute | solution.py:40
  80.7 2.1 %collective-permute-start.24 = (bf16[64,512]{1,0:T(8,128)(2,1)S(1)}, bf16[64,512]{1,0:T(8,128)(2,1)S(1)}, u32[]{:S(2)}, u32[]{:S(2)}) collective-permute-start(bf16[64,512]{1,0:T(8,128)(2,1)S(1)} %add_convert_fusion.3), channel_id=1, source_target_pairs={{0,8},{4,12},{8,0},{12,4},{1,9},{5,13},{9,1},{13,5},{2,10},{6,14},... | collective-permute-start | bytes 196616 | tf_op jit(solution)/shard_map/ppermute | solution.py:35
  82.9 2.1 %collective-permute-start.25 = (bf16[64,512]{1,0:T(8,128)(2,1)S(1)}, bf16[64,512]{1,0:T(8,128)(2,1)S(1)}, u32[]{:S(2)}, u32[]{:S(2)}) collective-permute-start(bf16[64,512]{1,0:T(8,128)(2,1)S(1)} %add_convert_fusion.3), channel_id=1, source_target_pairs={{0,4},{4,8},{8,12},{12,0},{1,5},{5,9},{9,13},{13,1},{2,6},{6,10},{... | collective-permute-start | bytes 196616 | tf_op jit(solution)/shard_map/ppermute | solution.py:35
  90.5 2.6 %collective-permute-start.14 = (bf16[4,128,512]{2,1,0:T(8,128)(2,1)}, bf16[4,128,512]{2,1,0:T(8,128)(2,1)}, u32[]{:S(2)}, u32[]{:S(2)}) collective-permute-start(bf16[4,128,512]{2,1,0:T(8,128)(2,1)} %get-tuple-element.69), channel_id=1, source_target_pairs={{0,8},{4,12},{8,0},{12,4},{1,9},{5,13},{9,1},{13,5},{2,10},{6,14},... | collective-permute-start | bytes 1572872 | tf_op jit(solution)/shard_map/ppermute | solution.py:30
  93.1 16.7 %couple_kernel.1 = bf16[512,512]{1,0:T(8,128)(2,1)} custom-call(bf16[3,96,512]{2,1,0:T(8,128)(2,1)S(1)} %collective-permute-done.19.north_ref, bf16[4,96,512]{2,1,0:T(8,128)(2,1)S(1)} %get-tuple-element.22.own_ref, bf16[3,96,512]{2,1,0:T(8,128)(2,1)S(1)} %collective-permute-done.20.south_ref, bf16[512,384]{1,0:T(8,128)(2,1)S(1)} %get-tuple-element.23.gct_ref, ...), custom_call_target="tpu_custom_call" | custom-call | flops 10066329600 | bytes 4194304 | tf_op jit(solution)/shard_map/couple_kernel/pallas_call | solution.py:263
  109.8 4.2 %all-to-all-start = ((bf16[16,32,512]{2,1,0:T(8,128)(2,1)}), bf16[16,32,512]{2,1,0:T(8,128)(2,1)}, u32[]{:S(2)}, u32[]{:S(2)}) async-start(bf16[16,32,512]{2,1,0:T(8,128)(2,1)} %bitcast.31), calls=%async_computation | async-start | bytes 1048576 | tf_op jit(solution)/shard_map/all_to_all | solution.py:376
  114.1 2.5 %collective-permute-start.15 = (bf16[4,128,512]{2,1,0:T(8,128)(2,1)}, bf16[4,128,512]{2,1,0:T(8,128)(2,1)S(1)}, u32[]{:S(2)}, u32[]{:S(2)}) collective-permute-start(bf16[4,128,512]{2,1,0:T(8,128)(2,1)} %get-tuple-element.68), channel_id=1, source_target_pairs={{0,12},{4,0},{8,4},{12,8},{1,13},{5,1},{9,5},{13,9},{2,14},{6,2},{... | collective-permute-start | bytes 1572872 | tf_op jit(solution)/shard_map/ppermute | solution.py:30
  116.5 1.9 fusion.5
  118.5 1.7 collective-permute-start.11
  121.2 10.1 %collective-permute-done.15 = bf16[4,128,512]{2,1,0:T(8,128)(2,1)S(1)} collective-permute-done((bf16[4,128,512]{2,1,0:T(8,128)(2,1)}, bf16[4,128,512]{2,1,0:T(8,128)(2,1)S(1)}, u32[]{:S(2)}, u32[]{:S(2)}) %collective-permute-start.15) | collective-permute-done | bytes 524320 | tf_op jit(solution)/shard_map/ppermute | solution.py:30
  131.3 1.5 fusion.2
  133.7 2.5 %collective-permute-start.17 = (bf16[128,512]{1,0:T(8,128)(2,1)S(1)}, bf16[128,512]{1,0:T(8,128)(2,1)S(1)}, u32[]{:S(2)}, u32[]{:S(2)}) collective-permute-start(bf16[128,512]{1,0:T(8,128)(2,1)S(1)} %get-tuple-element.79), channel_id=1, source_target_pairs={{0,32},{16,48},{32,0},{48,16},{1,33},{17,49},{33,1},{49,17},{2,34}... | collective-permute-start | bytes 393224 | tf_op jit(solution)/shard_map/ppermute | solution.py:30
  137.5 2.6 %collective-permute-done.16 = bf16[128,512]{1,0:T(8,128)(2,1)S(1)} collective-permute-done((bf16[128,512]{1,0:T(8,128)(2,1)S(1)}, bf16[128,512]{1,0:T(8,128)(2,1)S(1)}, u32[]{:S(2)}, u32[]{:S(2)}) %collective-permute-start.16) | collective-permute-done | bytes 131104 | tf_op jit(solution)/shard_map/ppermute | solution.py:30
  142.9 26.8 %all_to_all.10 = bf16[8,136,512]{2,1,0:T(8,128)(2,1)S(1)} all-to-all(bf16[8,136,512]{2,1,0:T(8,128)(2,1)S(1)} %maximum_maximum_fusion), channel_id=1, replica_groups=mesh['zh'=2,'core'=2,'x'=4,'y'=4,'lat'=4] {'zh','lat'}, dimensions={0} | all-to-all | bytes 2228224 | tf_op jit(solution)/shard_map/all_to_all | solution.py:391
  170.2 10.8 %collective-permute-start.27 = (f32[2,136,512]{2,1,0:T(8,128)S(1)}, f32[2,136,512]{2,1,0:T(8,128)S(1)}, u32[]{:S(2)}, u32[]{:S(2)}) collective-permute-start(f32[2,136,512]{2,1,0:T(8,128)S(1)} %pad_maximum_fusion), channel_id=1, source_target_pairs={{0,64},{64,0},{1,65},{65,1},{2,66},{66,2},{3,67},{67,3},{4,68},{68... | collective-permute-start | bytes 1671176 | tf_op jit(solution)/shard_map/ppermute | solution.py:395
  (132 shorter events, 36.5 us)
Async XLA Ops:
  0.6 12.6 %copy-start.15 = (s32[4,90]{1,0:T(4,128)S(1)}, s32[4,90]{1,0:T(4,128)}, u32[]{:S(2)}) copy-start(s32[4,90]{1,0:T(4,128)} %param.15) | copy-start | bytes 4324
  2.6 7.0 %collective-permute-start = (bf16[4,3,640]{2,1,0:T(4,128)(2,1)S(1)}, bf16[4,3,640]{2,1,0:T(4,128)(2,1)S(1)}, u32[]{:S(2)}, u32[]{:S(2)}) collective-permute-start(bf16[4,3,640]{2,1,0:T(4,128)(2,1)S(1)} %get-tuple-element.80), channel_id=1, source_target_pairs={{0,4},{4,8},{8,12},{12,16},{16,20},{20,24},{24,28},{28,32},{32,36}... | collective-permute-start | bytes 46088 | tf_op jit(solution)/shard_map/ppermute | solution.py:305
  4.8 4.8 %collective-permute-start.1 = (bf16[4,3,640]{2,1,0:T(4,128)(2,1)S(1)}, bf16[4,3,640]{2,1,0:T(4,128)(2,1)S(1)}, u32[]{:S(2)}, u32[]{:S(2)}) collective-permute-start(bf16[4,3,640]{2,1,0:T(4,128)(2,1)S(1)} %get-tuple-element.81), channel_id=1, source_target_pairs={{0,60},{4,0},{8,4},{12,8},{16,12},{20,16},{24,20},{28,24},{32,28},... | collective-permute-start | bytes 46088 | tf_op jit(solution)/shard_map/ppermute | solution.py:306
  9.8 4.8 %collective-permute-start.2 = (bf16[4,96,512]{2,1,0:T(8,128)(2,1)S(1)}, bf16[4,96,512]{2,1,0:T(8,128)(2,1)S(1)}, u32[]{:S(2)}, u32[]{:S(2)}) collective-permute-start(bf16[4,96,512]{2,1,0:T(8,128)(2,1)S(1)} %get-tuple-element.63), channel_id=1, source_target_pairs={{0,64},{64,0},{1,65},{65,1},{2,66},{66,2},{3,67},{67,3},{4,68},{68... | collective-permute-start | bytes 1179656 | tf_op jit(solution)/shard_map/ppermute | solution.py:312
  14.7 13.9 %copy-start.18 = (bf16[512,512]{1,0:T(8,128)(2,1)S(1)}, bf16[512,512]{1,0:T(8,128)(2,1)}, u32[]{:S(2)}) copy-start(bf16[512,512]{1,0:T(8,128)(2,1)} %param.25) | copy-start | bytes 1572868
  14.7 13.9 %copy-start.19 = (bf16[512,512]{1,0:T(8,128)(2,1)S(1)}, bf16[512,512]{1,0:T(8,128)(2,1)}, u32[]{:S(2)}) copy-start(bf16[512,512]{1,0:T(8,128)(2,1)} %param.24) | copy-start | bytes 1572868
  14.8 10.1 %collective-permute-start.3 = (bf16[2,96,512]{2,1,0:T(8,128)(2,1)S(1)}, bf16[2,96,512]{2,1,0:T(8,128)(2,1)S(1)}, u32[]{:S(2)}, u32[]{:S(2)}) collective-permute-start(bf16[2,96,512]{2,1,0:T(8,128)(2,1)S(1)} %fusion.21), channel_id=1, source_target_pairs={{0,128},{128,0},{1,129},{129,1},{2,130},{130,2},{3,131},{131,3},{4... | collective-permute-start | bytes 589832 | tf_op jit(solution)/shard_map/ppermute | solution.py:316
  24.9 3.4 %collective-permute-start.4 = (bf16[2,96,512]{2,1,0:T(8,128)(2,1)S(1)}, bf16[2,96,512]{2,1,0:T(8,128)(2,1)S(1)}, u32[]{:S(2)}, u32[]{:S(2)}) collective-permute-start(bf16[2,96,512]{2,1,0:T(8,128)(2,1)S(1)} %collective-permute-done.3), channel_id=1, source_target_pairs={{0,64},{64,0},{1,65},{65,1},{2,66},{66,2},{3,67},{67,3},{4,68},{68... | collective-permute-start | bytes 589832 | tf_op jit(solution)/shard_map/ppermute | solution.py:317
  30.1 11.9 %collective-permute-start.5 = (bf16[3,96,512]{2,1,0:T(8,128)(2,1)}, bf16[3,96,512]{2,1,0:T(8,128)(2,1)S(1)}, u32[]{:S(2)}, u32[]{:S(2)}) collective-permute-start(bf16[3,96,512]{2,1,0:T(8,128)(2,1)} %get-tuple-element.85), channel_id=1, source_target_pairs={{0,1},{1,2},{2,3},{4,5},{5,6},{6,7},{8,9},{9,10},{10,11},{12,13},{... | collective-permute-start | bytes 884744 | tf_op jit(solution)/shard_map/ppermute | solution.py:40
  35.6 10.0 %collective-permute-start.6 = (bf16[3,96,512]{2,1,0:T(8,128)(2,1)}, bf16[3,96,512]{2,1,0:T(8,128)(2,1)S(1)}, u32[]{:S(2)}, u32[]{:S(2)}) collective-permute-start(bf16[3,96,512]{2,1,0:T(8,128)(2,1)} %get-tuple-element.84), channel_id=1, source_target_pairs={{1,0},{2,1},{3,2},{5,4},{6,5},{7,6},{9,8},{10,9},{11,10},{13,12},{... | collective-permute-start | bytes 884744 | tf_op jit(solution)/shard_map/ppermute | solution.py:41
  70.7 9.9 %collective-permute-start.21 = (bf16[64,512]{1,0:T(8,128)(2,1)S(1)}, bf16[64,512]{1,0:T(8,128)(2,1)S(1)}, u32[]{:S(2)}, u32[]{:S(2)}) collective-permute-start(bf16[64,512]{1,0:T(8,128)(2,1)S(1)} %convert_element_type.219), channel_id=1, source_target_pairs={{0,32},{16,48},{32,0},{48,16},{1,33},{17,49},{33,1},{49,17},{2,34}... | collective-permute-start | bytes 196616 | tf_op jit(solution)/shard_map/ppermute | solution.py:35
  72.4 8.3 %collective-permute-start.22 = (bf16[64,512]{1,0:T(8,128)(2,1)S(1)}, bf16[64,512]{1,0:T(8,128)(2,1)S(1)}, u32[]{:S(2)}, u32[]{:S(2)}) collective-permute-start(bf16[64,512]{1,0:T(8,128)(2,1)S(1)} %convert_element_type.219), channel_id=1, source_target_pairs={{0,16},{16,32},{32,48},{48,0},{1,17},{17,33},{33,49},{49,1},{2,18}... | collective-permute-start | bytes 196616 | tf_op jit(solution)/shard_map/ppermute | solution.py:35
  72.7 8.0 %collective-permute-start.23 = (bf16[64,512]{1,0:T(8,128)(2,1)S(1)}, bf16[64,512]{1,0:T(8,128)(2,1)S(1)}, u32[]{:S(2)}, u32[]{:S(2)}) collective-permute-start(bf16[64,512]{1,0:T(8,128)(2,1)S(1)} %convert_element_type.219), channel_id=1, source_target_pairs={{0,48},{16,0},{32,16},{48,32},{1,49},{17,1},{33,17},{49,33},{2,50}... | collective-permute-start | bytes 196616 | tf_op jit(solution)/shard_map/ppermute | solution.py:35
  75.1 14.5 %collective-permute-start.19 = (bf16[3,96,512]{2,1,0:T(8,128)(2,1)S(1)}, bf16[3,96,512]{2,1,0:T(8,128)(2,1)S(1)}, u32[]{:S(2)}, u32[]{:S(2)}) collective-permute-start(bf16[3,96,512]{2,1,0:T(8,128)(2,1)S(1)} %get-tuple-element.83), channel_id=1, source_target_pairs={{0,1},{1,2},{2,3},{4,5},{5,6},{6,7},{8,9},{9,10},{10,11},{12,13},{... | collective-permute-start | bytes 884744 | tf_op jit(solution)/shard_map/ppermute | solution.py:40
  78.1 12.4 %collective-permute-start.20 = (bf16[3,96,512]{2,1,0:T(8,128)(2,1)S(1)}, bf16[3,96,512]{2,1,0:T(8,128)(2,1)S(1)}, u32[]{:S(2)}, u32[]{:S(2)}) collective-permute-start(bf16[3,96,512]{2,1,0:T(8,128)(2,1)S(1)} %get-tuple-element.82), channel_id=1, source_target_pairs={{1,0},{2,1},{3,2},{5,4},{6,5},{7,6},{9,8},{10,9},{11,10},{13,12},{... | collective-permute-start | bytes 884744 | tf_op jit(solution)/shard_map/ppermute | solution.py:41
  80.7 6.0 %collective-permute-start.24 = (bf16[64,512]{1,0:T(8,128)(2,1)S(1)}, bf16[64,512]{1,0:T(8,128)(2,1)S(1)}, u32[]{:S(2)}, u32[]{:S(2)}) collective-permute-start(bf16[64,512]{1,0:T(8,128)(2,1)S(1)} %add_convert_fusion.3), channel_id=1, source_target_pairs={{0,8},{4,12},{8,0},{12,4},{1,9},{5,13},{9,1},{13,5},{2,10},{6,14},... | collective-permute-start | bytes 196616 | tf_op jit(solution)/shard_map/ppermute | solution.py:35
  82.9 4.3 %collective-permute-start.25 = (bf16[64,512]{1,0:T(8,128)(2,1)S(1)}, bf16[64,512]{1,0:T(8,128)(2,1)S(1)}, u32[]{:S(2)}, u32[]{:S(2)}) collective-permute-start(bf16[64,512]{1,0:T(8,128)(2,1)S(1)} %add_convert_fusion.3), channel_id=1, source_target_pairs={{0,4},{4,8},{8,12},{12,0},{1,5},{5,9},{9,13},{13,1},{2,6},{6,10},{... | collective-permute-start | bytes 196616 | tf_op jit(solution)/shard_map/ppermute | solution.py:35
  85.0 3.4 %collective-permute-start.26 = (bf16[64,512]{1,0:T(8,128)(2,1)S(1)}, bf16[64,512]{1,0:T(8,128)(2,1)S(1)}, u32[]{:S(2)}, u32[]{:S(2)}) collective-permute-start(bf16[64,512]{1,0:T(8,128)(2,1)S(1)} %add_convert_fusion.3), channel_id=1, source_target_pairs={{0,12},{4,0},{8,4},{12,8},{1,13},{5,1},{9,5},{13,9},{2,14},{6,2},{... | collective-permute-start | bytes 196616 | tf_op jit(solution)/shard_map/ppermute | solution.py:35
  86.7 27.3 %collective-permute-start.7 = (bf16[128,2048]{1,0:T(8,128)(2,1)}, bf16[128,2048]{1,0:T(8,128)(2,1)}, u32[]{:S(2)}, u32[]{:S(2)}) collective-permute-start(bf16[128,2048]{1,0:T(8,128)(2,1)} %get-tuple-element.64), channel_id=1, source_target_pairs={{0,16},{16,32},{32,48},{48,0},{1,17},{17,33},{33,49},{49,1},{2,18}... | collective-permute-start | bytes 1572872 | tf_op jit(solution)/shard_map/ppermute | solution.py:30
  87.2 29.4 %collective-permute-start.8 = (bf16[128,2048]{1,0:T(8,128)(2,1)}, bf16[128,2048]{1,0:T(8,128)(2,1)}, u32[]{:S(2)}, u32[]{:S(2)}) collective-permute-start(bf16[128,2048]{1,0:T(8,128)(2,1)} %get-tuple-element.66), channel_id=1, source_target_pairs={{0,32},{16,48},{32,0},{48,16},{1,33},{17,49},{33,1},{49,17},{2,34}... | collective-permute-start | bytes 1572872 | tf_op jit(solution)/shard_map/ppermute | solution.py:30
  88.4 28.2 %collective-permute-start.9 = (bf16[128,2048]{1,0:T(8,128)(2,1)}, bf16[128,2048]{1,0:T(8,128)(2,1)}, u32[]{:S(2)}, u32[]{:S(2)}) collective-permute-start(bf16[128,2048]{1,0:T(8,128)(2,1)} %get-tuple-element.65), channel_id=1, source_target_pairs={{0,48},{16,0},{32,16},{48,32},{1,49},{17,1},{33,17},{49,33},{2,50}... | collective-permute-start | bytes 1572872 | tf_op jit(solution)/shard_map/ppermute | solution.py:30
  89.6 30.7 %collective-permute-start.13 = (bf16[4,128,512]{2,1,0:T(8,128)(2,1)}, bf16[4,128,512]{2,1,0:T(8,128)(2,1)}, u32[]{:S(2)}, u32[]{:S(2)}) collective-permute-start(bf16[4,128,512]{2,1,0:T(8,128)(2,1)} %get-tuple-element.67), channel_id=1, source_target_pairs={{0,4},{4,8},{8,12},{12,0},{1,5},{5,9},{9,13},{13,1},{2,6},{6,10},{... | collective-permute-start | bytes 1572872 | tf_op jit(solution)/shard_map/ppermute | solution.py:30
  90.5 30.7 %collective-permute-start.14 = (bf16[4,128,512]{2,1,0:T(8,128)(2,1)}, bf16[4,128,512]{2,1,0:T(8,128)(2,1)}, u32[]{:S(2)}, u32[]{:S(2)}) collective-permute-start(bf16[4,128,512]{2,1,0:T(8,128)(2,1)} %get-tuple-element.69), channel_id=1, source_target_pairs={{0,8},{4,12},{8,0},{12,4},{1,9},{5,13},{9,1},{13,5},{2,10},{6,14},... | collective-permute-start | bytes 1572872 | tf_op jit(solution)/shard_map/ppermute | solution.py:30
  109.8 31.9 %all-to-all-start = ((bf16[16,32,512]{2,1,0:T(8,128)(2,1)}), bf16[16,32,512]{2,1,0:T(8,128)(2,1)}, u32[]{:S(2)}, u32[]{:S(2)}) async-start(bf16[16,32,512]{2,1,0:T(8,128)(2,1)} %bitcast.31), calls=%async_computation | async-start | bytes 1048576 | tf_op jit(solution)/shard_map/all_to_all | solution.py:376
  114.1 17.2 %collective-permute-start.15 = (bf16[4,128,512]{2,1,0:T(8,128)(2,1)}, bf16[4,128,512]{2,1,0:T(8,128)(2,1)S(1)}, u32[]{:S(2)}, u32[]{:S(2)}) collective-permute-start(bf16[4,128,512]{2,1,0:T(8,128)(2,1)} %get-tuple-element.68), channel_id=1, source_target_pairs={{0,12},{4,0},{8,4},{12,8},{1,13},{5,1},{9,5},{13,9},{2,14},{6,2},{... | collective-permute-start | bytes 1572872 | tf_op jit(solution)/shard_map/ppermute | solution.py:30
  118.4 17.7 %collective-permute-start.10 = (bf16[32,2048]{1,0:T(8,128)(2,1)S(1)}, bf16[32,2048]{1,0:T(8,128)(2,1)S(1)}, u32[]{:S(2)}, u32[]{:S(2)}) collective-permute-start(bf16[32,2048]{1,0:T(8,128)(2,1)S(1)} %get-tuple-element.74), channel_id=1, source_target_pairs={{0,4},{4,8},{8,12},{12,0},{1,5},{5,9},{9,13},{13,1},{2,6},{6,10},{... | collective-permute-start | bytes 393224 | tf_op jit(solution)/shard_map/ppermute | solution.py:30
  118.5 18.8 %collective-permute-start.11 = (bf16[32,2048]{1,0:T(8,128)(2,1)S(1)}, bf16[32,2048]{1,0:T(8,128)(2,1)S(1)}, u32[]{:S(2)}, u32[]{:S(2)}) collective-permute-start(bf16[32,2048]{1,0:T(8,128)(2,1)S(1)} %get-tuple-element.76), channel_id=1, source_target_pairs={{0,8},{4,12},{8,0},{12,4},{1,9},{5,13},{9,1},{13,5},{2,10},{6,14},... | collective-permute-start | bytes 393224 | tf_op jit(solution)/shard_map/ppermute | solution.py:30
  120.3 17.0 %collective-permute-start.12 = (bf16[32,2048]{1,0:T(8,128)(2,1)S(1)}, bf16[32,2048]{1,0:T(8,128)(2,1)S(1)}, u32[]{:S(2)}, u32[]{:S(2)}) collective-permute-start(bf16[32,2048]{1,0:T(8,128)(2,1)S(1)} %get-tuple-element.75), channel_id=1, source_target_pairs={{0,12},{4,0},{8,4},{12,8},{1,13},{5,1},{9,5},{13,9},{2,14},{6,2},{... | collective-permute-start | bytes 393224 | tf_op jit(solution)/shard_map/ppermute | solution.py:30
  133.6 6.5 %collective-permute-start.16 = (bf16[128,512]{1,0:T(8,128)(2,1)S(1)}, bf16[128,512]{1,0:T(8,128)(2,1)S(1)}, u32[]{:S(2)}, u32[]{:S(2)}) collective-permute-start(bf16[128,512]{1,0:T(8,128)(2,1)S(1)} %get-tuple-element.77), channel_id=1, source_target_pairs={{0,16},{16,32},{32,48},{48,0},{1,17},{17,33},{33,49},{49,1},{2,18}... | collective-permute-start | bytes 393224 | tf_op jit(solution)/shard_map/ppermute | solution.py:30
  133.7 6.4 %collective-permute-start.17 = (bf16[128,512]{1,0:T(8,128)(2,1)S(1)}, bf16[128,512]{1,0:T(8,128)(2,1)S(1)}, u32[]{:S(2)}, u32[]{:S(2)}) collective-permute-start(bf16[128,512]{1,0:T(8,128)(2,1)S(1)} %get-tuple-element.79), channel_id=1, source_target_pairs={{0,32},{16,48},{32,0},{48,16},{1,33},{17,49},{33,1},{49,17},{2,34}... | collective-permute-start | bytes 393224 | tf_op jit(solution)/shard_map/ppermute | solution.py:30
  136.2 4.5 %collective-permute-start.18 = (bf16[128,512]{1,0:T(8,128)(2,1)S(1)}, bf16[128,512]{1,0:T(8,128)(2,1)S(1)}, u32[]{:S(2)}, u32[]{:S(2)}) collective-permute-start(bf16[128,512]{1,0:T(8,128)(2,1)S(1)} %get-tuple-element.78), channel_id=1, source_target_pairs={{0,48},{16,0},{32,16},{48,32},{1,49},{17,1},{33,17},{49,33},{2,50}... | collective-permute-start | bytes 393224 | tf_op jit(solution)/shard_map/ppermute | solution.py:30
  170.2 12.3 %collective-permute-start.27 = (f32[2,136,512]{2,1,0:T(8,128)S(1)}, f32[2,136,512]{2,1,0:T(8,128)S(1)}, u32[]{:S(2)}, u32[]{:S(2)}) collective-permute-start(f32[2,136,512]{2,1,0:T(8,128)S(1)} %pad_maximum_fusion), channel_id=1, source_target_pairs={{0,64},{64,0},{1,65},{65,1},{2,66},{66,2},{3,67},{67,3},{4,68},{68... | collective-permute-start | bytes 1671176 | tf_op jit(solution)/shard_map/ppermute | solution.py:395
  (17 other events, 65.2 us)
where the time goes:
time: 189 us; the launch traced here: 188 us
  starting transfers between devices  66.6 us (35%)
  Pallas kernels  33.2 us (18%)
  blocking collectives  26.8 us (14%)
  waiting for transfers between devices  26.7 us (14%)
  local copies, waits for them, and re-layouts  24.1 us (13%)
  other arithmetic  8.97 us (5%)
    all_to_all x1, blocking collectives, on_device(): lax.all_to_all(jnp.concatenate([pieces, pieces], axis=0), ('zh', 'lat'),...  26.8 us
    pallas_call x1, Pallas kernels, couple(): pl.pallas_call(couple_kernel, out_shape=jax.ShapeDtypeStruct((512, 512),...  16.7 us
    pallas_call x1, Pallas kernels, block(): pl.pallas_call(block_kernel, out_shape=(jax.ShapeDtypeStruct((4, 90, 512)...  16.5 us
    ppermute x12, starting transfers between devices, scatter_sum(): total = total + lax.ppermute(out, axis, ring(4, step)).astype(f32)  14.3 us
    ppermute x12, waiting for transfers between devices, scatter_sum(): total = total + lax.ppermute(out, axis, ring(4, step)).astype(f32)  13.3 us
    unnamed x42, local copies, waits for them, and re-layouts  12.1 us
    ppermute x1, starting transfers between devices, on_device(): sums_beside = lax.ppermute(sums, 'core', ring(2, 1))  10.8 us
    ppermute x6, starting transfers between devices, all_sum(): lax.ppermute(block, axis, ring(4, step)).astype(f32)  9.11 us
  transfers between devices with their start and end apart: 29, of which 12 were waited for; matrix products, arithmetic and copies ran while one was open for 7% of the time, Pallas kernels for 9%

commit v1 on v0

--- a/solution.py
+++ b/solution.py
@@ -22,18 +22,23 @@
     return [(i, (i + step) % count) for i in range(count)]
 
 
-def scatter_sum(parts, axis, dim):
-    me = lax.axis_index(axis)
-    total = lax.dynamic_index_in_dim(parts, me, dim, keepdims=False).astype(f32)
-    for step in (1, 2, 3):
-        out = lax.dynamic_index_in_dim(parts, lax.rem(me + step, 4), dim, keepdims=False)
-        total = total + lax.ppermute(out, axis, ring(4, step)).astype(f32)
-    return total
-
-
-def all_sum(block, axis):
-    one, two, three = (lax.ppermute(block, axis, ring(4, step)).astype(f32) for step in (1, 2, 3))
-    return (block.astype(f32) + two) + (one + three)
+def cross(step, x_core):
+    pairs = []
+    for c in range(2):
+        for x in range(4):
+            for y in range(4):
+                to = (x, (y + step) % 4) if c != x_core else ((x + step) % 4, y)
+                pairs.append((c * 16 + x * 4 + y, c * 16 + to[0] * 4 + to[1]))
+    return pairs
+
+
+def total_of(parts):
+    own, one, two, three = [part.astype(f32) for part in parts]
+    return (own + two) + (one + three)
+
+
+def place(parts, index):
+    return lax.dynamic_index_in_dim(parts, index, 0, keepdims=False)
 
 
 def lat_halo(tile):
@@ -67,9 +72,10 @@
     w_in_sea,
     w_out_sea,
     result_ref,
-    gwi_ref,
-    gwo_ref,
-    small_ref,
+    out_0,
+    out_1,
+    out_2,
+    out_3,
     gct_ref,
     w_in,
     w_out,
@@ -81,8 +87,12 @@
     gb,
     branch,
     gnorm,
+    small,
     sems,
 ):
+    outs = (out_0, out_1, out_2, out_3)
+    here, far_step, near_step = ocean_ref[1], ocean_ref[2], ocean_ref[3]
+
     @pl.when(ocean_ref[0] == 1)
     def _():
         pltpu.make_async_copy(w_in_sea, w_in, sems.at[0]).start()
@@ -131,15 +141,24 @@
         scales.append(scale)
         normed[rows, :] = z
         norm_in[rows, :] = (z * gain).astype(bf16)
-    norm_in_t[...] = norm_in[...].T
+    turned = norm_in[...].T
+    for j in range(16):
+        far = lax.rem(lax.div(j, far_step), 4)
+        near = lax.rem(lax.div(j, near_step), 4)
+        k = lax.rem(far + 4 - here, 4)
+        rows = pl.ds(pl.multiple_of(k * 128 + near * 32, 32), 32)
+        norm_in_t[rows, :] = turned[j * 32 : j * 32 + 32]
     branch[...] = jnp.zeros_like(branch)
     gnorm[...] = jnp.zeros_like(gnorm)
     pltpu.make_async_copy(w_in_air, w_in, sems.at[0]).wait()
     pltpu.make_async_copy(w_out_air, w_out, sems.at[1]).wait()
 
-    def mlp_step(n, carry):
-        cols = pl.ds(pl.multiple_of(n * 256, 256), 256)
-        wi, wo = w_in[:, cols], w_out[cols, :]
+    def mlp_step(p, k):
+        far = lax.rem(here + k, 4)
+        blocks = [far * far_step + (2 * p + b) * near_step for b in (0, 1)]
+        picked = [pl.ds(pl.multiple_of(block * 128, 128), 128) for block in blocks]
+        wi = jnp.concatenate([w_in[:, cols] for cols in picked], axis=1)
+        wo = jnp.concatenate([w_out[cols, :] for cols in picked], axis=0)
         pre = mm(norm_in[...], wi)
         square = pre * pre
         tangent = jnp.tanh(tanh_scale * (pre + cubic_term * square * pre))
@@ -151,11 +170,27 @@
         gpre = (mm(gb[...], wo, ((1,), (1,))) * slope).astype(bf16)
         branch[...] += mm(hidden, wo)
         gnorm[...] += mm(gpre, wi, ((1,), (1,)))
-        gwi_ref[:, cols] = mm(norm_in_t[...], gpre).astype(bf16)
-        gwo_ref[cols, :] = mm(hidden, gb[...], ((0,), (0,))).astype(bf16)
-        return carry
-
-    lax.fori_loop(0, 8, mlp_step, 0)
+        gwi = mm(norm_in_t[...], gpre).astype(bf16)
+        gwo = mm(hidden, gb[...], ((0,), (0,))).astype(bf16)
+        for b in (0, 1):
+            lanes = pl.ds(pl.multiple_of(lax.rem(blocks[b], 4) * 128, 128), 128)
+            band = lax.div(blocks[b], 4) * 32
+            for j in range(4):
+                for near in range(4):
+                    rows = pl.ds(pl.multiple_of(near * 256 + band, 32), 32)
+                    outs[j][rows, lanes] = gwi[
+                        j * 128 + near * 32 : j * 128 + near * 32 + 32, b * 128 : b * 128 + 128
+                    ]
+            rows = pl.ds(pl.multiple_of((2 * p + b) * 256 + 128, 128), 128)
+            outs[k][rows, :] = gwo[b * 128 : b * 128 + 128]
+
+    for k in range(4):
+
+        def pair_step(p, carry, k=k):
+            mlp_step(p, k)
+            return carry
+
+        lax.fori_loop(0, 2, pair_step, 0)
 
     back = picker(96, 96, 12, 8)
     ggain = jnp.zeros((1, 512), f32)
@@ -194,11 +229,13 @@
                 for v in range(7):
                     acc[v] = acc[v] + g * q[t + v]
         rows = [jnp.sum(a, axis=0, keepdims=True) for a in acc] + [jnp.zeros((1, 128), f32)]
-        small_ref[pl.ds(pl.multiple_of(u * 8, 8), 8), lanes] = jnp.concatenate(rows, axis=0)
+        small[pl.ds(pl.multiple_of(u * 8, 8), 8), lanes] = jnp.concatenate(rows, axis=0)
         return carry
 
     lax.fori_loop(0, 28, kern_step, 0)
-    small_ref[56:64, :] = jnp.concatenate([ggain, jnp.zeros((7, 512), f32)], axis=0)
+    small[56:64, :] = jnp.concatenate([ggain, jnp.zeros((7, 512), f32)], axis=0)
+    for out in outs:
+        out[1024:1088, :] = small[...].astype(bf16)
 
 
 def block(ocean, north, own, south, cot, mask, kern, gain, wia, woa, wis, wos):
@@ -209,13 +246,11 @@
         block_kernel,
         out_shape=(
             jax.ShapeDtypeStruct((4, 90, 512), bf16),
-            jax.ShapeDtypeStruct((512, 2048), bf16),
-            jax.ShapeDtypeStruct((2048, 512), bf16),
-            jax.ShapeDtypeStruct((64, 512), f32),
+            *[jax.ShapeDtypeStruct((1088, 512), bf16)] * 4,
             jax.ShapeDtypeStruct((512, 384), bf16),
         ),
         in_specs=[pl.BlockSpec(memory_space=pltpu.SMEM)] + [vmem] * 7 + [hbm] * 4,
-        out_specs=(vmem,) * 5,
+        out_specs=(vmem,) * 6,
         scratch_shapes=[
             pltpu.VMEM((512, 2048), bf16),
             pltpu.VMEM((2048, 512), bf16),
@@ -227,9 +262,10 @@
             pltpu.VMEM((384, 512), bf16),
             pltpu.VMEM((384, 512), f32),
             pltpu.VMEM((384, 512), f32),
+            pltpu.VMEM((64, 512), f32),
             pltpu.SemaphoreType.DMA((2,)),
         ],
-        compiler_params=pltpu.CompilerParams(vmem_limit_bytes=40 * 1024 * 1024),
+        compiler_params=pltpu.CompilerParams(vmem_limit_bytes=56 * 1024 * 1024),
         cost_estimate=pl.CostEstimate(
             flops=flops, bytes_accessed=12 * 1024 * 1024, transcendentals=384 * 2048
         ),
@@ -270,7 +306,7 @@
             pltpu.VMEM((512, 512), f32),
             pltpu.VMEM((512, 384), bf16),
         ],
-        compiler_params=pltpu.CompilerParams(vmem_limit_bytes=40 * 1024 * 1024),
+        compiler_params=pltpu.CompilerParams(vmem_limit_bytes=56 * 1024 * 1024),
         cost_estimate=pl.CostEstimate(
             flops=2 * 50 * 384 * 512 * 512, bytes_accessed=4 * 1024 * 1024, transcendentals=0
         ),
@@ -345,8 +381,16 @@
     masked, north = lax.optimization_barrier((masked, north))
     masked_north, masked_south = lat_halo(masked)
 
-    result, grad_w_in, grad_w_out, small, grad_conv_t = block(
-        is_ocean.astype(jnp.int32).reshape(1),
+    x, y, lat = (lax.axis_index(axis) for axis in ("x", "y", "lat"))
+    result, *parts, grad_conv_t = block(
+        jnp.stack(
+            [
+                is_ocean.astype(jnp.int32),
+                jnp.where(core == 0, x, y),
+                jnp.where(core == 0, 4, 1),
+                jnp.where(core == 0, 1, 4),
+            ]
+        ),
         north,
         field,
         south,
@@ -360,9 +404,8 @@
         ocean_contract_weight,
     )
 
-    in_x = scatter_sum(grad_w_in.reshape(4, 128, 2048), "x", 0).astype(bf16)
-    out_y = scatter_sum(grad_w_out.reshape(4, 4, 128, 512), "y", 1).astype(bf16)
-    small = all_sum(small.astype(bf16), "x").astype(bf16)
+    for k in (1, 2, 3):
+        parts[k] = lax.ppermute(parts[k], ("core", "x", "y"), cross(k, 0))
 
     grad_couple = couple(
         masked_north,
@@ -373,36 +416,45 @@
         kernel_rows,
         jnp.where(is_ocean, 1.0 / copies, 1.0).astype(f32).reshape(1),
     )
+    tables = [part[:1024].reshape(4, 256, 512) for part in parts]
+    small = total_of([part[1024:] for part in parts])
+    messages = []
+    for k in range(4):
+        table = total_of([place(t, lax.rem(jnp.where(core == 0, y, x) + k, 4)) for t in tables])
+        messages.append(jnp.concatenate([table, small], axis=0).astype(bf16))
+    for k in (1, 2, 3):
+        messages[k] = lax.ppermute(messages[k], ("core", "x", "y"), cross(k, 1))
     gathered = lax.all_to_all(grad_couple.reshape(16, 32, 512), LON, 0, 0, tiled=True)
-    in_xy = scatter_sum(in_x.reshape(4, 32, 2048), "y", 0).astype(bf16)
-    out_xy = scatter_sum(out_y, "x", 0).astype(bf16)
-    small = all_sum(small, "y").astype(bf16)
-    gathered = jnp.sum(gathered.astype(f32), axis=0).astype(bf16)
+    gathered = jnp.sum(gathered.astype(f32), axis=0)
+    table = total_of(messages)
 
     pieces = jnp.concatenate(
         [
-            in_xy.reshape(4, 32, 512),
-            out_xy.reshape(4, 32, 512),
+            table[:128].reshape(4, 4, 8, 512).transpose(1, 0, 2, 3).reshape(4, 32, 512),
+            table[128:256].reshape(4, 32, 512),
             gathered.reshape(4, 8, 512),
-            jnp.broadcast_to(small[None], (4, 64, 512)),
+            jnp.broadcast_to(table[256:][None], (4, 64, 512)),
         ],
         axis=1,
-    )
-    column = lax.all_to_all(
-        jnp.concatenate([pieces, pieces], axis=0), ("zh", "lat"), 0, 0, tiled=True
-    ).astype(f32)
-    sums = jnp.stack([jnp.sum(column[:4], axis=0), jnp.sum(column[4:], axis=0)])
-    sums_beside = lax.ppermute(sums, "core", ring(2, 1))
+    ).astype(bf16)
+    rows = [place(pieces, lax.rem(lat + k, 4)) for k in range(4)]
+    for k in (1, 2, 3):
+        rows[k] = lax.ppermute(rows[k], "lat", ring(4, k))
+    mine = total_of(rows).astype(bf16)
+    across = lax.ppermute(mine, "zh", ring(2, 1))
+    sums = jnp.where(zh == 0, jnp.stack([mine, across]), jnp.stack([across, mine]))
+    sums_beside = lax.ppermute(sums, "core", ring(2, 1)).astype(f32)
+    sums = sums.astype(f32)
     first = jnp.where(core == 0, sums, sums_beside)
     second = jnp.where(core == 0, sums_beside, sums)
-    air = (first[0] + first[1]) + second[0]
+    air = (first[0] + second[0]) + first[1]
     sea_part = second[1]
 
     def split(total):
         return (
             total[72:128].reshape(7, 8, 512)[:, :7].reshape(49, 512),
             total[128],
-            total[:32].reshape(8, 2048),
+            total[:32].reshape(4, 8, 512).transpose(1, 0, 2).reshape(8, 2048),
             total[32:64],
         )
 

time: 189 us -> 156 us (0.83)
  blocking collectives: 26.8 us -> 0 us
  starting transfers between devices: 66.6 us -> 57.3 us
  waiting for transfers between devices: 26.7 us -> 34.7 us
  local copies, waits for them, and re-layouts: 24.1 us -> 16.9 us
  Pallas kernels: 33.2 us -> 38.9 us
  other arithmetic: 8.97 us -> 5.16 us
    all_to_all x1 -> x0, blocking collectives: 26.8 us -> none  [on_device(): lax.all_to_all(jnp.concatenate([pieces, pieces], axis=0), ('zh', 'lat'),...]
    ppermute x19 -> x11, starting transfers between devices: 34.2 us -> 23.4 us  [the longest x1 8 us: on_device(): sums_beside = lax.ppermute(sums, 'core', ring(2, 1)).astype(f32)]
    unnamed x42 -> x28, local copies, waits for them, and re-layouts: 12.1 us -> 2.84 us
    ppermute x19 -> x11, waiting for transfers between devices: 14.7 us -> 20.1 us  [the longest x3 9.1 us: on_device(): messages[k] = lax.ppermute(messages[k], ('core', 'x', 'y'), cross(k, 1))]
    convert_element_type x8 -> x1, other arithmetic: 4.73 us -> 0.08 us  [on_device(): mine = total_of(rows).astype(bf16)]
    slice x0 -> x7, local copies, waits for them, and re-layouts: none -> 4.54 us  [the longest x5 4.52 us: on_device(): tables = [part[:1024].reshape(4, 256, 512) for part in parts]]
    ppermute x1, waiting for transfers between devices: 1.08 us -> 5.04 us  [on_device(): west = lax.ppermute(marked[:, 87:], LON, ring(16, 1))]
    pallas_call x1, Pallas kernels: 16.5 us -> 20.2 us  [block(): pl.pallas_call(block_kernel, out_shape=(jax.ShapeDtypeStruct((4, 90, 512)...]
  transfers between devices with their start and end apart: 29 -> 21, of which waited for: 12 -> 13; matrix products, arithmetic and copies ran while one was open for 7% -> 9% of each run, Pallas kernels for 9% -> 25%
where the time goes in v1:
time: 156 us
  starting transfers between devices  57.3 us (37%)
  Pallas kernels  38.9 us (25%)
  waiting for transfers between devices  34.7 us (22%)
  local copies, waits for them, and re-layouts  16.9 us (11%)
  other arithmetic  5.16 us (3%)
  matrix products  1.57 us (1%)
    pallas_call x1, Pallas kernels, block(): pl.pallas_call(block_kernel, out_shape=(jax.ShapeDtypeStruct((4, 90, 512)...  20.2 us
    pallas_call x1, Pallas kernels, couple(): pl.pallas_call(couple_kernel, out_shape=jax.ShapeDtypeStruct((512, 512),...  18.8 us
    ppermute x2, starting transfers between devices, lat_halo(): north = lax.ppermute(tile[1:4], 'lat', [(i, i + 1) for i in range(3)])  10.9 us
    ppermute x3, waiting for transfers between devices, on_device(): messages[k] = lax.ppermute(messages[k], ('core', 'x', 'y'), cross(k, 1))  9.1 us
    ppermute x1, starting transfers between devices, on_device(): sums_beside = lax.ppermute(sums, 'core', ring(2, 1)).astype(f32)  8 us
    ppermute x3, waiting for transfers between devices, on_device(): rows[k] = lax.ppermute(rows[k], 'lat', ring(4, k))  7.52 us
    ppermute x1, starting transfers between devices, on_device(): got = lax.ppermute(half, 'zh', ring(2, 1))  7 us
    ppermute x1, starting transfers between devices, on_device(): east = lax.ppermute(marked[:, :3], LON, ring(16, -1))  5.84 us
  transfers between devices with their start and end apart: 21, of which 13 were waited for; matrix products, arithmetic and copies ran while one was open for 9% of the time, Pallas kernels for 25%

profile of v1, /device:TPU:1, one launch (start us, length us, event | category | flops | bytes accessed | tf_op | source)
XLA Modules:
  0.0 155.6 jit_solution(5231204226575396325)
XLA Ops:
  1.3 1.1 copy.39
  2.6 5.8 %collective-permute-start.1 = (bf16[4,3,640]{2,1,0:T(4,128)(2,1)S(1)}, bf16[4,3,640]{2,1,0:T(4,128)(2,1)S(1)}, u32[]{:S(2)}, u32[]{:S(2)}) collective-permute-start(bf16[4,3,640]{2,1,0:T(4,128)(2,1)S(1)} %get-tuple-element.65), channel_id=1, source_target_pairs={{0,60},{4,0},{8,4},{12,8},{16,12},{20,16},{24,20},{28,24},{32,28},... | collective-permute-start | bytes 46088 | tf_op jit(solution)/shard_map/ppermute | solution.py:342
  9.3 5.0 %collective-permute-done = bf16[4,3,640]{2,1,0:T(4,128)(2,1)S(1)} collective-permute-done((bf16[4,3,640]{2,1,0:T(4,128)(2,1)S(1)}, bf16[4,3,640]{2,1,0:T(4,128)(2,1)S(1)}, u32[]{:S(2)}, u32[]{:S(2)}) %collective-permute-start) | collective-permute-done | bytes 15392 | tf_op jit(solution)/shard_map/ppermute | solution.py:341
  14.5 2.2 %collective-permute-start.2 = (bf16[4,96,512]{2,1,0:T(8,128)(2,1)S(1)}, bf16[4,96,512]{2,1,0:T(8,128)(2,1)S(1)}, u32[]{:S(2)}, u32[]{:S(2)}) collective-permute-start(bf16[4,96,512]{2,1,0:T(8,128)(2,1)S(1)} %get-tuple-element.52), channel_id=1, source_target_pairs={{0,64},{64,0},{1,65},{65,1},{2,66},{66,2},{3,67},{67,3},{4,68},{68... | collective-permute-start | bytes 1179656 | tf_op jit(solution)/shard_map/ppermute | solution.py:348
  16.9 1.2 collective-permute-done.2
  18.2 7.0 %collective-permute-start.3 = (bf16[2,96,512]{2,1,0:T(8,128)(2,1)S(1)}, bf16[2,96,512]{2,1,0:T(8,128)(2,1)S(1)}, u32[]{:S(2)}, u32[]{:S(2)}) collective-permute-start(bf16[2,96,512]{2,1,0:T(8,128)(2,1)S(1)} %fusion.15), channel_id=1, source_target_pairs={{0,128},{128,0},{1,129},{129,1},{2,130},{130,2},{3,131},{131,3},{4... | collective-permute-start | bytes 589832 | tf_op jit(solution)/shard_map/ppermute | solution.py:352
  25.4 4.8 %collective-permute-done.3 = bf16[2,96,512]{2,1,0:T(8,128)(2,1)S(1)} collective-permute-done((bf16[2,96,512]{2,1,0:T(8,128)(2,1)S(1)}, bf16[2,96,512]{2,1,0:T(8,128)(2,1)S(1)}, u32[]{:S(2)}, u32[]{:S(2)}) %collective-permute-start.3) | collective-permute-done | bytes 196640 | tf_op jit(solution)/shard_map/ppermute | solution.py:352
  32.5 1.6 %convert_select_fusion = f32[384,512]{1,0:T(8,128)S(1)} fusion(bf16[384,512]{1,0:T(8,128)(2,1)S(1)} %bitcast.98, bf16[512,512]{1,0:T(8,128)(2,1)} %param.25, bf16[512,512]{1,0:T(8,128)(2,1)} %param.24, pred[]{:T(512)S(6)} %and.16), kind=kOutput, calls=%fused_computation.3 | convolution fusion | flops 202375168 | bytes 2228225 | tf_op jit(solution)/shard_map/dot_general | solution.py:375
  34.3 6.8 %collective-permute-start.5 = (bf16[3,96,512]{2,1,0:T(8,128)(2,1)S(1)}, bf16[3,96,512]{2,1,0:T(8,128)(2,1)S(1)}, u32[]{:S(2)}, u32[]{:S(2)}) collective-permute-start(bf16[3,96,512]{2,1,0:T(8,128)(2,1)S(1)} %get-tuple-element.69), channel_id=1, source_target_pairs={{0,1},{1,2},{2,3},{4,5},{5,6},{6,7},{8,9},{9,10},{10,11},{12,13},{... | collective-permute-start | bytes 884744 | tf_op jit(solution)/shard_map/ppermute | solution.py:45
  41.8 1.3 collective-permute-start.6
  45.4 1.7 %collective-permute-done.5.north_ref = bf16[3,96,512]{2,1,0:T(8,128)(2,1)S(1)} collective-permute-done((bf16[3,96,512]{2,1,0:T(8,128)(2,1)S(1)}, bf16[3,96,512]{2,1,0:T(8,128)(2,1)S(1)}, u32[]{:S(2)}, u32[]{:S(2)}) %collective-permute-start.5) | collective-permute-done | bytes 294944 | tf_op jit(solution)/shard_map/ppermute | solution.py:45
  48.1 4.1 %collective-permute-start.13 = (bf16[3,96,512]{2,1,0:T(8,128)(2,1)}, bf16[3,96,512]{2,1,0:T(8,128)(2,1)S(1)}, u32[]{:S(2)}, u32[]{:S(2)}) collective-permute-start(bf16[3,96,512]{2,1,0:T(8,128)(2,1)} %get-tuple-element.67), channel_id=1, source_target_pairs={{0,1},{1,2},{2,3},{4,5},{5,6},{6,7},{8,9},{9,10},{10,11},{12,13},{... | collective-permute-start | bytes 884744 | tf_op jit(solution)/shard_map/ppermute | solution.py:45
  52.2 1.3 collective-permute-start.14
  54.3 20.2 %block_kernel.1 = (bf16[4,90,512]{2,1,0:T(8,128)(2,1)}, bf16[1088,512]{1,0:T(8,128)(2,1)}, bf16[1088,512]{1,0:T(8,128)(2,1)}, bf16[1088,512]{1,0:T(8,128)(2,1)},...) custom-call(s32[4]{0:T(128)} %pad_add_fusion.ocean_ref, bf16[3,96,512]{2,1,0:T(8,128)(2,1)} %copy-done.11, ...), custom_call_target="tpu_custom_call" | custom-call | flops 4831838208 | bytes 12582912 | tf_op jit(solution)/shard_map/block_kernel/pallas_call | solution.py:245
  74.8 1.5 collective-permute-start.8
  76.8 1.4 pad.14.kern_ref
  78.2 1.3 slice.142
  80.2 18.8 %couple_kernel.1 = bf16[512,512]{1,0:T(8,128)(2,1)} custom-call(bf16[3,96,512]{2,1,0:T(8,128)(2,1)} %copy-done.10, bf16[4,96,512]{2,1,0:T(8,128)(2,1)} %copy-done.1, bf16[3,96,512]{2,1,0:T(8,128)(2,1)} %collective-permute-done.14.south_ref, bf16[512,384]{1,0:T(8,128)(2,1)} %get-tuple-element.26.gct_ref, bf16[4,96,512]{2,1,0:T(8,128)(2,1)} %pad.12.cot_ref, ...), custom_call_target="tpu_custom_call" | custom-call | flops 10066329600 | bytes 4194304 | tf_op jit(solution)/shard_map/couple_kernel/pallas_call | solution.py:299
  99.0 4.3 %all-to-all-start = ((bf16[16,32,512]{2,1,0:T(8,128)(2,1)}), bf16[16,32,512]{2,1,0:T(8,128)(2,1)S(1)}, u32[]{:S(2)}, u32[]{:S(2)}) async-start(bf16[16,32,512]{2,1,0:T(8,128)(2,1)} %bitcast.92), calls=%async_computation | async-start | bytes 1048576 | tf_op jit(solution)/shard_map/all_to_all | solution.py:427
  103.4 1.7 %slice.181 = bf16[1024,512]{1,0:T(8,128)(2,1)S(1)} slice(bf16[1088,512]{1,0:T(8,128)(2,1)} %collective-permute-done.8), slice={[0:1024], [0:512]} | slice | bytes 2097152 | tf_op jit(solution)/shard_map/slice | solution.py:419
  106.0 1.4 slice.180
  108.2 2.7 %collective-permute-start.12 = (bf16[320,512]{1,0:T(8,128)(2,1)S(1)}, bf16[320,512]{1,0:T(8,128)(2,1)S(1)}, u32[]{:S(2)}, u32[]{:S(2)}) collective-permute-start(bf16[320,512]{1,0:T(8,128)(2,1)S(1)} %get-tuple-element.76), channel_id=1, source_target_pairs={{0,12},{4,0},{8,4},{12,8},{16,28},{20,16},{24,20},{28,24},{32,44},... | collective-permute-start | bytes 983048 | tf_op jit(solution)/shard_map/ppermute | solution.py:426
  110.9 1.8 %collective-permute-start.10 = (bf16[320,512]{1,0:T(8,128)(2,1)S(1)}, bf16[320,512]{1,0:T(8,128)(2,1)S(1)}, u32[]{:S(2)}, u32[]{:S(2)}) collective-permute-start(bf16[320,512]{1,0:T(8,128)(2,1)S(1)} %get-tuple-element.74), channel_id=1, source_target_pairs={{0,8},{4,12},{8,0},{12,4},{16,24},{20,28},{24,16},{28,20},{32,40},... | collective-permute-start | bytes 983048 | tf_op jit(solution)/shard_map/ppermute | solution.py:426
  112.7 5.7 %collective-permute-done.12 = bf16[320,512]{1,0:T(8,128)(2,1)S(1)} collective-permute-done((bf16[320,512]{1,0:T(8,128)(2,1)S(1)}, bf16[320,512]{1,0:T(8,128)(2,1)S(1)}, u32[]{:S(2)}, u32[]{:S(2)}) %collective-permute-start.12) | collective-permute-done | bytes 327712 | tf_op jit(solution)/shard_map/ppermute | solution.py:426
  118.4 3.4 %collective-permute-done.11 = bf16[320,512]{1,0:T(8,128)(2,1)S(1)} collective-permute-done((bf16[320,512]{1,0:T(8,128)(2,1)S(1)}, bf16[320,512]{1,0:T(8,128)(2,1)S(1)}, u32[]{:S(2)}, u32[]{:S(2)}) %collective-permute-start.11) | collective-permute-done | bytes 327712 | tf_op jit(solution)/shard_map/ppermute | solution.py:426
  122.2 3.7 %collective-permute-start.17 = (bf16[136,512]{1,0:T(8,128)(2,1)S(1)}, bf16[136,512]{1,0:T(8,128)(2,1)S(1)}, u32[]{:S(2)}, u32[]{:S(2)}) collective-permute-start(bf16[136,512]{1,0:T(8,128)(2,1)S(1)} %get-tuple-element.62), channel_id=1, source_target_pairs={{0,3},{1,0},{2,1},{3,2},{4,7},{5,4},{6,5},{7,6},{8,11},{9,8},{10,9... | collective-permute-start | bytes 417800 | tf_op jit(solution)/shard_map/ppermute | solution.py:442
  126.6 1.3 collective-permute-done.17
  127.9 3.9 %collective-permute-done.16 = bf16[136,512]{1,0:T(8,128)(2,1)S(1)} collective-permute-done((bf16[136,512]{1,0:T(8,128)(2,1)S(1)}, bf16[136,512]{1,0:T(8,128)(2,1)S(1)}, u32[]{:S(2)}, u32[]{:S(2)}) %collective-permute-start.16) | collective-permute-done | bytes 139296 | tf_op jit(solution)/shard_map/ppermute | solution.py:442
  131.8 2.3 %collective-permute-done.15 = bf16[136,512]{1,0:T(8,128)(2,1)S(1)} collective-permute-done((bf16[136,512]{1,0:T(8,128)(2,1)S(1)}, bf16[136,512]{1,0:T(8,128)(2,1)S(1)}, u32[]{:S(2)}, u32[]{:S(2)}) %collective-permute-start.15) | collective-permute-done | bytes 139296 | tf_op jit(solution)/shard_map/ppermute | solution.py:442
  134.2 4.9 %collective-permute-start.18 = (bf16[136,512]{1,0:T(8,128)(2,1)S(1)}, bf16[136,512]{1,0:T(8,128)(2,1)S(1)}, u32[]{:S(2)}, u32[]{:S(2)}) collective-permute-start(bf16[136,512]{1,0:T(8,128)(2,1)S(1)} %fusion.10), channel_id=1, source_target_pairs={{0,128},{128,0},{1,129},{129,1},{2,130},{130,2},{3,131},{131,3},{4... | collective-permute-start | bytes 417800 | tf_op jit(solution)/shard_map/ppermute | solution.py:444
  139.1 3.3 %collective-permute-done.18 = bf16[136,512]{1,0:T(8,128)(2,1)S(1)} collective-permute-done((bf16[136,512]{1,0:T(8,128)(2,1)S(1)}, bf16[136,512]{1,0:T(8,128)(2,1)S(1)}, u32[]{:S(2)}, u32[]{:S(2)}) %collective-permute-start.18) | collective-permute-done | bytes 139296 | tf_op jit(solution)/shard_map/ppermute | solution.py:444
  142.4 8.0 %collective-permute-start.19 = (bf16[2,136,512]{2,1,0:T(8,128)(2,1)S(1)}, bf16[2,136,512]{2,1,0:T(8,128)(2,1)S(1)}, u32[]{:S(2)}, u32[]{:S(2)}) collective-permute-start(bf16[2,136,512]{2,1,0:T(8,128)(2,1)S(1)} %maximum_select_fusion.1), channel_id=1, source_target_pairs={{0,64},{64,0},{1,65},{65,1},{2,66},{66,2},{3,67},{67,3},{4,68},{68... | collective-permute-start | bytes 835592 | tf_op jit(solution)/shard_map/ppermute | solution.py:446
  (100 shorter events, 19.2 us)
Async XLA Ops:
  2.5 14.2 %copy-start.7 = (s32[4,90]{1,0:T(4,128)S(1)}, s32[4,90]{1,0:T(4,128)}, u32[]{:S(2)}) copy-start(s32[4,90]{1,0:T(4,128)} %param.15) | copy-start | bytes 4324
  2.5 14.2 %copy-start.4 = (bf16[1,4,90,512]{3,1,2,0:T(4,128)(2,1)S(1)}, bf16[1,4,90,512]{3,1,2,0:T(4,128)(2,1)}, u32[]{:S(2)}) copy-start(bf16[1,4,90,512]{3,1,2,0:T(4,128)(2,1)} %param.14) | copy-start | bytes 1105924
  2.6 6.7 %collective-permute-start.1 = (bf16[4,3,640]{2,1,0:T(4,128)(2,1)S(1)}, bf16[4,3,640]{2,1,0:T(4,128)(2,1)S(1)}, u32[]{:S(2)}, u32[]{:S(2)}) collective-permute-start(bf16[4,3,640]{2,1,0:T(4,128)(2,1)S(1)} %get-tuple-element.65), channel_id=1, source_target_pairs={{0,60},{4,0},{8,4},{12,8},{16,12},{20,16},{24,20},{28,24},{32,28},... | collective-permute-start | bytes 46088 | tf_op jit(solution)/shard_map/ppermute | solution.py:342
  8.4 6.0 %collective-permute-start = (bf16[4,3,640]{2,1,0:T(4,128)(2,1)S(1)}, bf16[4,3,640]{2,1,0:T(4,128)(2,1)S(1)}, u32[]{:S(2)}, u32[]{:S(2)}) collective-permute-start(bf16[4,3,640]{2,1,0:T(4,128)(2,1)S(1)} %get-tuple-element.64), channel_id=1, source_target_pairs={{0,4},{4,8},{8,12},{12,16},{16,20},{20,24},{24,28},{28,32},{32,36}... | collective-permute-start | bytes 46088 | tf_op jit(solution)/shard_map/ppermute | solution.py:341
  14.5 3.5 %collective-permute-start.2 = (bf16[4,96,512]{2,1,0:T(8,128)(2,1)S(1)}, bf16[4,96,512]{2,1,0:T(8,128)(2,1)S(1)}, u32[]{:S(2)}, u32[]{:S(2)}) collective-permute-start(bf16[4,96,512]{2,1,0:T(8,128)(2,1)S(1)} %get-tuple-element.52), channel_id=1, source_target_pairs={{0,64},{64,0},{1,65},{65,1},{2,66},{66,2},{3,67},{67,3},{4,68},{68... | collective-permute-start | bytes 1179656 | tf_op jit(solution)/shard_map/ppermute | solution.py:348
  16.9 8.4 %copy-start.5 = (f32[49,512]{1,0:T(8,128)S(1)}, f32[49,512]{1,0:T(8,128)}, u32[]{:S(2)}) copy-start(f32[49,512]{1,0:T(8,128)} %param.20) | copy-start | bytes 301060
  16.9 8.3 %copy-start.6 = (f32[49,512]{1,0:T(8,128)S(1)}, f32[49,512]{1,0:T(8,128)}, u32[]{:S(2)}) copy-start(f32[49,512]{1,0:T(8,128)} %param.16) | copy-start | bytes 301060
  18.2 12.0 %collective-permute-start.3 = (bf16[2,96,512]{2,1,0:T(8,128)(2,1)S(1)}, bf16[2,96,512]{2,1,0:T(8,128)(2,1)S(1)}, u32[]{:S(2)}, u32[]{:S(2)}) collective-permute-start(bf16[2,96,512]{2,1,0:T(8,128)(2,1)S(1)} %fusion.15), channel_id=1, source_target_pairs={{0,128},{128,0},{1,129},{129,1},{2,130},{130,2},{3,131},{131,3},{4... | collective-permute-start | bytes 589832 | tf_op jit(solution)/shard_map/ppermute | solution.py:352
  30.2 2.1 %collective-permute-start.4 = (bf16[2,96,512]{2,1,0:T(8,128)(2,1)S(1)}, bf16[2,96,512]{2,1,0:T(8,128)(2,1)S(1)}, u32[]{:S(2)}, u32[]{:S(2)}) collective-permute-start(bf16[2,96,512]{2,1,0:T(8,128)(2,1)S(1)} %collective-permute-done.3), channel_id=1, source_target_pairs={{0,64},{64,0},{1,65},{65,1},{2,66},{66,2},{3,67},{67,3},{4,68},{68... | collective-permute-start | bytes 589832 | tf_op jit(solution)/shard_map/ppermute | solution.py:353
  32.5 14.7 %copy-start.1 = (bf16[4,96,512]{2,1,0:T(8,128)(2,1)}, bf16[4,96,512]{2,1,0:T(8,128)(2,1)S(1)}, u32[]{:S(2)}) copy-start(bf16[4,96,512]{2,1,0:T(8,128)(2,1)S(1)} %get-tuple-element.25.own_ref) | copy-start | bytes 1179652
  34.1 7.1 %copy-start.8 = (f32[512]{0:T(512)S(1)}, f32[512]{0:T(512)}, u32[]{:S(2)}) copy-start(f32[512]{0:T(512)} %param.21) | copy-start | bytes 6148
  34.1 7.1 %copy-start.9 = (f32[512]{0:T(512)S(1)}, f32[512]{0:T(512)}, u32[]{:S(2)}) copy-start(f32[512]{0:T(512)} %param.17) | copy-start | bytes 6148
  34.3 11.2 %copy-start.2 = (bf16[4,96,512]{2,1,0:T(8,128)(2,1)}, bf16[4,96,512]{2,1,0:T(8,128)(2,1)S(1)}, u32[]{:S(2)}) copy-start(bf16[4,96,512]{2,1,0:T(8,128)(2,1)S(1)} %add_convert_fusion.own_ref) | copy-start | bytes 1179652
  34.3 12.8 %collective-permute-start.5 = (bf16[3,96,512]{2,1,0:T(8,128)(2,1)S(1)}, bf16[3,96,512]{2,1,0:T(8,128)(2,1)S(1)}, u32[]{:S(2)}, u32[]{:S(2)}) collective-permute-start(bf16[3,96,512]{2,1,0:T(8,128)(2,1)S(1)} %get-tuple-element.69), channel_id=1, source_target_pairs={{0,1},{1,2},{2,3},{4,5},{5,6},{6,7},{8,9},{9,10},{10,11},{12,13},{... | collective-permute-start | bytes 884744 | tf_op jit(solution)/shard_map/ppermute | solution.py:45
  41.8 11.7 %collective-permute-start.6 = (bf16[3,96,512]{2,1,0:T(8,128)(2,1)S(1)}, bf16[3,96,512]{2,1,0:T(8,128)(2,1)S(1)}, u32[]{:S(2)}, u32[]{:S(2)}) collective-permute-start(bf16[3,96,512]{2,1,0:T(8,128)(2,1)S(1)} %get-tuple-element.68), channel_id=1, source_target_pairs={{1,0},{2,1},{3,2},{5,4},{6,5},{7,6},{9,8},{10,9},{11,10},{13,12},{... | collective-permute-start | bytes 884744 | tf_op jit(solution)/shard_map/ppermute | solution.py:46
  47.1 7.2 %copy-start.11 = (bf16[3,96,512]{2,1,0:T(8,128)(2,1)}, bf16[3,96,512]{2,1,0:T(8,128)(2,1)S(1)}, u32[]{:S(2)}) copy-start(bf16[3,96,512]{2,1,0:T(8,128)(2,1)S(1)} %collective-permute-done.5.north_ref) | copy-start | bytes 884740
  48.1 31.4 %collective-permute-start.13 = (bf16[3,96,512]{2,1,0:T(8,128)(2,1)}, bf16[3,96,512]{2,1,0:T(8,128)(2,1)S(1)}, u32[]{:S(2)}, u32[]{:S(2)}) collective-permute-start(bf16[3,96,512]{2,1,0:T(8,128)(2,1)} %get-tuple-element.67), channel_id=1, source_target_pairs={{0,1},{1,2},{2,3},{4,5},{5,6},{6,7},{8,9},{9,10},{10,11},{12,13},{... | collective-permute-start | bytes 884744 | tf_op jit(solution)/shard_map/ppermute | solution.py:45
  52.2 27.3 %collective-permute-start.14 = (bf16[3,96,512]{2,1,0:T(8,128)(2,1)}, bf16[3,96,512]{2,1,0:T(8,128)(2,1)}, u32[]{:S(2)}, u32[]{:S(2)}) collective-permute-start(bf16[3,96,512]{2,1,0:T(8,128)(2,1)} %get-tuple-element.66), channel_id=1, source_target_pairs={{1,0},{2,1},{3,2},{5,4},{6,5},{7,6},{9,8},{10,9},{11,10},{13,12},{... | collective-permute-start | bytes 884744 | tf_op jit(solution)/shard_map/ppermute | solution.py:46
  74.5 28.8 %collective-permute-start.9 = (bf16[1088,512]{1,0:T(8,128)(2,1)}, bf16[1088,512]{1,0:T(8,128)(2,1)S(1)}, u32[]{:S(2)}, u32[]{:S(2)}) collective-permute-start(bf16[1088,512]{1,0:T(8,128)(2,1)} %get-tuple-element.24), channel_id=1, source_target_pairs={{0,48},{4,52},{8,56},{12,60},{16,0},{20,4},{24,8},{28,12},{32,16},... | collective-permute-start | bytes 3342344 | tf_op jit(solution)/shard_map/ppermute | solution.py:408
  74.8 28.6 %collective-permute-start.8 = (bf16[1088,512]{1,0:T(8,128)(2,1)}, bf16[1088,512]{1,0:T(8,128)(2,1)}, u32[]{:S(2)}, u32[]{:S(2)}) collective-permute-start(bf16[1088,512]{1,0:T(8,128)(2,1)} %get-tuple-element.23), channel_id=1, source_target_pairs={{0,16},{4,20},{8,24},{12,28},{16,32},{20,36},{24,40},{28,44},{32,4... | collective-permute-start | bytes 3342344 | tf_op jit(solution)/shard_map/ppermute | solution.py:408
  76.2 28.8 %collective-permute-start.7 = (bf16[1088,512]{1,0:T(8,128)(2,1)}, bf16[1088,512]{1,0:T(8,128)(2,1)}, u32[]{:S(2)}, u32[]{:S(2)}) collective-permute-start(bf16[1088,512]{1,0:T(8,128)(2,1)} %get-tuple-element.22), channel_id=1, source_target_pairs={{0,32},{4,36},{8,40},{12,44},{16,48},{20,52},{24,56},{28,60},{32,0... | collective-permute-start | bytes 3342344 | tf_op jit(solution)/shard_map/ppermute | solution.py:408
  99.0 13.7 %all-to-all-start = ((bf16[16,32,512]{2,1,0:T(8,128)(2,1)}), bf16[16,32,512]{2,1,0:T(8,128)(2,1)S(1)}, u32[]{:S(2)}, u32[]{:S(2)}) async-start(bf16[16,32,512]{2,1,0:T(8,128)(2,1)} %bitcast.92), calls=%async_computation | async-start | bytes 1048576 | tf_op jit(solution)/shard_map/all_to_all | solution.py:427
  103.3 1.7 %copy-start = (bf16[1088,512]{1,0:T(8,128)(2,1)}, bf16[1088,512]{1,0:T(8,128)(2,1)S(1)}, u32[]{:S(2)}) copy-start(bf16[1088,512]{1,0:T(8,128)(2,1)S(1)} %collective-permute-done.9) | copy-start | bytes 3342340
  108.2 10.2 %collective-permute-start.12 = (bf16[320,512]{1,0:T(8,128)(2,1)S(1)}, bf16[320,512]{1,0:T(8,128)(2,1)S(1)}, u32[]{:S(2)}, u32[]{:S(2)}) collective-permute-start(bf16[320,512]{1,0:T(8,128)(2,1)S(1)} %get-tuple-element.76), channel_id=1, source_target_pairs={{0,12},{4,0},{8,4},{12,8},{16,28},{20,16},{24,20},{28,24},{32,44},... | collective-permute-start | bytes 983048 | tf_op jit(solution)/shard_map/ppermute | solution.py:426
  110.9 10.9 %collective-permute-start.11 = (bf16[320,512]{1,0:T(8,128)(2,1)S(1)}, bf16[320,512]{1,0:T(8,128)(2,1)S(1)}, u32[]{:S(2)}, u32[]{:S(2)}) collective-permute-start(bf16[320,512]{1,0:T(8,128)(2,1)S(1)} %get-tuple-element.75), channel_id=1, source_target_pairs={{0,4},{4,8},{8,12},{12,0},{16,20},{20,24},{24,28},{28,16},{32,36},... | collective-permute-start | bytes 983048 | tf_op jit(solution)/shard_map/ppermute | solution.py:426
  110.9 10.9 %collective-permute-start.10 = (bf16[320,512]{1,0:T(8,128)(2,1)S(1)}, bf16[320,512]{1,0:T(8,128)(2,1)S(1)}, u32[]{:S(2)}, u32[]{:S(2)}) collective-permute-start(bf16[320,512]{1,0:T(8,128)(2,1)S(1)} %get-tuple-element.74), channel_id=1, source_target_pairs={{0,8},{4,12},{8,0},{12,4},{16,24},{20,28},{24,16},{28,20},{32,40},... | collective-permute-start | bytes 983048 | tf_op jit(solution)/shard_map/ppermute | solution.py:426
  122.1 28.3 %copy-start.3 = (bf16[4,90,512]{2,1,0:T(8,128)(2,1)S(1)}, bf16[4,90,512]{2,1,0:T(8,128)(2,1)}, u32[]{:S(2)}) copy-start(bf16[4,90,512]{2,1,0:T(8,128)(2,1)} %get-tuple-element.20) | copy-start | bytes 1105924
  122.2 5.8 %collective-permute-start.17 = (bf16[136,512]{1,0:T(8,128)(2,1)S(1)}, bf16[136,512]{1,0:T(8,128)(2,1)S(1)}, u32[]{:S(2)}, u32[]{:S(2)}) collective-permute-start(bf16[136,512]{1,0:T(8,128)(2,1)S(1)} %get-tuple-element.62), channel_id=1, source_target_pairs={{0,3},{1,0},{2,1},{3,2},{4,7},{5,4},{6,5},{7,6},{8,11},{9,8},{10,9... | collective-permute-start | bytes 417800 | tf_op jit(solution)/shard_map/ppermute | solution.py:442
  125.9 5.9 %collective-permute-start.16 = (bf16[136,512]{1,0:T(8,128)(2,1)S(1)}, bf16[136,512]{1,0:T(8,128)(2,1)S(1)}, u32[]{:S(2)}, u32[]{:S(2)}) collective-permute-start(bf16[136,512]{1,0:T(8,128)(2,1)S(1)} %get-tuple-element.63), channel_id=1, source_target_pairs={{0,1},{1,2},{2,3},{3,0},{4,5},{5,6},{6,7},{7,4},{8,9},{9,10},{10,1... | collective-permute-start | bytes 417800 | tf_op jit(solution)/shard_map/ppermute | solution.py:442
  125.9 8.2 %collective-permute-start.15 = (bf16[136,512]{1,0:T(8,128)(2,1)S(1)}, bf16[136,512]{1,0:T(8,128)(2,1)S(1)}, u32[]{:S(2)}, u32[]{:S(2)}) collective-permute-start(bf16[136,512]{1,0:T(8,128)(2,1)S(1)} %get-tuple-element.61), channel_id=1, source_target_pairs={{0,2},{1,3},{2,0},{3,1},{4,6},{5,7},{6,4},{7,5},{8,10},{9,11},{10,... | collective-permute-start | bytes 417800 | tf_op jit(solution)/shard_map/ppermute | solution.py:442
  134.2 8.2 %collective-permute-start.18 = (bf16[136,512]{1,0:T(8,128)(2,1)S(1)}, bf16[136,512]{1,0:T(8,128)(2,1)S(1)}, u32[]{:S(2)}, u32[]{:S(2)}) collective-permute-start(bf16[136,512]{1,0:T(8,128)(2,1)S(1)} %fusion.10), channel_id=1, source_target_pairs={{0,128},{128,0},{1,129},{129,1},{2,130},{130,2},{3,131},{131,3},{4... | collective-permute-start | bytes 417800 | tf_op jit(solution)/shard_map/ppermute | solution.py:444
  142.4 9.2 %collective-permute-start.19 = (bf16[2,136,512]{2,1,0:T(8,128)(2,1)S(1)}, bf16[2,136,512]{2,1,0:T(8,128)(2,1)S(1)}, u32[]{:S(2)}, u32[]{:S(2)}) collective-permute-start(bf16[2,136,512]{2,1,0:T(8,128)(2,1)S(1)} %maximum_select_fusion.1), channel_id=1, source_target_pairs={{0,64},{64,0},{1,65},{65,1},{2,66},{66,2},{3,67},{67,3},{4,68},{68... | collective-permute-start | bytes 835592 | tf_op jit(solution)/shard_map/ppermute | solution.py:446
  (3 other events, 3.1 us)

commit v2 on v1

--- a/solution.py
+++ b/solution.py
@@ -13,6 +13,7 @@
 eps_norm = 1e-06
 bf16 = jnp.bfloat16
 f32 = jnp.float32
+PARTS = ((0, 1, 2, 3),)
 
 COMP = ("zh", "core")
 LON = ("x", "y")
@@ -72,10 +73,10 @@
     w_in_sea,
     w_out_sea,
     result_ref,
-    out_0,
-    out_1,
-    out_2,
-    out_3,
+    to_0,
+    to_1,
+    to_2,
+    to_3,
     gct_ref,
     w_in,
     w_out,
@@ -88,20 +89,39 @@
     branch,
     gnorm,
     small,
+    packed,
+    out_0,
+    out_1,
+    out_2,
+    out_3,
     sems,
 ):
     outs = (out_0, out_1, out_2, out_3)
+    targets = (to_0, to_1, to_2, to_3)
+
+    def send(j, first, count, sem):
+        rows = pl.ds(first, count)
+        return pltpu.make_async_copy(outs[j].at[rows], targets[j].at[rows], sems.at[sem])
+
     here, far_step, near_step = ocean_ref[1], ocean_ref[2], ocean_ref[3]
+
+    def weight_copies(expand, contract):
+        copies = []
+        for n in range(4):
+            a, b = pl.ds(n * 128, 128), pl.ds(n * 512, 512)
+            copies.append(pltpu.make_async_copy(expand.at[a], w_in.at[a], sems.at[n]))
+            copies.append(pltpu.make_async_copy(contract.at[b], w_out.at[b], sems.at[n + 4]))
+        return copies
 
     @pl.when(ocean_ref[0] == 1)
     def _():
-        pltpu.make_async_copy(w_in_sea, w_in, sems.at[0]).start()
-        pltpu.make_async_copy(w_out_sea, w_out, sems.at[1]).start()
+        for copy in weight_copies(w_in_sea, w_out_sea):
+            copy.start()
 
     @pl.when(ocean_ref[0] == 0)
     def _():
-        pltpu.make_async_copy(w_in_air, w_in, sems.at[0]).start()
-        pltpu.make_async_copy(w_out_air, w_out, sems.at[1]).start()
+        for copy in weight_copies(w_in_air, w_out_air):
+            copy.start()
 
     spread = picker(144, 96, 8, 12)
     for r in range(10):
@@ -150,47 +170,42 @@
         norm_in_t[rows, :] = turned[j * 32 : j * 32 + 32]
     branch[...] = jnp.zeros_like(branch)
     gnorm[...] = jnp.zeros_like(gnorm)
-    pltpu.make_async_copy(w_in_air, w_in, sems.at[0]).wait()
-    pltpu.make_async_copy(w_out_air, w_out, sems.at[1]).wait()
-
-    def mlp_step(p, k):
+    for copy in weight_copies(w_in_air, w_out_air):
+        copy.wait()
+
+    for k in range(4):
         far = lax.rem(here + k, 4)
-        blocks = [far * far_step + (2 * p + b) * near_step for b in (0, 1)]
+        blocks = [far * far_step + near * near_step for near in range(4)]
         picked = [pl.ds(pl.multiple_of(block * 128, 128), 128) for block in blocks]
-        wi = jnp.concatenate([w_in[:, cols] for cols in picked], axis=1)
-        wo = jnp.concatenate([w_out[cols, :] for cols in picked], axis=0)
-        pre = mm(norm_in[...], wi)
-        square = pre * pre
-        tangent = jnp.tanh(tanh_scale * (pre + cubic_term * square * pre))
-        half = 0.5 * (1.0 + tangent)
-        hidden = (pre * half).astype(bf16)
-        slope = half + 0.5 * pre * (1.0 - tangent * tangent) * (
-            tanh_scale * (1.0 + 3.0 * cubic_term * square)
-        )
-        gpre = (mm(gb[...], wo, ((1,), (1,))) * slope).astype(bf16)
-        branch[...] += mm(hidden, wo)
-        gnorm[...] += mm(gpre, wi, ((1,), (1,)))
-        gwi = mm(norm_in_t[...], gpre).astype(bf16)
-        gwo = mm(hidden, gb[...], ((0,), (0,))).astype(bf16)
-        for b in (0, 1):
-            lanes = pl.ds(pl.multiple_of(lax.rem(blocks[b], 4) * 128, 128), 128)
-            band = lax.div(blocks[b], 4) * 32
-            for j in range(4):
-                for near in range(4):
-                    rows = pl.ds(pl.multiple_of(near * 256 + band, 32), 32)
-                    outs[j][rows, lanes] = gwi[
-                        j * 128 + near * 32 : j * 128 + near * 32 + 32, b * 128 : b * 128 + 128
-                    ]
-            rows = pl.ds(pl.multiple_of((2 * p + b) * 256 + 128, 128), 128)
-            outs[k][rows, :] = gwo[b * 128 : b * 128 + 128]
-
-    for k in range(4):
-
-        def pair_step(p, carry, k=k):
-            mlp_step(p, k)
-            return carry
-
-        lax.fori_loop(0, 2, pair_step, 0)
+        for p in PARTS:
+            wi = jnp.concatenate([w_in[:, picked[q]] for q in p], axis=1)
+            wo = jnp.concatenate([w_out[picked[q], :] for q in p], axis=0)
+            pre = mm(norm_in[...], wi)
+            square = pre * pre
+            half = 0.5 + 0.5 * jnp.tanh(pre * (tanh_scale + (tanh_scale * cubic_term) * square))
+            value = pre * half
+            hidden = value.astype(bf16)
+            slope = half + value * (1.0 - half) * (
+                2.0 * tanh_scale + (6.0 * tanh_scale * cubic_term) * square
+            )
+            gpre = (mm(gb[...], wo, ((1,), (1,))) * slope).astype(bf16)
+            branch[...] += mm(hidden, wo)
+            gnorm[...] += mm(gpre, wi, ((1,), (1,)))
+            gwi = mm(norm_in_t[...], gpre).astype(bf16)
+            gwo = mm(hidden, gb[...], ((0,), (0,))).astype(bf16)
+            for n, q in enumerate(p):
+                lanes = pl.ds(pl.multiple_of(lax.rem(blocks[q], 4) * 128, 128), 128)
+                band = lax.div(blocks[q], 4) * 32
+                for j in range(4):
+                    for near in range(4):
+                        rows = pl.ds(pl.multiple_of(near * 256 + band, 32), 32)
+                        outs[j][rows, lanes] = gwi[
+                            j * 128 + near * 32 : j * 128 + near * 32 + 32,
+                            n * 128 : n * 128 + 128,
+                        ]
+                outs[k][q * 256 + 128 : q * 256 + 256, :] = gwo[n * 128 : n * 128 + 128]
+    for j in range(4):
+        send(j, 0, 1024, 8 + j).start()
 
     back = picker(96, 96, 12, 8)
     ggain = jnp.zeros((1, 512), f32)
@@ -233,9 +248,17 @@
         return carry
 
     lax.fori_loop(0, 28, kern_step, 0)
-    small[56:64, :] = jnp.concatenate([ggain, jnp.zeros((7, 512), f32)], axis=0)
+    for u in range(7):
+        packed[u * 7 : u * 7 + 7, :] = small[u * 8 : u * 8 + 7, :]
+    packed[49:50, :] = ggain
+    packed[50:64, :] = jnp.zeros((14, 512), f32)
     for out in outs:
-        out[1024:1088, :] = small[...].astype(bf16)
+        out[1024:1088, :] = packed[...].astype(bf16)
+    for j in range(4):
+        send(j, 1024, 64, 12 + j).start()
+    for j in range(4):
+        send(j, 0, 1024, 8 + j).wait()
+        send(j, 1024, 64, 12 + j).wait()
 
 
 def block(ocean, north, own, south, cot, mask, kern, gain, wia, woa, wis, wos):
@@ -250,7 +273,7 @@
             jax.ShapeDtypeStruct((512, 384), bf16),
         ),
         in_specs=[pl.BlockSpec(memory_space=pltpu.SMEM)] + [vmem] * 7 + [hbm] * 4,
-        out_specs=(vmem,) * 6,
+        out_specs=(vmem,) + (hbm,) * 4 + (vmem,),
         scratch_shapes=[
             pltpu.VMEM((512, 2048), bf16),
             pltpu.VMEM((2048, 512), bf16),
@@ -262,8 +285,10 @@
             pltpu.VMEM((384, 512), bf16),
             pltpu.VMEM((384, 512), f32),
             pltpu.VMEM((384, 512), f32),
+            pltpu.VMEM((56, 512), f32),
             pltpu.VMEM((64, 512), f32),
-            pltpu.SemaphoreType.DMA((2,)),
+            *[pltpu.VMEM((1088, 512), bf16)] * 4,
+            pltpu.SemaphoreType.DMA((16,)),
         ],
         compiler_params=pltpu.CompilerParams(vmem_limit_bytes=56 * 1024 * 1024),
         cost_estimate=pl.CostEstimate(
@@ -273,28 +298,34 @@
     )(ocean, north, own, south, cot, mask, kern, gain, wia, woa, wis, wos)
 
 
-def couple_kernel(north_ref, own_ref, south_ref, gct_ref, cot_ref, kern_ref, scale_ref, out_ref, rows16, acc, cot_t):
+def couple_kernel(
+    north_ref, own_ref, south_ref, gct_ref, cot_ref, kern_ref, scale_ref, out_ref, rows16, acc, gct, taps
+):
     spread = picker(192, 96, 16, 6)
     for r in range(10):
         src = north_ref[r] if r < 3 else own_ref[r - 3] if r < 7 else south_ref[r - 7]
         rows16[r] = mm(spread, src).astype(bf16)
     order = picker(96, 96, 16, 6)
     moved = [mm(order, cot_ref[i]).astype(bf16) for i in range(4)]
-    cot_t[...] = jnp.concatenate(moved, axis=0).T
-    acc[...] = mm(cot_t[...], rows16[3:7, 48:144, :].reshape(384, 512))
+    acc[...] = mm(jnp.concatenate(moved, axis=0).T, rows16[3:7, 48:144, :].reshape(384, 512))
+    gct[...] = gct_ref[...].astype(f32)
+    turned = kern_ref[...].T
+    for u in range(7):
+        taps[u] = turned[:, u * 8 : u * 8 + 8]
 
     def step(u, carry):
+        left, right = [], []
         for v in range(7):
-            part = rows16[pl.ds(u, 4), v * 16 : v * 16 + 96, :].reshape(384, 512)
-            k = kern_ref[u, :, v : v + 1]
-            acc[...] += k * mm(gct_ref[...], part)
+            left.append((taps[u, :, v : v + 1] * gct[...]).astype(bf16))
+            right.append(rows16[pl.ds(u, 4), v * 16 : v * 16 + 96, :].reshape(384, 512))
+        acc[...] += mm(jnp.concatenate(left, axis=1), jnp.concatenate(right, axis=0))
         return carry
 
     lax.fori_loop(0, 7, step, 0)
-    out_ref[...] = (acc[...] * scale_ref[0]).T.astype(bf16)
-
-
-def couple(north, own, south, gct, cot, kern_t, scale):
+    out_ref[...] = (acc[...] * scale_ref[0]).astype(bf16).T
+
+
+def couple(north, own, south, gct, cot, kern, scale):
     vmem = pl.BlockSpec(memory_space=pltpu.VMEM)
     return pl.pallas_call(
         couple_kernel,
@@ -304,14 +335,52 @@
         scratch_shapes=[
             pltpu.VMEM((10, 192, 512), bf16),
             pltpu.VMEM((512, 512), f32),
-            pltpu.VMEM((512, 384), bf16),
+            pltpu.VMEM((512, 384), f32),
+            pltpu.VMEM((7, 512, 8), f32),
         ],
-        compiler_params=pltpu.CompilerParams(vmem_limit_bytes=56 * 1024 * 1024),
+        compiler_params=pltpu.CompilerParams(vmem_limit_bytes=24 * 1024 * 1024),
         cost_estimate=pl.CostEstimate(
             flops=2 * 50 * 384 * 512 * 512, bytes_accessed=4 * 1024 * 1024, transcendentals=0
         ),
         name="couple_kernel",
-    )(north, own, south, gct, cot, kern_t, scale)
+    )(north, own, south, gct, cot, kern, scale)
+
+
+def finish_kernel(place_ref, mine_ref, mine_beside_ref, across_ref, across_beside_ref, *refs):
+    outs, total = refs[:10], refs[10]
+    first_zh, first_core = place_ref[0] == 0, place_ref[1] == 0
+    mine, across = mine_ref[...].astype(f32), across_ref[...].astype(f32)
+    mine_beside = mine_beside_ref[...].astype(f32)
+    across_beside = across_beside_ref[...].astype(f32)
+    near = jnp.where(first_zh, mine, across)
+    near_beside = jnp.where(first_zh, mine_beside, across_beside)
+    far = jnp.where(first_zh, across, mine)
+    far_beside = jnp.where(first_zh, across_beside, mine_beside)
+    far_air = jnp.where(first_core, far, far_beside)
+    total[0] = (near + near_beside) + far_air
+    total[1] = jnp.where(first_core, far_beside, far)
+    for n in range(2):
+        kern_ref, gain_ref, expand_ref, contract_ref = outs[n * 4 : n * 4 + 4]
+        kern_ref[...] = total[n, 72:121, :]
+        gain_ref[...] = total[n, 121:122, :]
+        for cb in range(4):
+            expand_ref[:, cb * 512 : cb * 512 + 512] = total[n, cb * 8 : cb * 8 + 8, :]
+        contract_ref[...] = total[n, 32:64, :]
+        outs[8 + n][...] = total[n, 64:72, :]
+
+
+def finish(here, mine, mine_beside, across, across_beside):
+    vmem = pl.BlockSpec(memory_space=pltpu.VMEM)
+    shapes = [(49, 512), (1, 512), (8, 2048), (32, 512)] * 2 + [(8, 512)] * 2
+    return pl.pallas_call(
+        finish_kernel,
+        out_shape=[jax.ShapeDtypeStruct(shape, f32) for shape in shapes],
+        in_specs=[pl.BlockSpec(memory_space=pltpu.SMEM)] + [vmem] * 4,
+        out_specs=[vmem] * 10,
+        scratch_shapes=[pltpu.VMEM((2, 128, 512), f32)],
+        compiler_params=pltpu.CompilerParams(vmem_limit_bytes=8 * 1024 * 1024),
+        name="finish_kernel",
+    )(here, mine, mine_beside, across, across_beside)
 
 
 def on_device(
@@ -335,11 +404,12 @@
     sea = (1 - land).astype(f32)
     local = component_snapshots[0]
 
-    marked = jnp.concatenate(
-        [local, jnp.broadcast_to(sea.astype(bf16)[:, :, None], (4, 90, 128))], axis=2
-    )
-    west = lax.ppermute(marked[:, 87:], LON, ring(16, 1))
-    east = lax.ppermute(marked[:, :3], LON, ring(16, -1))
+    def edge(columns):
+        flags = jnp.broadcast_to(sea[:, columns].astype(bf16)[:, :, None], (4, 3, 128))
+        return jnp.concatenate([local[:, columns], flags], axis=2)
+
+    west = lax.ppermute(edge(slice(87, 90)), LON, ring(16, 1))
+    east = lax.ppermute(edge(slice(0, 3)), LON, ring(16, -1))
     local = jnp.concatenate([west[:, :, :512], local, east[:, :, :512]], axis=1)
     sea_wide = jnp.concatenate(
         [west[:, :, 512].astype(f32), sea, east[:, :, 512].astype(f32)], axis=1
@@ -350,15 +420,6 @@
     payload = jnp.where(zh == 0, pair_sum, jnp.where(core == 0, beside, local))
     half = lax.dynamic_slice_in_dim(payload, core * 2, 2, axis=0)
     got = lax.ppermute(half, "zh", ring(2, 1))
-    got_beside = lax.ppermute(got, "core", ring(2, 1))
-    full = jnp.where(
-        core == 0,
-        jnp.concatenate([got, got_beside], axis=0),
-        jnp.concatenate([got_beside, got], axis=0),
-    )
-    ocean_sum = (full.astype(f32) + beside.astype(f32)).astype(bf16)
-    partner = jnp.where(zh == 0, full, jnp.where(core == 0, beside, ocean_sum))
-
     coupling = jnp.where(is_ocean, flux_weight, marine_to_air_map)
     kernel = jnp.where(is_ocean, ocean_kernel, atmosphere_kernel)
     gain = jnp.where(is_ocean, ocean_gain, atmosphere_gain)
@@ -368,9 +429,18 @@
     mask = jnp.pad(mask, ((0, 0), (0, 6))).reshape(4, 8, 12).transpose(0, 2, 1).reshape(384, 1)
     mask = jnp.broadcast_to(mask, (384, 128))
     kernel_lanes = kernel.reshape(49, 4, 128).transpose(1, 0, 2)
-    kernel_rows = jnp.pad(
-        kernel.reshape(7, 7, 512).transpose(0, 2, 1), ((0, 0), (0, 0), (0, 1))
-    )
+    kernel_rows = jnp.pad(kernel.reshape(7, 7, 512), ((0, 1), (0, 1), (0, 0))).reshape(64, 512)
+    got, coupling, kernel_lanes, kernel_rows, gain, mask, grad_branch = lax.optimization_barrier(
+        (got, coupling, kernel_lanes, kernel_rows, gain, mask, grad_branch)
+    )
+    got_beside = lax.ppermute(got, "core", ring(2, 1))
+    full = jnp.where(
+        core == 0,
+        jnp.concatenate([got, got_beside], axis=0),
+        jnp.concatenate([got_beside, got], axis=0),
+    )
+    ocean_sum = (full.astype(f32) + beside.astype(f32)).astype(bf16)
+    partner = jnp.where(zh == 0, full, jnp.where(core == 0, beside, ocean_sum))
 
     projected = jnp.dot(partner.reshape(384, 512), coupling, preferred_element_type=f32)
     forcing = jnp.where(is_ocean, projected / copies, projected.astype(bf16).astype(f32))
@@ -378,7 +448,6 @@
     field = field.astype(bf16)
     north, south = lat_halo(field)
     masked = (sea_wide[:, :, None] * partner.astype(f32)).astype(bf16)
-    masked, north = lax.optimization_barrier((masked, north))
     masked_north, masked_south = lat_halo(masked)
 
     x, y, lat = (lax.axis_index(axis) for axis in ("x", "y", "lat"))
@@ -416,15 +485,17 @@
         kernel_rows,
         jnp.where(is_ocean, 1.0 / copies, 1.0).astype(f32).reshape(1),
     )
-    tables = [part[:1024].reshape(4, 256, 512) for part in parts]
-    small = total_of([part[1024:] for part in parts])
+    small = total_of([part[1024:1080] for part in parts])
+    near = jnp.where(core == 0, y, x)
     messages = []
     for k in range(4):
-        table = total_of([place(t, lax.rem(jnp.where(core == 0, y, x) + k, 4)) for t in tables])
+        start = lax.rem(near + k, 4) * 256
+        table = total_of([lax.dynamic_slice_in_dim(part, start, 256, 0) for part in parts])
         messages.append(jnp.concatenate([table, small], axis=0).astype(bf16))
     for k in (1, 2, 3):
         messages[k] = lax.ppermute(messages[k], ("core", "x", "y"), cross(k, 1))
     gathered = lax.all_to_all(grad_couple.reshape(16, 32, 512), LON, 0, 0, tiled=True)
+    result, gathered = lax.optimization_barrier((result[None], gathered))
     gathered = jnp.sum(gathered.astype(f32), axis=0)
     table = total_of(messages)
 
@@ -433,7 +504,7 @@
             table[:128].reshape(4, 4, 8, 512).transpose(1, 0, 2, 3).reshape(4, 32, 512),
             table[128:256].reshape(4, 32, 512),
             gathered.reshape(4, 8, 512),
-            jnp.broadcast_to(table[256:][None], (4, 64, 512)),
+            jnp.broadcast_to(table[256:][None], (4, 56, 512)),
         ],
         axis=1,
     ).astype(bf16)
@@ -441,28 +512,15 @@
     for k in (1, 2, 3):
         rows[k] = lax.ppermute(rows[k], "lat", ring(4, k))
     mine = total_of(rows).astype(bf16)
+    mine_beside = lax.ppermute(mine, "core", ring(2, 1))
     across = lax.ppermute(mine, "zh", ring(2, 1))
-    sums = jnp.where(zh == 0, jnp.stack([mine, across]), jnp.stack([across, mine]))
-    sums_beside = lax.ppermute(sums, "core", ring(2, 1)).astype(f32)
-    sums = sums.astype(f32)
-    first = jnp.where(core == 0, sums, sums_beside)
-    second = jnp.where(core == 0, sums_beside, sums)
-    air = (first[0] + second[0]) + first[1]
-    sea_part = second[1]
-
-    def split(total):
-        return (
-            total[72:128].reshape(7, 8, 512)[:, :7].reshape(49, 512),
-            total[128],
-            total[:32].reshape(4, 8, 512).transpose(1, 0, 2).reshape(8, 2048),
-            total[32:64],
-        )
-
+    across_beside = lax.ppermute(across, "core", ring(2, 1))
+    outs = finish(jnp.stack([zh, core]), mine, mine_beside, across, across_beside)
     return (
-        (result[None],)
-        + split(air)
-        + split(sea_part)
-        + (air[64:72], sea_part[64:72])
+        (result,)
+        + (outs[0], outs[1].reshape(512), outs[2], outs[3])
+        + (outs[4], outs[5].reshape(512), outs[6], outs[7])
+        + (outs[8], outs[9])
     )
 
 

time: 156 us -> 140 us (0.90); the launches traced: 156 us -> 138 us
  waiting for transfers between devices: 34.7 us -> 22.7 us
  local copies, waits for them, and re-layouts: 16.9 us -> 7 us
  starting transfers between devices: 57.3 us -> 65.8 us
  Pallas kernels: 38.9 us -> 32.9 us
  other arithmetic: 5.16 us -> 7.53 us
    slice x9 -> x2, local copies, waits for them, and re-layouts: 6.99 us -> 0.1 us  [the longest x1 0.08 us: edge(): sea[:, columns].astype(bf16)[:, :, None]]
    ppermute x3 -> x4, waiting for transfers between devices: 6.1 us -> 0.01 us  [the longest x1 0.01 us: on_device(): west = lax.ppermute(edge(slice(87, 90)), LON, ring(16, 1))]
    ppermute x3 -> x4, starting transfers between devices: 13.8 us -> 19.5 us  [the longest x1 10.6 us: on_device(): mine_beside = lax.ppermute(mine, 'core', ring(2, 1))]
    pallas_call x1, Pallas kernels: 18.8 us -> 14.2 us  [couple(): pl.pallas_call(couple_kernel, out_shape=jax.ShapeDtypeStruct((512, 512),...]
    ppermute x3, waiting for transfers between devices: 0.01 us -> 4.31 us  [on_device(): parts[k] = lax.ppermute(parts[k], ('core', 'x', 'y'), cross(k, 0))]
    ppermute x3, waiting for transfers between devices: 7.52 us -> 3.27 us  [on_device(): rows[k] = lax.ppermute(rows[k], 'lat', ring(4, k))]
    ppermute x1, waiting for transfers between devices: 3.28 us -> 0.01 us  [on_device(): across = lax.ppermute(mine, 'zh', ring(2, 1))]
    pallas_call x1, Pallas kernels: 20.2 us -> 17.2 us  [block(): pl.pallas_call(block_kernel, out_shape=(jax.ShapeDtypeStruct((4, 90, 512)...]
  transfers between devices with their start and end apart: 21 -> 22, of which waited for: 13 -> 10; matrix products, arithmetic and copies ran while one was open for 9% -> 6% of each run, Pallas kernels for 25% -> 23%
where the time goes in v2:
time: 140 us; the launch traced here: 138 us
  starting transfers between devices  65.8 us (47%)
  Pallas kernels  32.9 us (24%)
  waiting for transfers between devices  22.7 us (16%)
  other arithmetic  7.53 us (5%)
  local copies, waits for them, and re-layouts  7 us (5%)
    pallas_call x1, Pallas kernels, block(): pl.pallas_call(block_kernel, out_shape=(jax.ShapeDtypeStruct((4, 90, 512)...  17.2 us
    pallas_call x1, Pallas kernels, couple(): pl.pallas_call(couple_kernel, out_shape=jax.ShapeDtypeStruct((512, 512),...  14.2 us
    ppermute x1, starting transfers between devices, on_device(): mine_beside = lax.ppermute(mine, 'core', ring(2, 1))  10.6 us
    ppermute x2, starting transfers between devices, lat_halo(): north = lax.ppermute(tile[1:4], 'lat', [(i, i + 1) for i in range(3)])  9.57 us
    ppermute x3, waiting for transfers between devices, on_device(): messages[k] = lax.ppermute(messages[k], ('core', 'x', 'y'), cross(k, 1))  6.47 us
    all_to_all x1, starting transfers between devices, on_device(): lax.all_to_all(grad_couple.reshape(16, 32, 512), LON, 0, 0, tiled=True)  5.85 us
    ppermute x1, starting transfers between devices, on_device(): across = lax.ppermute(mine, 'zh', ring(2, 1))  5.42 us
    ppermute x1, starting transfers between devices, on_device(): got = lax.ppermute(half, 'zh', ring(2, 1))  5.26 us
  transfers between devices with their start and end apart: 22, of which 10 were waited for; matrix products, arithmetic and copies ran while one was open for 6% of the time, Pallas kernels for 23%

profile of v2, /device:TPU:1, one launch (start us, length us, event | category | flops | bytes accessed | tf_op | source)
XLA Modules:
  0.0 137.5 jit_solution(1952880925739374259)
XLA Ops:
  0.7 1.1 copy.38
  2.7 2.2 %collective-permute-start = (bf16[4,3,640]{2,1,0:T(4,128)(2,1)S(1)}, bf16[4,3,640]{2,1,0:T(4,128)(2,1)S(1)}, u32[]{:S(2)}, u32[]{:S(2)}) collective-permute-start(bf16[4,3,640]{2,1,0:T(4,128)(2,1)S(1)} %pad_maximum_fusion.6), channel_id=1, source_target_pairs={{0,4},{4,8},{8,12},{12,16},{16,20},{20,24},{24,28},{28,32},{32,36}... | collective-permute-start | bytes 46088 | tf_op jit(solution)/shard_map/ppermute | solution.py:411
  5.0 3.7 %collective-permute-start.1 = (bf16[4,3,640]{2,1,0:T(4,128)(2,1)S(1)}, bf16[4,3,640]{2,1,0:T(4,128)(2,1)S(1)}, u32[]{:S(2)}, u32[]{:S(2)}) collective-permute-start(bf16[4,3,640]{2,1,0:T(4,128)(2,1)S(1)} %pad_maximum_fusion.7), channel_id=1, source_target_pairs={{0,60},{4,0},{8,4},{12,8},{16,12},{20,16},{24,20},{28,24},{32,28},... | collective-permute-start | bytes 46088 | tf_op jit(solution)/shard_map/ppermute | solution.py:412
  11.7 2.9 %collective-permute-start.2 = (bf16[4,96,512]{2,1,0:T(8,128)(2,1)S(1)}, bf16[4,96,512]{2,1,0:T(8,128)(2,1)S(1)}, u32[]{:S(2)}, u32[]{:S(2)}) collective-permute-start(bf16[4,96,512]{2,1,0:T(8,128)(2,1)S(1)} %get-tuple-element.86), channel_id=1, source_target_pairs={{0,64},{64,0},{1,65},{65,1},{2,66},{66,2},{3,67},{67,3},{4,68},{68... | collective-permute-start | bytes 1179656 | tf_op jit(solution)/shard_map/ppermute | solution.py:418
  16.1 5.3 %collective-permute-start.3 = (bf16[2,96,512]{2,1,0:T(8,128)(2,1)S(1)}, bf16[2,96,512]{2,1,0:T(8,128)(2,1)S(1)}, u32[]{:S(2)}, u32[]{:S(2)}) collective-permute-start(bf16[2,96,512]{2,1,0:T(8,128)(2,1)S(1)} %fusion.6), channel_id=1, source_target_pairs={{0,128},{128,0},{1,129},{129,1},{2,130},{130,2},{3,131},{131,3},{4... | collective-permute-start | bytes 589832 | tf_op jit(solution)/shard_map/ppermute | solution.py:422
  21.5 4.7 %collective-permute-done.3 = bf16[2,96,512]{2,1,0:T(8,128)(2,1)S(1)} collective-permute-done((bf16[2,96,512]{2,1,0:T(8,128)(2,1)S(1)}, bf16[2,96,512]{2,1,0:T(8,128)(2,1)S(1)}, u32[]{:S(2)}, u32[]{:S(2)}) %collective-permute-start.3) | collective-permute-done | bytes 196640 | tf_op jit(solution)/shard_map/ppermute | solution.py:422
  27.0 2.4 %collective-permute-start.4 = (bf16[2,96,512]{2,1,0:T(8,128)(2,1)S(1)}, bf16[2,96,512]{2,1,0:T(8,128)(2,1)S(1)}, u32[]{:S(2)}, u32[]{:S(2)}) collective-permute-start(bf16[2,96,512]{2,1,0:T(8,128)(2,1)S(1)} %collective-permute-done.3), channel_id=1, source_target_pairs={{0,64},{64,0},{1,65},{65,1},{2,66},{66,2},{3,67},{67,3},{4,68},{68... | collective-permute-start | bytes 589832 | tf_op jit(solution)/shard_map/ppermute | solution.py:436
  31.3 5.6 %collective-permute-start.5 = (bf16[3,96,512]{2,1,0:T(8,128)(2,1)S(1)}, bf16[3,96,512]{2,1,0:T(8,128)(2,1)S(1)}, u32[]{:S(2)}, u32[]{:S(2)}) collective-permute-start(bf16[3,96,512]{2,1,0:T(8,128)(2,1)S(1)} %get-tuple-element.97), channel_id=1, source_target_pairs={{0,1},{1,2},{2,3},{4,5},{5,6},{6,7},{8,9},{9,10},{10,11},{12,13},{... | collective-permute-start | bytes 884744 | tf_op jit(solution)/shard_map/ppermute | solution.py:46
  36.9 1.3 collective-permute-start.6
  38.8 4.0 %collective-permute-start.7 = (bf16[3,96,512]{2,1,0:T(8,128)(2,1)S(1)}, bf16[3,96,512]{2,1,0:T(8,128)(2,1)S(1)}, u32[]{:S(2)}, u32[]{:S(2)}) collective-permute-start(bf16[3,96,512]{2,1,0:T(8,128)(2,1)S(1)} %get-tuple-element.95), channel_id=1, source_target_pairs={{0,1},{1,2},{2,3},{4,5},{5,6},{6,7},{8,9},{9,10},{10,11},{12,13},{... | collective-permute-start | bytes 884744 | tf_op jit(solution)/shard_map/ppermute | solution.py:46
  42.8 1.5 %collective-permute-start.8 = (bf16[3,96,512]{2,1,0:T(8,128)(2,1)S(1)}, bf16[3,96,512]{2,1,0:T(8,128)(2,1)S(1)}, u32[]{:S(2)}, u32[]{:S(2)}) collective-permute-start(bf16[3,96,512]{2,1,0:T(8,128)(2,1)S(1)} %get-tuple-element.94), channel_id=1, source_target_pairs={{1,0},{2,1},{3,2},{5,4},{6,5},{7,6},{9,8},{10,9},{11,10},{13,12},{... | collective-permute-start | bytes 884744 | tf_op jit(solution)/shard_map/ppermute | solution.py:47
  44.3 2.3 %collective-permute-done.6.south_ref = bf16[3,96,512]{2,1,0:T(8,128)(2,1)S(1)} collective-permute-done((bf16[3,96,512]{2,1,0:T(8,128)(2,1)S(1)}, bf16[3,96,512]{2,1,0:T(8,128)(2,1)S(1)}, u32[]{:S(2)}, u32[]{:S(2)}) %collective-permute-start.6) | collective-permute-done | bytes 294944 | tf_op jit(solution)/shard_map/ppermute | solution.py:47
  47.4 17.2 %block_kernel.1 = (bf16[4,90,512]{2,1,0:T(8,128)(2,1)}, bf16[1088,512]{1,0:T(8,128)(2,1)}, bf16[1088,512]{1,0:T(8,128)(2,1)}, bf16[1088,512]{1,0:T(8,128)(2,1)},...) custom-call(s32[4]{0:T(128)} %pad_add_fusion.ocean_ref, bf16[3,96,512]{2,1,0:T(8,128)(2,1)} %copy-done.12, ...), custom_call_target="tpu_custom_call" | custom-call | flops 4831838208 | bytes 12582912 | tf_op jit(solution)/shard_map/block_kernel/pallas_call | solution.py:268
  64.7 2.7 %collective-permute-start.11 = (bf16[1088,512]{1,0:T(8,128)(2,1)}, bf16[1088,512]{1,0:T(8,128)(2,1)}, u32[]{:S(2)}, u32[]{:S(2)}) collective-permute-start(bf16[1088,512]{1,0:T(8,128)(2,1)} %get-tuple-element.49), channel_id=1, source_target_pairs={{0,48},{4,52},{8,56},{12,60},{16,0},{20,4},{24,8},{28,12},{32,16},... | collective-permute-start | bytes 3342344 | tf_op jit(solution)/shard_map/ppermute | solution.py:477
  67.5 1.0 copy-done.1
  68.5 14.2 %couple_kernel.1 = bf16[512,512]{1,0:T(8,128)(2,1)} custom-call(bf16[3,96,512]{2,1,0:T(8,128)(2,1)S(1)} %collective-permute-done.7.north_ref, bf16[4,96,512]{2,1,0:T(8,128)(2,1)S(1)} %get-tuple-element.83.own_ref, bf16[3,96,512]{2,1,0:T(8,128)(2,1)S(1)} %collective-permute-done.8.south_ref, bf16[512,384]{1,0:T(8,128)(2,1)S(1)} %copy-done.1, ...), custom_call_target="tpu_custom_call" | custom-call | flops 10066329600 | bytes 4194304 | tf_op jit(solution)/shard_map/couple_kernel/pallas_call | solution.py:330
  82.7 5.9 %all-to-all-start = ((bf16[16,32,512]{2,1,0:T(8,128)(2,1)}), bf16[16,32,512]{2,1,0:T(8,128)(2,1)S(1)}, u32[]{:S(2)}, u32[]{:S(2)}) async-start(bf16[16,32,512]{2,1,0:T(8,128)(2,1)} %bitcast.14), calls=%async_computation | async-start | bytes 1048576 | tf_op jit(solution)/shard_map/all_to_all | solution.py:497
  88.6 3.8 %collective-permute-done.11 = bf16[1088,512]{1,0:T(8,128)(2,1)} collective-permute-done((bf16[1088,512]{1,0:T(8,128)(2,1)}, bf16[1088,512]{1,0:T(8,128)(2,1)}, u32[]{:S(2)}, u32[]{:S(2)}) %collective-permute-start.11) | collective-permute-done | bytes 1114144 | tf_op jit(solution)/shard_map/ppermute | solution.py:477
  93.8 2.4 %add_convert_fusion.5 = (bf16[256,512]{1,0:T(8,128)(2,1)S(1)}, bf16[256,512]{1,0:T(8,128)(2,1)S(1)}, bf16[256,512]{1,0:T(8,128)(2,1)S(1)}, bf16[256,512]{1,0:T(8,128)(2,1)S(1)}) fusion(bf16[1088,512]{1,0:T(8,128)(2,1)} %collective-permute-done.11, s32[]{:T(128)S(6)} %select_n.147, bf16[1088,512]{1,0:T(8,128)(2,1)} %collective-permute-done.10, ...), kind=kLoop, calls=%fused_computation.15 | loop fusion | flops 4194304 | bytes 5242896 | tf_op jit(solution)/shard_map/convert.22
  96.3 2.2 %collective-permute-start.12 = (bf16[312,512]{1,0:T(8,128)(2,1)S(1)}, bf16[312,512]{1,0:T(8,128)(2,1)S(1)}, u32[]{:S(2)}, u32[]{:S(2)}) collective-permute-start(bf16[312,512]{1,0:T(8,128)(2,1)S(1)} %get-tuple-element.102), channel_id=1, source_target_pairs={{0,8},{4,12},{8,0},{12,4},{16,24},{20,28},{24,16},{28,20},{32,40},... | collective-permute-start | bytes 958472 | tf_op jit(solution)/shard_map/ppermute | solution.py:496
  98.5 1.1 collective-permute-start.13
  99.6 1.6 %collective-permute-start.14 = (bf16[312,512]{1,0:T(8,128)(2,1)S(1)}, bf16[312,512]{1,0:T(8,128)(2,1)S(1)}, u32[]{:S(2)}, u32[]{:S(2)}) collective-permute-start(bf16[312,512]{1,0:T(8,128)(2,1)S(1)} %get-tuple-element.104), channel_id=1, source_target_pairs={{0,12},{4,0},{8,4},{12,8},{16,28},{20,16},{24,20},{28,24},{32,44},... | collective-permute-start | bytes 958472 | tf_op jit(solution)/shard_map/ppermute | solution.py:496
  101.3 2.5 %collective-permute-done.12 = bf16[312,512]{1,0:T(8,128)(2,1)S(1)} collective-permute-done((bf16[312,512]{1,0:T(8,128)(2,1)S(1)}, bf16[312,512]{1,0:T(8,128)(2,1)S(1)}, u32[]{:S(2)}, u32[]{:S(2)}) %collective-permute-start.12) | collective-permute-done | bytes 319520 | tf_op jit(solution)/shard_map/ppermute | solution.py:496
  103.8 3.7 %collective-permute-done.13 = bf16[312,512]{1,0:T(8,128)(2,1)S(1)} collective-permute-done((bf16[312,512]{1,0:T(8,128)(2,1)S(1)}, bf16[312,512]{1,0:T(8,128)(2,1)S(1)}, u32[]{:S(2)}, u32[]{:S(2)}) %collective-permute-start.13) | collective-permute-done | bytes 319520 | tf_op jit(solution)/shard_map/ppermute | solution.py:496
  108.1 1.1 collective-permute-start.15
  109.3 3.2 %collective-permute-start.17 = (bf16[128,512]{1,0:T(8,128)(2,1)S(1)}, bf16[128,512]{1,0:T(8,128)(2,1)S(1)}, u32[]{:S(2)}, u32[]{:S(2)}) collective-permute-start(bf16[128,512]{1,0:T(8,128)(2,1)S(1)} %get-tuple-element.92), channel_id=1, source_target_pairs={{0,3},{1,0},{2,1},{3,2},{4,7},{5,4},{6,5},{7,6},{8,11},{9,8},{10,9... | collective-permute-start | bytes 393224 | tf_op jit(solution)/shard_map/ppermute | solution.py:513
  112.5 3.3 %collective-permute-done.15 = bf16[128,512]{1,0:T(8,128)(2,1)S(1)} collective-permute-done((bf16[128,512]{1,0:T(8,128)(2,1)S(1)}, bf16[128,512]{1,0:T(8,128)(2,1)S(1)}, u32[]{:S(2)}, u32[]{:S(2)}) %collective-permute-start.15) | collective-permute-done | bytes 131104 | tf_op jit(solution)/shard_map/ppermute | solution.py:513
  115.8 5.4 %collective-permute-start.19 = (bf16[128,512]{1,0:T(8,128)(2,1)S(1)}, bf16[128,512]{1,0:T(8,128)(2,1)S(1)}, u32[]{:S(2)}, u32[]{:S(2)}) collective-permute-start(bf16[128,512]{1,0:T(8,128)(2,1)S(1)} %fusion.5.mine_ref), channel_id=1, source_target_pairs={{0,128},{128,0},{1,129},{129,1},{2,130},{130,2},{3,131},{131,3},{4... | collective-permute-start | bytes 393224 | tf_op jit(solution)/shard_map/ppermute | solution.py:516
  121.2 10.6 %collective-permute-start.18 = (bf16[128,512]{1,0:T(8,128)(2,1)S(1)}, bf16[128,512]{1,0:T(8,128)(2,1)S(1)}, u32[]{:S(2)}, u32[]{:S(2)}) collective-permute-start(bf16[128,512]{1,0:T(8,128)(2,1)S(1)} %fusion.5.mine_ref), channel_id=1, source_target_pairs={{0,64},{64,0},{1,65},{65,1},{2,66},{66,2},{3,67},{67,3},{4,68},{68... | collective-permute-start | bytes 393224 | tf_op jit(solution)/shard_map/ppermute | solution.py:515
  131.9 3.0 %collective-permute-start.20 = (bf16[128,512]{1,0:T(8,128)(2,1)S(1)}, bf16[128,512]{1,0:T(8,128)(2,1)S(1)}, u32[]{:S(2)}, u32[]{:S(2)}) collective-permute-start(bf16[128,512]{1,0:T(8,128)(2,1)S(1)} %collective-permute-done.19.across_ref), channel_id=1, source_target_pairs={{0,64},{64,0},{1,65},{65,1},{2,66},{66,2},{3,67},{67,3},{4,68},{68... | collective-permute-start | bytes 393224 | tf_op jit(solution)/shard_map/ppermute | solution.py:517
  134.9 1.0 copy.33
  136.0 1.5 %finish_kernel.1 = (f32[49,512]{1,0:T(8,128)}, f32[1,512]{1,0:T(1,128)}, f32[8,2048]{1,0:T(8,128)}, f32[32,512]{1,0:T(8,128)}, f32[49,512]{1,0:T(8,128)}, /*inde...) custom-call(s32[2]{0:T(128)S(1)} %pad_add_fusion.1.place_ref, ...), custom_call_target="tpu_custom_call" | custom-call | tf_op jit(solution)/shard_map/finish_kernel/pallas_call | solution.py:375
  (94 shorter events, 12.1 us)
Async XLA Ops:
  0.6 8.7 %copy-start.7 = (bf16[1,4,90,512]{3,1,2,0:T(4,128)(2,1)S(1)}, bf16[1,4,90,512]{3,1,2,0:T(4,128)(2,1)}, u32[]{:S(2)}) copy-start(bf16[1,4,90,512]{3,1,2,0:T(4,128)(2,1)} %param.14) | copy-start | bytes 1105924
  0.7 8.9 %copy-start.9 = (f32[49,512]{1,0:T(8,128)S(1)}, f32[49,512]{1,0:T(8,128)}, u32[]{:S(2)}) copy-start(f32[49,512]{1,0:T(8,128)} %param.16) | copy-start | bytes 301060
  0.7 8.9 %copy-start.8 = (f32[49,512]{1,0:T(8,128)S(1)}, f32[49,512]{1,0:T(8,128)}, u32[]{:S(2)}) copy-start(f32[49,512]{1,0:T(8,128)} %param.20) | copy-start | bytes 301060
  2.7 8.8 %collective-permute-start = (bf16[4,3,640]{2,1,0:T(4,128)(2,1)S(1)}, bf16[4,3,640]{2,1,0:T(4,128)(2,1)S(1)}, u32[]{:S(2)}, u32[]{:S(2)}) collective-permute-start(bf16[4,3,640]{2,1,0:T(4,128)(2,1)S(1)} %pad_maximum_fusion.6), channel_id=1, source_target_pairs={{0,4},{4,8},{8,12},{12,16},{16,20},{20,24},{24,28},{28,32},{32,36}... | collective-permute-start | bytes 46088 | tf_op jit(solution)/shard_map/ppermute | solution.py:411
  5.0 6.5 %collective-permute-start.1 = (bf16[4,3,640]{2,1,0:T(4,128)(2,1)S(1)}, bf16[4,3,640]{2,1,0:T(4,128)(2,1)S(1)}, u32[]{:S(2)}, u32[]{:S(2)}) collective-permute-start(bf16[4,3,640]{2,1,0:T(4,128)(2,1)S(1)} %pad_maximum_fusion.7), channel_id=1, source_target_pairs={{0,60},{4,0},{8,4},{12,8},{16,12},{20,16},{24,20},{28,24},{32,28},... | collective-permute-start | bytes 46088 | tf_op jit(solution)/shard_map/ppermute | solution.py:412
  10.6 4.0 %copy-start.10 = (f32[512]{0:T(512)S(1)}, f32[512]{0:T(512)}, u32[]{:S(2)}) copy-start(f32[512]{0:T(512)} %param.21) | copy-start | bytes 6148
  10.6 4.6 %copy-start.4 = (bf16[512,512]{1,0:T(8,128)(2,1)S(1)}, bf16[512,512]{1,0:T(8,128)(2,1)}, u32[]{:S(2)}) copy-start(bf16[512,512]{1,0:T(8,128)(2,1)} %param.25) | copy-start | bytes 1572868
  10.6 4.5 %copy-start.5 = (bf16[512,512]{1,0:T(8,128)(2,1)S(1)}, bf16[512,512]{1,0:T(8,128)(2,1)}, u32[]{:S(2)}) copy-start(bf16[512,512]{1,0:T(8,128)(2,1)} %param.24) | copy-start | bytes 1572868
  11.7 4.3 %collective-permute-start.2 = (bf16[4,96,512]{2,1,0:T(8,128)(2,1)S(1)}, bf16[4,96,512]{2,1,0:T(8,128)(2,1)S(1)}, u32[]{:S(2)}, u32[]{:S(2)}) collective-permute-start(bf16[4,96,512]{2,1,0:T(8,128)(2,1)S(1)} %get-tuple-element.86), channel_id=1, source_target_pairs={{0,64},{64,0},{1,65},{65,1},{2,66},{66,2},{3,67},{67,3},{4,68},{68... | collective-permute-start | bytes 1179656 | tf_op jit(solution)/shard_map/ppermute | solution.py:418
  16.1 10.1 %collective-permute-start.3 = (bf16[2,96,512]{2,1,0:T(8,128)(2,1)S(1)}, bf16[2,96,512]{2,1,0:T(8,128)(2,1)S(1)}, u32[]{:S(2)}, u32[]{:S(2)}) collective-permute-start(bf16[2,96,512]{2,1,0:T(8,128)(2,1)S(1)} %fusion.6), channel_id=1, source_target_pairs={{0,128},{128,0},{1,129},{129,1},{2,130},{130,2},{3,131},{131,3},{4... | collective-permute-start | bytes 589832 | tf_op jit(solution)/shard_map/ppermute | solution.py:422
  27.0 3.4 %collective-permute-start.4 = (bf16[2,96,512]{2,1,0:T(8,128)(2,1)S(1)}, bf16[2,96,512]{2,1,0:T(8,128)(2,1)S(1)}, u32[]{:S(2)}, u32[]{:S(2)}) collective-permute-start(bf16[2,96,512]{2,1,0:T(8,128)(2,1)S(1)} %collective-permute-done.3), channel_id=1, source_target_pairs={{0,64},{64,0},{1,65},{65,1},{2,66},{66,2},{3,67},{67,3},{4,68},{68... | collective-permute-start | bytes 589832 | tf_op jit(solution)/shard_map/ppermute | solution.py:436
  31.2 7.6 %copy-start.2 = (bf16[4,96,512]{2,1,0:T(8,128)(2,1)}, bf16[4,96,512]{2,1,0:T(8,128)(2,1)S(1)}, u32[]{:S(2)}) copy-start(bf16[4,96,512]{2,1,0:T(8,128)(2,1)S(1)} %add_convert_fusion.own_ref) | copy-start | bytes 1179652
  31.3 13.0 %collective-permute-start.5 = (bf16[3,96,512]{2,1,0:T(8,128)(2,1)S(1)}, bf16[3,96,512]{2,1,0:T(8,128)(2,1)S(1)}, u32[]{:S(2)}, u32[]{:S(2)}) collective-permute-start(bf16[3,96,512]{2,1,0:T(8,128)(2,1)S(1)} %get-tuple-element.97), channel_id=1, source_target_pairs={{0,1},{1,2},{2,3},{4,5},{5,6},{6,7},{8,9},{9,10},{10,11},{12,13},{... | collective-permute-start | bytes 884744 | tf_op jit(solution)/shard_map/ppermute | solution.py:46
  36.9 9.8 %collective-permute-start.6 = (bf16[3,96,512]{2,1,0:T(8,128)(2,1)S(1)}, bf16[3,96,512]{2,1,0:T(8,128)(2,1)S(1)}, u32[]{:S(2)}, u32[]{:S(2)}) collective-permute-start(bf16[3,96,512]{2,1,0:T(8,128)(2,1)S(1)} %get-tuple-element.96), channel_id=1, source_target_pairs={{1,0},{2,1},{3,2},{5,4},{6,5},{7,6},{9,8},{10,9},{11,10},{13,12},{... | collective-permute-start | bytes 884744 | tf_op jit(solution)/shard_map/ppermute | solution.py:47
  38.8 28.7 %collective-permute-start.7 = (bf16[3,96,512]{2,1,0:T(8,128)(2,1)S(1)}, bf16[3,96,512]{2,1,0:T(8,128)(2,1)S(1)}, u32[]{:S(2)}, u32[]{:S(2)}) collective-permute-start(bf16[3,96,512]{2,1,0:T(8,128)(2,1)S(1)} %get-tuple-element.95), channel_id=1, source_target_pairs={{0,1},{1,2},{2,3},{4,5},{5,6},{6,7},{8,9},{9,10},{10,11},{12,13},{... | collective-permute-start | bytes 884744 | tf_op jit(solution)/shard_map/ppermute | solution.py:46
  42.8 24.7 %collective-permute-start.8 = (bf16[3,96,512]{2,1,0:T(8,128)(2,1)S(1)}, bf16[3,96,512]{2,1,0:T(8,128)(2,1)S(1)}, u32[]{:S(2)}, u32[]{:S(2)}) collective-permute-start(bf16[3,96,512]{2,1,0:T(8,128)(2,1)S(1)} %get-tuple-element.94), channel_id=1, source_target_pairs={{1,0},{2,1},{3,2},{5,4},{6,5},{7,6},{9,8},{10,9},{11,10},{13,12},{... | collective-permute-start | bytes 884744 | tf_op jit(solution)/shard_map/ppermute | solution.py:47
  47.4 20.1 %copy-start = (bf16[4,96,512]{2,1,0:T(8,128)(2,1)S(1)}, bf16[4,96,512]{2,1,0:T(8,128)(2,1)}, u32[]{:S(2)}) copy-start(bf16[4,96,512]{2,1,0:T(8,128)(2,1)} %pad.14.cot_ref) | copy-start | bytes 1179652
  64.6 24.0 %collective-permute-start.10 = (bf16[1088,512]{1,0:T(8,128)(2,1)}, bf16[1088,512]{1,0:T(8,128)(2,1)}, u32[]{:S(2)}, u32[]{:S(2)}) collective-permute-start(bf16[1088,512]{1,0:T(8,128)(2,1)} %get-tuple-element.48), channel_id=1, source_target_pairs={{0,16},{4,20},{8,24},{12,28},{16,32},{20,36},{24,40},{28,44},{32,4... | collective-permute-start | bytes 3342344 | tf_op jit(solution)/shard_map/ppermute | solution.py:477
  64.7 27.7 %collective-permute-start.11 = (bf16[1088,512]{1,0:T(8,128)(2,1)}, bf16[1088,512]{1,0:T(8,128)(2,1)}, u32[]{:S(2)}, u32[]{:S(2)}) collective-permute-start(bf16[1088,512]{1,0:T(8,128)(2,1)} %get-tuple-element.49), channel_id=1, source_target_pairs={{0,48},{4,52},{8,56},{12,60},{16,0},{20,4},{24,8},{28,12},{32,16},... | collective-permute-start | bytes 3342344 | tf_op jit(solution)/shard_map/ppermute | solution.py:477
  67.3 25.6 %collective-permute-start.9 = (bf16[1088,512]{1,0:T(8,128)(2,1)}, bf16[1088,512]{1,0:T(8,128)(2,1)}, u32[]{:S(2)}, u32[]{:S(2)}) collective-permute-start(bf16[1088,512]{1,0:T(8,128)(2,1)} %get-tuple-element.47), channel_id=1, source_target_pairs={{0,32},{4,36},{8,40},{12,44},{16,48},{20,52},{24,56},{28,60},{32,0... | collective-permute-start | bytes 3342344 | tf_op jit(solution)/shard_map/ppermute | solution.py:477
  68.5 24.4 %copy-start.3 = (bf16[1088,512]{1,0:T(8,128)(2,1)S(1)}, bf16[1088,512]{1,0:T(8,128)(2,1)}, u32[]{:S(2)}) copy-start(bf16[1088,512]{1,0:T(8,128)(2,1)} %get-tuple-element.46) | copy-start | bytes 3342340
  82.7 18.5 %all-to-all-start = ((bf16[16,32,512]{2,1,0:T(8,128)(2,1)}), bf16[16,32,512]{2,1,0:T(8,128)(2,1)S(1)}, u32[]{:S(2)}, u32[]{:S(2)}) async-start(bf16[16,32,512]{2,1,0:T(8,128)(2,1)} %bitcast.14), calls=%async_computation | async-start | bytes 1048576 | tf_op jit(solution)/shard_map/all_to_all | solution.py:497
  96.3 7.5 %collective-permute-start.12 = (bf16[312,512]{1,0:T(8,128)(2,1)S(1)}, bf16[312,512]{1,0:T(8,128)(2,1)S(1)}, u32[]{:S(2)}, u32[]{:S(2)}) collective-permute-start(bf16[312,512]{1,0:T(8,128)(2,1)S(1)} %get-tuple-element.102), channel_id=1, source_target_pairs={{0,8},{4,12},{8,0},{12,4},{16,24},{20,28},{24,16},{28,20},{32,40},... | collective-permute-start | bytes 958472 | tf_op jit(solution)/shard_map/ppermute | solution.py:496
  98.5 8.9 %collective-permute-start.13 = (bf16[312,512]{1,0:T(8,128)(2,1)S(1)}, bf16[312,512]{1,0:T(8,128)(2,1)S(1)}, u32[]{:S(2)}, u32[]{:S(2)}) collective-permute-start(bf16[312,512]{1,0:T(8,128)(2,1)S(1)} %get-tuple-element.103), channel_id=1, source_target_pairs={{0,4},{4,8},{8,12},{12,0},{16,20},{20,24},{24,28},{28,16},{32,36},... | collective-permute-start | bytes 958472 | tf_op jit(solution)/shard_map/ppermute | solution.py:496
  99.6 8.1 %collective-permute-start.14 = (bf16[312,512]{1,0:T(8,128)(2,1)S(1)}, bf16[312,512]{1,0:T(8,128)(2,1)S(1)}, u32[]{:S(2)}, u32[]{:S(2)}) collective-permute-start(bf16[312,512]{1,0:T(8,128)(2,1)S(1)} %get-tuple-element.104), channel_id=1, source_target_pairs={{0,12},{4,0},{8,4},{12,8},{16,28},{20,16},{24,20},{28,24},{32,44},... | collective-permute-start | bytes 958472 | tf_op jit(solution)/shard_map/ppermute | solution.py:496
  108.0 26.9 %copy-start.6 = (bf16[4,90,512]{2,1,0:T(8,128)(2,1)S(1)}, bf16[4,90,512]{2,1,0:T(8,128)(2,1)}, u32[]{:S(2)}) copy-start(bf16[4,90,512]{2,1,0:T(8,128)(2,1)} %get-tuple-element.42) | copy-start | bytes 1105924
  108.1 7.6 %collective-permute-start.15 = (bf16[128,512]{1,0:T(8,128)(2,1)S(1)}, bf16[128,512]{1,0:T(8,128)(2,1)S(1)}, u32[]{:S(2)}, u32[]{:S(2)}) collective-permute-start(bf16[128,512]{1,0:T(8,128)(2,1)S(1)} %get-tuple-element.91), channel_id=1, source_target_pairs={{0,2},{1,3},{2,0},{3,1},{4,6},{5,7},{6,4},{7,5},{8,10},{9,11},{10,... | collective-permute-start | bytes 393224 | tf_op jit(solution)/shard_map/ppermute | solution.py:513
  109.2 6.5 %collective-permute-start.16 = (bf16[128,512]{1,0:T(8,128)(2,1)S(1)}, bf16[128,512]{1,0:T(8,128)(2,1)S(1)}, u32[]{:S(2)}, u32[]{:S(2)}) collective-permute-start(bf16[128,512]{1,0:T(8,128)(2,1)S(1)} %get-tuple-element.93), channel_id=1, source_target_pairs={{0,1},{1,2},{2,3},{3,0},{4,5},{5,6},{6,7},{7,4},{8,9},{9,10},{10,1... | collective-permute-start | bytes 393224 | tf_op jit(solution)/shard_map/ppermute | solution.py:513
  109.3 6.4 %collective-permute-start.17 = (bf16[128,512]{1,0:T(8,128)(2,1)S(1)}, bf16[128,512]{1,0:T(8,128)(2,1)S(1)}, u32[]{:S(2)}, u32[]{:S(2)}) collective-permute-start(bf16[128,512]{1,0:T(8,128)(2,1)S(1)} %get-tuple-element.92), channel_id=1, source_target_pairs={{0,3},{1,0},{2,1},{3,2},{4,7},{5,4},{6,5},{7,6},{8,11},{9,8},{10,9... | collective-permute-start | bytes 393224 | tf_op jit(solution)/shard_map/ppermute | solution.py:513
  115.8 16.1 %collective-permute-start.19 = (bf16[128,512]{1,0:T(8,128)(2,1)S(1)}, bf16[128,512]{1,0:T(8,128)(2,1)S(1)}, u32[]{:S(2)}, u32[]{:S(2)}) collective-permute-start(bf16[128,512]{1,0:T(8,128)(2,1)S(1)} %fusion.5.mine_ref), channel_id=1, source_target_pairs={{0,128},{128,0},{1,129},{129,1},{2,130},{130,2},{3,131},{131,3},{4... | collective-permute-start | bytes 393224 | tf_op jit(solution)/shard_map/ppermute | solution.py:516
  121.2 14.7 %collective-permute-start.18 = (bf16[128,512]{1,0:T(8,128)(2,1)S(1)}, bf16[128,512]{1,0:T(8,128)(2,1)S(1)}, u32[]{:S(2)}, u32[]{:S(2)}) collective-permute-start(bf16[128,512]{1,0:T(8,128)(2,1)S(1)} %fusion.5.mine_ref), channel_id=1, source_target_pairs={{0,64},{64,0},{1,65},{65,1},{2,66},{66,2},{3,67},{67,3},{4,68},{68... | collective-permute-start | bytes 393224 | tf_op jit(solution)/shard_map/ppermute | solution.py:515
  131.9 4.1 %collective-permute-start.20 = (bf16[128,512]{1,0:T(8,128)(2,1)S(1)}, bf16[128,512]{1,0:T(8,128)(2,1)S(1)}, u32[]{:S(2)}, u32[]{:S(2)}) collective-permute-start(bf16[128,512]{1,0:T(8,128)(2,1)S(1)} %collective-permute-done.19.across_ref), channel_id=1, source_target_pairs={{0,64},{64,0},{1,65},{65,1},{2,66},{66,2},{3,67},{67,3},{4,68},{68... | collective-permute-start | bytes 393224 | tf_op jit(solution)/shard_map/ppermute | solution.py:517
  (4 other events, 8.1 us)

commit v3 on v2

--- a/solution.py
+++ b/solution.py
@@ -263,7 +263,7 @@
 
 def block(ocean, north, own, south, cot, mask, kern, gain, wia, woa, wis, wos):
     vmem = pl.BlockSpec(memory_space=pltpu.VMEM)
-    hbm = pl.BlockSpec(memory_space=pl.ANY)
+    hbm = pl.BlockSpec(memory_space=pltpu.HBM)
     flops = 2 * 6 * 384 * 512 * 2048
     return pl.pallas_call(
         block_kernel,
@@ -290,7 +290,7 @@
             *[pltpu.VMEM((1088, 512), bf16)] * 4,
             pltpu.SemaphoreType.DMA((16,)),
         ],
-        compiler_params=pltpu.CompilerParams(vmem_limit_bytes=56 * 1024 * 1024),
+        compiler_params=pltpu.CompilerParams(vmem_limit_bytes=40 * 1024 * 1024),
         cost_estimate=pl.CostEstimate(
             flops=flops, bytes_accessed=12 * 1024 * 1024, transcendentals=384 * 2048
         ),
@@ -361,12 +361,12 @@
     total[1] = jnp.where(first_core, far_beside, far)
     for n in range(2):
         kern_ref, gain_ref, expand_ref, contract_ref = outs[n * 4 : n * 4 + 4]
-        kern_ref[...] = total[n, 72:121, :]
-        gain_ref[...] = total[n, 121:122, :]
+        kern_ref[...] = total[n, 64:113, :]
+        gain_ref[...] = total[n, 113:114, :]
         for cb in range(4):
             expand_ref[:, cb * 512 : cb * 512 + 512] = total[n, cb * 8 : cb * 8 + 8, :]
         contract_ref[...] = total[n, 32:64, :]
-        outs[8 + n][...] = total[n, 64:72, :]
+        outs[8 + n][...] = total[n, 120:128, :]
 
 
 def finish(here, mine, mine_beside, across, across_beside):
@@ -494,8 +494,13 @@
         messages.append(jnp.concatenate([table, small], axis=0).astype(bf16))
     for k in (1, 2, 3):
         messages[k] = lax.ppermute(messages[k], ("core", "x", "y"), cross(k, 1))
-    gathered = lax.all_to_all(grad_couple.reshape(16, 32, 512), LON, 0, 0, tiled=True)
-    result, gathered = lax.optimization_barrier((result[None], gathered))
+    shares = grad_couple.reshape(16, 4, 8, 512)
+    shares = [
+        lax.dynamic_index_in_dim(shares, lax.rem(lat + k, 4), 1, keepdims=False) for k in range(4)
+    ]
+    for k in (1, 2, 3):
+        shares[k] = lax.ppermute(shares[k], "lat", ring(4, k))
+    gathered = lax.all_to_all(total_of(shares).astype(bf16), LON, 0, 0, tiled=True)
     gathered = jnp.sum(gathered.astype(f32), axis=0)
     table = total_of(messages)
 
@@ -503,7 +508,6 @@
         [
             table[:128].reshape(4, 4, 8, 512).transpose(1, 0, 2, 3).reshape(4, 32, 512),
             table[128:256].reshape(4, 32, 512),
-            gathered.reshape(4, 8, 512),
             jnp.broadcast_to(table[256:][None], (4, 56, 512)),
         ],
         axis=1,
@@ -511,13 +515,13 @@
     rows = [place(pieces, lax.rem(lat + k, 4)) for k in range(4)]
     for k in (1, 2, 3):
         rows[k] = lax.ppermute(rows[k], "lat", ring(4, k))
-    mine = total_of(rows).astype(bf16)
+    mine = jnp.concatenate([total_of(rows), gathered], axis=0).astype(bf16)
     mine_beside = lax.ppermute(mine, "core", ring(2, 1))
     across = lax.ppermute(mine, "zh", ring(2, 1))
     across_beside = lax.ppermute(across, "core", ring(2, 1))
     outs = finish(jnp.stack([zh, core]), mine, mine_beside, across, across_beside)
     return (
-        (result,)
+        (result[None],)
         + (outs[0], outs[1].reshape(512), outs[2], outs[3])
         + (outs[4], outs[5].reshape(512), outs[6], outs[7])
         + (outs[8], outs[9])

time: 140 us -> 135 us (0.964); the launches traced: 138 us -> 134 us
  waiting for transfers between devices: 22.7 us -> 19.2 us
  Pallas kernels: 32.9 us -> 31 us
  other arithmetic: 7.53 us -> 9.09 us
  starting transfers between devices: 65.8 us -> 67.2 us
    ppermute x3, waiting for transfers between devices: 6.47 us -> 1.05 us  [on_device(): messages[k] = lax.ppermute(messages[k], ('core', 'x', 'y'), cross(k, 1))]
    ppermute x0 -> x3, starting transfers between devices: none -> 4.4 us  [on_device(): shares[k] = lax.ppermute(shares[k], 'lat', ring(4, k))]
    ppermute x1, starting transfers between devices: 10.6 us -> 7.35 us  [on_device(): mine_beside = lax.ppermute(mine, 'core', ring(2, 1))]
    all_to_all x1, starting transfers between devices: 5.85 us -> 3.51 us  [on_device(): lax.all_to_all(total_of(shares).astype(bf16), LON, 0, 0, tiled=True)]
    convert_element_type x1, other arithmetic: 0.07 us -> 1.7 us  [on_device(): total_of(shares).astype(bf16)]
    another operation x2 -> x3, other arithmetic: 3.3 us -> 3.38 us
    unnamed x30 -> x26, local copies, waits for them, and re-layouts: 3.92 us -> 3.91 us
  transfers between devices with their start and end apart: 22 -> 25, of which waited for: 10 -> 9; matrix products, arithmetic and copies ran while one was open for 6% -> 8% of each run, Pallas kernels for 23% -> 22%
where the time goes in v3:
time: 135 us; the launch traced here: 134 us
  starting transfers between devices  67.2 us (50%)
  Pallas kernels  31 us (23%)
  waiting for transfers between devices  19.2 us (14%)
  other arithmetic  9.09 us (7%)
  local copies, waits for them, and re-layouts  6.25 us (5%)
    pallas_call x1, Pallas kernels, block(): pl.pallas_call(block_kernel, out_shape=(jax.ShapeDtypeStruct((4, 90, 512)...  16.2 us
    pallas_call x1, Pallas kernels, couple(): pl.pallas_call(couple_kernel, out_shape=jax.ShapeDtypeStruct((512, 512),...  13.4 us
    ppermute x2, starting transfers between devices, lat_halo(): north = lax.ppermute(tile[1:4], 'lat', [(i, i + 1) for i in range(3)])  9.82 us
    ppermute x1, starting transfers between devices, on_device(): mine_beside = lax.ppermute(mine, 'core', ring(2, 1))  7.35 us
    ppermute x3, waiting for transfers between devices, on_device(): parts[k] = lax.ppermute(parts[k], ('core', 'x', 'y'), cross(k, 0))  5.69 us
    ppermute x1, starting transfers between devices, on_device(): across = lax.ppermute(mine, 'zh', ring(2, 1))  5.29 us
    ppermute x1, starting transfers between devices, on_device(): got = lax.ppermute(half, 'zh', ring(2, 1))  5.26 us
    ppermute x3, starting transfers between devices, on_device(): messages[k] = lax.ppermute(messages[k], ('core', 'x', 'y'), cross(k, 1))  5.23 us
  transfers between devices with their start and end apart: 25, of which 9 were waited for; matrix products, arithmetic and copies ran while one was open for 8% of the time, Pallas kernels for 22%

profile of v3, /device:TPU:1, one launch (start us, length us, event | category | flops | bytes accessed | tf_op | source)
XLA Modules:
  0.0 134.4 jit_solution(9716676125800120612)
XLA Ops:
  0.7 1.1 copy.38
  2.7 2.2 %collective-permute-start = (bf16[4,3,640]{2,1,0:T(4,128)(2,1)S(1)}, bf16[4,3,640]{2,1,0:T(4,128)(2,1)S(1)}, u32[]{:S(2)}, u32[]{:S(2)}) collective-permute-start(bf16[4,3,640]{2,1,0:T(4,128)(2,1)S(1)} %pad_maximum_fusion.7), channel_id=1, source_target_pairs={{0,4},{4,8},{8,12},{12,16},{16,20},{20,24},{24,28},{28,32},{32,36}... | collective-permute-start | bytes 46088 | tf_op jit(solution)/shard_map/ppermute | solution.py:411
  5.0 3.7 %collective-permute-start.1 = (bf16[4,3,640]{2,1,0:T(4,128)(2,1)S(1)}, bf16[4,3,640]{2,1,0:T(4,128)(2,1)S(1)}, u32[]{:S(2)}, u32[]{:S(2)}) collective-permute-start(bf16[4,3,640]{2,1,0:T(4,128)(2,1)S(1)} %pad_maximum_fusion.8), channel_id=1, source_target_pairs={{0,60},{4,0},{8,4},{12,8},{16,12},{20,16},{24,20},{28,24},{32,28},... | collective-permute-start | bytes 46088 | tf_op jit(solution)/shard_map/ppermute | solution.py:412
  10.3 3.1 %collective-permute-start.2 = (bf16[4,96,512]{2,1,0:T(8,128)(2,1)S(1)}, bf16[4,96,512]{2,1,0:T(8,128)(2,1)S(1)}, u32[]{:S(2)}, u32[]{:S(2)}) collective-permute-start(bf16[4,96,512]{2,1,0:T(8,128)(2,1)S(1)} %get-tuple-element.82), channel_id=1, source_target_pairs={{0,64},{64,0},{1,65},{65,1},{2,66},{66,2},{3,67},{67,3},{4,68},{68... | collective-permute-start | bytes 1179656 | tf_op jit(solution)/shard_map/ppermute | solution.py:418
  13.5 1.3 collective-permute-done.2
  14.9 5.3 %collective-permute-start.3 = (bf16[2,96,512]{2,1,0:T(8,128)(2,1)S(1)}, bf16[2,96,512]{2,1,0:T(8,128)(2,1)S(1)}, u32[]{:S(2)}, u32[]{:S(2)}) collective-permute-start(bf16[2,96,512]{2,1,0:T(8,128)(2,1)S(1)} %fusion.8), channel_id=1, source_target_pairs={{0,128},{128,0},{1,129},{129,1},{2,130},{130,2},{3,131},{131,3},{4... | collective-permute-start | bytes 589832 | tf_op jit(solution)/shard_map/ppermute | solution.py:422
  20.3 4.7 %collective-permute-done.3 = bf16[2,96,512]{2,1,0:T(8,128)(2,1)S(1)} collective-permute-done((bf16[2,96,512]{2,1,0:T(8,128)(2,1)S(1)}, bf16[2,96,512]{2,1,0:T(8,128)(2,1)S(1)}, u32[]{:S(2)}, u32[]{:S(2)}) %collective-permute-start.3) | collective-permute-done | bytes 196640 | tf_op jit(solution)/shard_map/ppermute | solution.py:422
  25.1 2.5 %collective-permute-start.4 = (bf16[2,96,512]{2,1,0:T(8,128)(2,1)S(1)}, bf16[2,96,512]{2,1,0:T(8,128)(2,1)S(1)}, u32[]{:S(2)}, u32[]{:S(2)}) collective-permute-start(bf16[2,96,512]{2,1,0:T(8,128)(2,1)S(1)} %collective-permute-done.3), channel_id=1, source_target_pairs={{0,64},{64,0},{1,65},{65,1},{2,66},{66,2},{3,67},{67,3},{4,68},{68... | collective-permute-start | bytes 589832 | tf_op jit(solution)/shard_map/ppermute | solution.py:436
  29.5 5.8 %collective-permute-start.5 = (bf16[3,96,512]{2,1,0:T(8,128)(2,1)S(1)}, bf16[3,96,512]{2,1,0:T(8,128)(2,1)S(1)}, u32[]{:S(2)}, u32[]{:S(2)}) collective-permute-start(bf16[3,96,512]{2,1,0:T(8,128)(2,1)S(1)} %get-tuple-element.96), channel_id=1, source_target_pairs={{0,1},{1,2},{2,3},{4,5},{5,6},{6,7},{8,9},{9,10},{10,11},{12,13},{... | collective-permute-start | bytes 884744 | tf_op jit(solution)/shard_map/ppermute | solution.py:46
  35.3 1.3 collective-permute-start.6
  37.5 4.0 %collective-permute-start.16 = (bf16[3,96,512]{2,1,0:T(8,128)(2,1)}, bf16[3,96,512]{2,1,0:T(8,128)(2,1)S(1)}, u32[]{:S(2)}, u32[]{:S(2)}) collective-permute-start(bf16[3,96,512]{2,1,0:T(8,128)(2,1)} %get-tuple-element.94), channel_id=1, source_target_pairs={{0,1},{1,2},{2,3},{4,5},{5,6},{6,7},{8,9},{9,10},{10,11},{12,13},{... | collective-permute-start | bytes 884744 | tf_op jit(solution)/shard_map/ppermute | solution.py:46
  41.5 1.3 collective-permute-start.17
  42.8 2.3 %collective-permute-done.6.south_ref = bf16[3,96,512]{2,1,0:T(8,128)(2,1)S(1)} collective-permute-done((bf16[3,96,512]{2,1,0:T(8,128)(2,1)S(1)}, bf16[3,96,512]{2,1,0:T(8,128)(2,1)S(1)}, u32[]{:S(2)}, u32[]{:S(2)}) %collective-permute-start.6) | collective-permute-done | bytes 294944 | tf_op jit(solution)/shard_map/ppermute | solution.py:47
  45.1 16.2 %block_kernel.1 = (bf16[4,90,512]{2,1,0:T(8,128)(2,1)S(1)}, bf16[1088,512]{1,0:T(8,128)(2,1)S(1)}, bf16[1088,512]{1,0:T(8,128)(2,1)}, bf16[1088,512]{1,0:T(8,128...) custom-call(s32[4]{0:T(128)S(1)} %pad_add_fusion.ocean_ref, ...), custom_call_target="tpu_custom_call" | custom-call | flops 4831838208 | bytes 12582912 | tf_op jit(solution)/shard_map/block_kernel/pallas_call | solution.py:268
  63.1 2.4 %collective-permute-start.8 = (bf16[1088,512]{1,0:T(8,128)(2,1)}, bf16[1088,512]{1,0:T(8,128)(2,1)}, u32[]{:S(2)}, u32[]{:S(2)}) collective-permute-start(bf16[1088,512]{1,0:T(8,128)(2,1)} %get-tuple-element.43), channel_id=1, source_target_pairs={{0,16},{4,20},{8,24},{12,28},{16,32},{20,36},{24,40},{28,44},{32,4... | collective-permute-start | bytes 3342344 | tf_op jit(solution)/shard_map/ppermute | solution.py:477
  66.8 13.4 %couple_kernel.1 = bf16[512,512]{1,0:T(8,128)(2,1)S(1)} custom-call(bf16[3,96,512]{2,1,0:T(8,128)(2,1)S(1)} %collective-permute-done.16.north_ref, bf16[4,96,512]{2,1,0:T(8,128)(2,1)S(1)} %get-tuple-element.79.own_ref, bf16[3,96,512]{2,1,0:T(8,128)(2,1)S(1)} %collective-permute-done.17.south_ref, bf16[512,384]{1,0:T(8,128)(2,1)S(1)} %copy-done.4, ...), custom_call_target="tpu_custom_call" | custom-call | flops 10066329600 | bytes 4194304 | tf_op jit(solution)/shard_map/couple_kernel/pallas_call | solution.py:330
  80.9 1.1 collective-permute-start.18
  82.0 3.3 %collective-permute-start.20 = (bf16[16,8,512]{2,1,0:T(8,128)(2,1)S(1)}, bf16[16,8,512]{2,1,0:T(8,128)(2,1)}, u32[]{:S(2)}, u32[]{:S(2)}) collective-permute-start(bf16[16,8,512]{2,1,0:T(8,128)(2,1)S(1)} %get-tuple-element.88), channel_id=1, source_target_pairs={{0,3},{1,0},{2,1},{3,2},{4,7},{5,4},{6,5},{7,6},{8,11},{9,8},{10,9... | collective-permute-start | bytes 393224 | tf_op jit(solution)/shard_map/ppermute | solution.py:502
  85.3 5.2 %collective-permute-done.8 = bf16[1088,512]{1,0:T(8,128)(2,1)} collective-permute-done((bf16[1088,512]{1,0:T(8,128)(2,1)}, bf16[1088,512]{1,0:T(8,128)(2,1)}, u32[]{:S(2)}, u32[]{:S(2)}) %collective-permute-start.8) | collective-permute-done | bytes 1114144 | tf_op jit(solution)/shard_map/ppermute | solution.py:477
  91.9 2.4 %add_convert_fusion.5 = (bf16[256,512]{1,0:T(8,128)(2,1)S(1)}, bf16[256,512]{1,0:T(8,128)(2,1)S(1)}, bf16[256,512]{1,0:T(8,128)(2,1)S(1)}, bf16[256,512]{1,0:T(8,128)(2,1)S(1)}) fusion(bf16[1088,512]{1,0:T(8,128)(2,1)} %collective-permute-done.9, s32[]{:T(128)S(6)} %select_n.151, bf16[1088,512]{1,0:T(8,128)(2,1)} %collective-permute-done.8, ...), kind=kLoop, calls=%fused_computation.14 | loop fusion | flops 4194304 | bytes 5242896 | tf_op jit(solution)/shard_map/convert.23
  94.4 2.5 %collective-permute-start.10 = (bf16[312,512]{1,0:T(8,128)(2,1)S(1)}, bf16[312,512]{1,0:T(8,128)(2,1)S(1)}, u32[]{:S(2)}, u32[]{:S(2)}) collective-permute-start(bf16[312,512]{1,0:T(8,128)(2,1)S(1)} %get-tuple-element.101), channel_id=1, source_target_pairs={{0,8},{4,12},{8,0},{12,4},{16,24},{20,28},{24,16},{28,20},{32,40},... | collective-permute-start | bytes 958472 | tf_op jit(solution)/shard_map/ppermute | solution.py:496
  97.7 1.9 %collective-permute-start.12 = (bf16[312,512]{1,0:T(8,128)(2,1)S(1)}, bf16[312,512]{1,0:T(8,128)(2,1)}, u32[]{:S(2)}, u32[]{:S(2)}) collective-permute-start(bf16[312,512]{1,0:T(8,128)(2,1)S(1)} %get-tuple-element.103), channel_id=1, source_target_pairs={{0,12},{4,0},{8,4},{12,8},{16,28},{20,16},{24,20},{28,24},{32,44},... | collective-permute-start | bytes 958472 | tf_op jit(solution)/shard_map/ppermute | solution.py:496
  99.6 1.7 %fusion.5 = bf16[16,8,512]{2,1,0:T(8,128)(2,1)} fusion(bf16[16,8,512]{2,1,0:T(8,128)(2,1)} %collective-permute-done.20, bf16[16,8,512]{2,1,0:T(8,128)(2,1)} %collective-permute-done.19, bf16[16,8,512]{2,1,0:T(8,128)(2,1)S(1)} %collective-permute-done.18, bf16[16,4,8,512]{3,2,1,0:T(8,128)(2,1)S(1)} %bitcast.54, s32[]{:T(128)S(6)} %select_n.155), kind=kLoop, calls=%fused_computation.26 | loop fusion | flops 524288 | bytes 655364 | tf_op jit(solution)/shard_map/convert_element_type | solution.py:503
  101.3 3.5 %all-to-all-start = ((bf16[16,8,512]{2,1,0:T(8,128)(2,1)}), bf16[16,8,512]{2,1,0:T(8,128)(2,1)S(1)}, u32[]{:S(2)}, u32[]{:S(2)}) async-start(bf16[16,8,512]{2,1,0:T(8,128)(2,1)} %fusion.5), calls=%async_computation | async-start | bytes 262144 | tf_op jit(solution)/shard_map/all_to_all | solution.py:503
  105.9 1.1 add_add_fusion
  107.2 1.1 collective-permute-start.13
  108.4 3.2 %collective-permute-start.15 = (bf16[120,512]{1,0:T(8,128)(2,1)S(1)}, bf16[120,512]{1,0:T(8,128)(2,1)S(1)}, u32[]{:S(2)}, u32[]{:S(2)}) collective-permute-start(bf16[120,512]{1,0:T(8,128)(2,1)S(1)} %get-tuple-element.91), channel_id=1, source_target_pairs={{0,3},{1,0},{2,1},{3,2},{4,7},{5,4},{6,5},{7,6},{8,11},{9,8},{10,9... | collective-permute-start | bytes 368648 | tf_op jit(solution)/shard_map/ppermute | solution.py:517
  111.6 3.2 %collective-permute-done.13 = bf16[120,512]{1,0:T(8,128)(2,1)S(1)} collective-permute-done((bf16[120,512]{1,0:T(8,128)(2,1)S(1)}, bf16[120,512]{1,0:T(8,128)(2,1)S(1)}, u32[]{:S(2)}, u32[]{:S(2)}) %collective-permute-start.13) | collective-permute-done | bytes 122912 | tf_op jit(solution)/shard_map/ppermute | solution.py:517
  114.9 5.3 %collective-permute-start.22 = (bf16[128,512]{1,0:T(8,128)(2,1)S(1)}, bf16[128,512]{1,0:T(8,128)(2,1)S(1)}, u32[]{:S(2)}, u32[]{:S(2)}) collective-permute-start(bf16[128,512]{1,0:T(8,128)(2,1)S(1)} %pad_maximum_fusion.6.mine_ref), channel_id=1, source_target_pairs={{0,128},{128,0},{1,129},{129,1},{2,130},{130,2},{3,131},{131,3},{4... | collective-permute-start | bytes 393224 | tf_op jit(solution)/shard_map/ppermute | solution.py:520
  120.2 7.3 %collective-permute-start.21 = (bf16[128,512]{1,0:T(8,128)(2,1)S(1)}, bf16[128,512]{1,0:T(8,128)(2,1)S(1)}, u32[]{:S(2)}, u32[]{:S(2)}) collective-permute-start(bf16[128,512]{1,0:T(8,128)(2,1)S(1)} %pad_maximum_fusion.6.mine_ref), channel_id=1, source_target_pairs={{0,64},{64,0},{1,65},{65,1},{2,66},{66,2},{3,67},{67,3},{4,68},{68... | collective-permute-start | bytes 393224 | tf_op jit(solution)/shard_map/ppermute | solution.py:519
  127.6 4.2 %collective-permute-start.23 = (bf16[128,512]{1,0:T(8,128)(2,1)S(1)}, bf16[128,512]{1,0:T(8,128)(2,1)S(1)}, u32[]{:S(2)}, u32[]{:S(2)}) collective-permute-start(bf16[128,512]{1,0:T(8,128)(2,1)S(1)} %collective-permute-done.22.across_ref), channel_id=1, source_target_pairs={{0,64},{64,0},{1,65},{65,1},{2,66},{66,2},{3,67},{67,3},{4,68},{68... | collective-permute-start | bytes 393224 | tf_op jit(solution)/shard_map/ppermute | solution.py:521
  132.9 1.5 %finish_kernel.1 = (f32[49,512]{1,0:T(8,128)}, f32[1,512]{1,0:T(1,128)}, f32[8,2048]{1,0:T(8,128)}, f32[32,512]{1,0:T(8,128)}, f32[49,512]{1,0:T(8,128)}, /*inde...) custom-call(s32[2]{0:T(128)S(1)} %pad_add_fusion.1.place_ref, ...), custom_call_target="tpu_custom_call" | custom-call | tf_op jit(solution)/shard_map/finish_kernel/pallas_call | solution.py:375
  (99 shorter events, 14.0 us)
Async XLA Ops:
  0.6 8.7 %copy-start.7 = (bf16[1,4,90,512]{3,1,2,0:T(4,128)(2,1)S(1)}, bf16[1,4,90,512]{3,1,2,0:T(4,128)(2,1)}, u32[]{:S(2)}) copy-start(bf16[1,4,90,512]{3,1,2,0:T(4,128)(2,1)} %param.14) | copy-start | bytes 1105924
  0.7 8.9 %copy-start.9 = (f32[49,512]{1,0:T(8,128)S(1)}, f32[49,512]{1,0:T(8,128)}, u32[]{:S(2)}) copy-start(f32[49,512]{1,0:T(8,128)} %param.16) | copy-start | bytes 301060
  0.7 8.9 %copy-start.8 = (f32[49,512]{1,0:T(8,128)S(1)}, f32[49,512]{1,0:T(8,128)}, u32[]{:S(2)}) copy-start(f32[49,512]{1,0:T(8,128)} %param.20) | copy-start | bytes 301060
  2.7 7.4 %collective-permute-start = (bf16[4,3,640]{2,1,0:T(4,128)(2,1)S(1)}, bf16[4,3,640]{2,1,0:T(4,128)(2,1)S(1)}, u32[]{:S(2)}, u32[]{:S(2)}) collective-permute-start(bf16[4,3,640]{2,1,0:T(4,128)(2,1)S(1)} %pad_maximum_fusion.7), channel_id=1, source_target_pairs={{0,4},{4,8},{8,12},{12,16},{16,20},{20,24},{24,28},{28,32},{32,36}... | collective-permute-start | bytes 46088 | tf_op jit(solution)/shard_map/ppermute | solution.py:411
  5.0 5.1 %collective-permute-start.1 = (bf16[4,3,640]{2,1,0:T(4,128)(2,1)S(1)}, bf16[4,3,640]{2,1,0:T(4,128)(2,1)S(1)}, u32[]{:S(2)}, u32[]{:S(2)}) collective-permute-start(bf16[4,3,640]{2,1,0:T(4,128)(2,1)S(1)} %pad_maximum_fusion.8), channel_id=1, source_target_pairs={{0,60},{4,0},{8,4},{12,8},{16,12},{20,16},{24,20},{28,24},{32,28},... | collective-permute-start | bytes 46088 | tf_op jit(solution)/shard_map/ppermute | solution.py:412
  10.0 3.4 %copy-start.10 = (f32[512]{0:T(512)S(1)}, f32[512]{0:T(512)}, u32[]{:S(2)}) copy-start(f32[512]{0:T(512)} %param.21) | copy-start | bytes 6148
  10.3 4.4 %collective-permute-start.2 = (bf16[4,96,512]{2,1,0:T(8,128)(2,1)S(1)}, bf16[4,96,512]{2,1,0:T(8,128)(2,1)S(1)}, u32[]{:S(2)}, u32[]{:S(2)}) collective-permute-start(bf16[4,96,512]{2,1,0:T(8,128)(2,1)S(1)} %get-tuple-element.82), channel_id=1, source_target_pairs={{0,64},{64,0},{1,65},{65,1},{2,66},{66,2},{3,67},{67,3},{4,68},{68... | collective-permute-start | bytes 1179656 | tf_op jit(solution)/shard_map/ppermute | solution.py:418
  14.9 10.1 %collective-permute-start.3 = (bf16[2,96,512]{2,1,0:T(8,128)(2,1)S(1)}, bf16[2,96,512]{2,1,0:T(8,128)(2,1)S(1)}, u32[]{:S(2)}, u32[]{:S(2)}) collective-permute-start(bf16[2,96,512]{2,1,0:T(8,128)(2,1)S(1)} %fusion.8), channel_id=1, source_target_pairs={{0,128},{128,0},{1,129},{129,1},{2,130},{130,2},{3,131},{131,3},{4... | collective-permute-start | bytes 589832 | tf_op jit(solution)/shard_map/ppermute | solution.py:422
  25.1 3.5 %collective-permute-start.4 = (bf16[2,96,512]{2,1,0:T(8,128)(2,1)S(1)}, bf16[2,96,512]{2,1,0:T(8,128)(2,1)S(1)}, u32[]{:S(2)}, u32[]{:S(2)}) collective-permute-start(bf16[2,96,512]{2,1,0:T(8,128)(2,1)S(1)} %collective-permute-done.3), channel_id=1, source_target_pairs={{0,64},{64,0},{1,65},{65,1},{2,66},{66,2},{3,67},{67,3},{4,68},{68... | collective-permute-start | bytes 589832 | tf_op jit(solution)/shard_map/ppermute | solution.py:436
  28.6 16.5 %copy-start.2 = (bf16[512,2048]{1,0:T(8,128)(2,1)S(1)}, bf16[512,2048]{1,0:T(8,128)(2,1)}, u32[]{:S(2)}) copy-start(bf16[512,2048]{1,0:T(8,128)(2,1)} %w_in_sea.1) | copy-start | bytes 6291460
  28.9 16.3 %copy-start.1 = (bf16[2048,512]{1,0:T(8,128)(2,1)S(1)}, bf16[2048,512]{1,0:T(8,128)(2,1)}, u32[]{:S(2)}) copy-start(bf16[2048,512]{1,0:T(8,128)(2,1)} %w_out_air.1) | copy-start | bytes 6291460
  29.4 15.7 %copy-start = (bf16[512,2048]{1,0:T(8,128)(2,1)S(1)}, bf16[512,2048]{1,0:T(8,128)(2,1)}, u32[]{:S(2)}) copy-start(bf16[512,2048]{1,0:T(8,128)(2,1)} %w_in_air.1) | copy-start | bytes 6291460
  29.5 13.3 %collective-permute-start.5 = (bf16[3,96,512]{2,1,0:T(8,128)(2,1)S(1)}, bf16[3,96,512]{2,1,0:T(8,128)(2,1)S(1)}, u32[]{:S(2)}, u32[]{:S(2)}) collective-permute-start(bf16[3,96,512]{2,1,0:T(8,128)(2,1)S(1)} %get-tuple-element.96), channel_id=1, source_target_pairs={{0,1},{1,2},{2,3},{4,5},{5,6},{6,7},{8,9},{9,10},{10,11},{12,13},{... | collective-permute-start | bytes 884744 | tf_op jit(solution)/shard_map/ppermute | solution.py:46
  35.3 9.8 %collective-permute-start.6 = (bf16[3,96,512]{2,1,0:T(8,128)(2,1)S(1)}, bf16[3,96,512]{2,1,0:T(8,128)(2,1)S(1)}, u32[]{:S(2)}, u32[]{:S(2)}) collective-permute-start(bf16[3,96,512]{2,1,0:T(8,128)(2,1)S(1)} %get-tuple-element.95), channel_id=1, source_target_pairs={{1,0},{2,1},{3,2},{5,4},{6,5},{7,6},{9,8},{10,9},{11,10},{13,12},{... | collective-permute-start | bytes 884744 | tf_op jit(solution)/shard_map/ppermute | solution.py:47
  37.5 28.3 %collective-permute-start.16 = (bf16[3,96,512]{2,1,0:T(8,128)(2,1)}, bf16[3,96,512]{2,1,0:T(8,128)(2,1)S(1)}, u32[]{:S(2)}, u32[]{:S(2)}) collective-permute-start(bf16[3,96,512]{2,1,0:T(8,128)(2,1)} %get-tuple-element.94), channel_id=1, source_target_pairs={{0,1},{1,2},{2,3},{4,5},{5,6},{6,7},{8,9},{9,10},{10,11},{12,13},{... | collective-permute-start | bytes 884744 | tf_op jit(solution)/shard_map/ppermute | solution.py:46
  41.5 24.3 %collective-permute-start.17 = (bf16[3,96,512]{2,1,0:T(8,128)(2,1)S(1)}, bf16[3,96,512]{2,1,0:T(8,128)(2,1)S(1)}, u32[]{:S(2)}, u32[]{:S(2)}) collective-permute-start(bf16[3,96,512]{2,1,0:T(8,128)(2,1)S(1)} %get-tuple-element.93), channel_id=1, source_target_pairs={{1,0},{2,1},{3,2},{5,4},{6,5},{7,6},{9,8},{10,9},{11,10},{13,12},{... | collective-permute-start | bytes 884744 | tf_op jit(solution)/shard_map/ppermute | solution.py:47
  62.1 19.9 %collective-permute-start.7 = (bf16[1088,512]{1,0:T(8,128)(2,1)}, bf16[1088,512]{1,0:T(8,128)(2,1)}, u32[]{:S(2)}, u32[]{:S(2)}) collective-permute-start(bf16[1088,512]{1,0:T(8,128)(2,1)} %get-tuple-element.42), channel_id=1, source_target_pairs={{0,32},{4,36},{8,40},{12,44},{16,48},{20,52},{24,56},{28,60},{32,0... | collective-permute-start | bytes 3342344 | tf_op jit(solution)/shard_map/ppermute | solution.py:477
  63.1 27.4 %collective-permute-start.8 = (bf16[1088,512]{1,0:T(8,128)(2,1)}, bf16[1088,512]{1,0:T(8,128)(2,1)}, u32[]{:S(2)}, u32[]{:S(2)}) collective-permute-start(bf16[1088,512]{1,0:T(8,128)(2,1)} %get-tuple-element.43), channel_id=1, source_target_pairs={{0,16},{4,20},{8,24},{12,28},{16,32},{20,36},{24,40},{28,44},{32,4... | collective-permute-start | bytes 3342344 | tf_op jit(solution)/shard_map/ppermute | solution.py:477
  65.5 25.5 %collective-permute-start.9 = (bf16[1088,512]{1,0:T(8,128)(2,1)}, bf16[1088,512]{1,0:T(8,128)(2,1)}, u32[]{:S(2)}, u32[]{:S(2)}) collective-permute-start(bf16[1088,512]{1,0:T(8,128)(2,1)} %get-tuple-element.44), channel_id=1, source_target_pairs={{0,48},{4,52},{8,56},{12,60},{16,0},{20,4},{24,8},{28,12},{32,16},... | collective-permute-start | bytes 3342344 | tf_op jit(solution)/shard_map/ppermute | solution.py:477
  80.9 16.8 %collective-permute-start.18 = (bf16[16,8,512]{2,1,0:T(8,128)(2,1)S(1)}, bf16[16,8,512]{2,1,0:T(8,128)(2,1)S(1)}, u32[]{:S(2)}, u32[]{:S(2)}) collective-permute-start(bf16[16,8,512]{2,1,0:T(8,128)(2,1)S(1)} %get-tuple-element.87), channel_id=1, source_target_pairs={{0,2},{1,3},{2,0},{3,1},{4,6},{5,7},{6,4},{7,5},{8,10},{9,11},{10,... | collective-permute-start | bytes 393224 | tf_op jit(solution)/shard_map/ppermute | solution.py:502
  82.0 17.6 %collective-permute-start.19 = (bf16[16,8,512]{2,1,0:T(8,128)(2,1)}, bf16[16,8,512]{2,1,0:T(8,128)(2,1)}, u32[]{:S(2)}, u32[]{:S(2)}) collective-permute-start(bf16[16,8,512]{2,1,0:T(8,128)(2,1)} %get-tuple-element.89), channel_id=1, source_target_pairs={{0,1},{1,2},{2,3},{3,0},{4,5},{5,6},{6,7},{7,4},{8,9},{9,10},{10,1... | collective-permute-start | bytes 393224 | tf_op jit(solution)/shard_map/ppermute | solution.py:502
  82.0 17.6 %collective-permute-start.20 = (bf16[16,8,512]{2,1,0:T(8,128)(2,1)S(1)}, bf16[16,8,512]{2,1,0:T(8,128)(2,1)}, u32[]{:S(2)}, u32[]{:S(2)}) collective-permute-start(bf16[16,8,512]{2,1,0:T(8,128)(2,1)S(1)} %get-tuple-element.88), channel_id=1, source_target_pairs={{0,3},{1,0},{2,1},{3,2},{4,7},{5,4},{6,5},{7,6},{8,11},{9,8},{10,9... | collective-permute-start | bytes 393224 | tf_op jit(solution)/shard_map/ppermute | solution.py:502
  94.4 10.5 %collective-permute-start.10 = (bf16[312,512]{1,0:T(8,128)(2,1)S(1)}, bf16[312,512]{1,0:T(8,128)(2,1)S(1)}, u32[]{:S(2)}, u32[]{:S(2)}) collective-permute-start(bf16[312,512]{1,0:T(8,128)(2,1)S(1)} %get-tuple-element.101), channel_id=1, source_target_pairs={{0,8},{4,12},{8,0},{12,4},{16,24},{20,28},{24,16},{28,20},{32,40},... | collective-permute-start | bytes 958472 | tf_op jit(solution)/shard_map/ppermute | solution.py:496
  96.9 8.6 %collective-permute-start.11 = (bf16[312,512]{1,0:T(8,128)(2,1)S(1)}, bf16[312,512]{1,0:T(8,128)(2,1)S(1)}, u32[]{:S(2)}, u32[]{:S(2)}) collective-permute-start(bf16[312,512]{1,0:T(8,128)(2,1)S(1)} %get-tuple-element.102), channel_id=1, source_target_pairs={{0,4},{4,8},{8,12},{12,0},{16,20},{20,24},{24,28},{28,16},{32,36},... | collective-permute-start | bytes 958472 | tf_op jit(solution)/shard_map/ppermute | solution.py:496
  97.7 8.2 %collective-permute-start.12 = (bf16[312,512]{1,0:T(8,128)(2,1)S(1)}, bf16[312,512]{1,0:T(8,128)(2,1)}, u32[]{:S(2)}, u32[]{:S(2)}) collective-permute-start(bf16[312,512]{1,0:T(8,128)(2,1)S(1)} %get-tuple-element.103), channel_id=1, source_target_pairs={{0,12},{4,0},{8,4},{12,8},{16,28},{20,16},{24,20},{28,24},{32,44},... | collective-permute-start | bytes 958472 | tf_op jit(solution)/shard_map/ppermute | solution.py:496
  101.3 10.3 %all-to-all-start = ((bf16[16,8,512]{2,1,0:T(8,128)(2,1)}), bf16[16,8,512]{2,1,0:T(8,128)(2,1)S(1)}, u32[]{:S(2)}, u32[]{:S(2)}) async-start(bf16[16,8,512]{2,1,0:T(8,128)(2,1)} %fusion.5), calls=%async_computation | async-start | bytes 262144 | tf_op jit(solution)/shard_map/all_to_all | solution.py:503
  107.2 7.6 %collective-permute-start.13 = (bf16[120,512]{1,0:T(8,128)(2,1)S(1)}, bf16[120,512]{1,0:T(8,128)(2,1)S(1)}, u32[]{:S(2)}, u32[]{:S(2)}) collective-permute-start(bf16[120,512]{1,0:T(8,128)(2,1)S(1)} %get-tuple-element.90), channel_id=1, source_target_pairs={{0,2},{1,3},{2,0},{3,1},{4,6},{5,7},{6,4},{7,5},{8,10},{9,11},{10,... | collective-permute-start | bytes 368648 | tf_op jit(solution)/shard_map/ppermute | solution.py:517
  108.3 6.5 %collective-permute-start.14 = (bf16[120,512]{1,0:T(8,128)(2,1)S(1)}, bf16[120,512]{1,0:T(8,128)(2,1)S(1)}, u32[]{:S(2)}, u32[]{:S(2)}) collective-permute-start(bf16[120,512]{1,0:T(8,128)(2,1)S(1)} %get-tuple-element.92), channel_id=1, source_target_pairs={{0,1},{1,2},{2,3},{3,0},{4,5},{5,6},{6,7},{7,4},{8,9},{9,10},{10,1... | collective-permute-start | bytes 368648 | tf_op jit(solution)/shard_map/ppermute | solution.py:517
  108.4 6.5 %collective-permute-start.15 = (bf16[120,512]{1,0:T(8,128)(2,1)S(1)}, bf16[120,512]{1,0:T(8,128)(2,1)S(1)}, u32[]{:S(2)}, u32[]{:S(2)}) collective-permute-start(bf16[120,512]{1,0:T(8,128)(2,1)S(1)} %get-tuple-element.91), channel_id=1, source_target_pairs={{0,3},{1,0},{2,1},{3,2},{4,7},{5,4},{6,5},{7,6},{8,11},{9,8},{10,9... | collective-permute-start | bytes 368648 | tf_op jit(solution)/shard_map/ppermute | solution.py:517
  114.9 12.6 %collective-permute-start.22 = (bf16[128,512]{1,0:T(8,128)(2,1)S(1)}, bf16[128,512]{1,0:T(8,128)(2,1)S(1)}, u32[]{:S(2)}, u32[]{:S(2)}) collective-permute-start(bf16[128,512]{1,0:T(8,128)(2,1)S(1)} %pad_maximum_fusion.6.mine_ref), channel_id=1, source_target_pairs={{0,128},{128,0},{1,129},{129,1},{2,130},{130,2},{3,131},{131,3},{4... | collective-permute-start | bytes 393224 | tf_op jit(solution)/shard_map/ppermute | solution.py:520
  120.2 12.6 %collective-permute-start.21 = (bf16[128,512]{1,0:T(8,128)(2,1)S(1)}, bf16[128,512]{1,0:T(8,128)(2,1)S(1)}, u32[]{:S(2)}, u32[]{:S(2)}) collective-permute-start(bf16[128,512]{1,0:T(8,128)(2,1)S(1)} %pad_maximum_fusion.6.mine_ref), channel_id=1, source_target_pairs={{0,64},{64,0},{1,65},{65,1},{2,66},{66,2},{3,67},{67,3},{4,68},{68... | collective-permute-start | bytes 393224 | tf_op jit(solution)/shard_map/ppermute | solution.py:519
  127.6 5.3 %collective-permute-start.23 = (bf16[128,512]{1,0:T(8,128)(2,1)S(1)}, bf16[128,512]{1,0:T(8,128)(2,1)S(1)}, u32[]{:S(2)}, u32[]{:S(2)}) collective-permute-start(bf16[128,512]{1,0:T(8,128)(2,1)S(1)} %collective-permute-done.22.across_ref), channel_id=1, source_target_pairs={{0,64},{64,0},{1,65},{65,1},{2,66},{66,2},{3,67},{67,3},{4,68},{68... | collective-permute-start | bytes 393224 | tf_op jit(solution)/shard_map/ppermute | solution.py:521
  (5 other events, 11.9 us)

commit v4 on v3

--- a/solution.py
+++ b/solution.py
@@ -42,10 +42,27 @@
     return lax.dynamic_index_in_dim(parts, index, 0, keepdims=False)
 
 
-def lat_halo(tile):
-    north = lax.ppermute(tile[1:4], "lat", [(i, i + 1) for i in range(3)])
-    south = lax.ppermute(tile[0:3], "lat", [(i + 1, i) for i in range(3)])
-    return north, south
+def lat_halo(tile, lat):
+    even = 1 - lax.rem(lat, 2)
+    outer = lax.dynamic_slice_in_dim(tile, even, 3, 0)
+    inner = lax.dynamic_slice_in_dim(tile, 1 - even, 3, 0)
+    outer = lax.ppermute(outer, "lat", [(0, 1), (1, 0), (2, 3), (3, 2)])
+    inner = lax.ppermute(inner, "lat", [(0, 0), (1, 2), (2, 1), (3, 3)])
+    return outer, inner
+
+
+def halo_rows(lat, outer_ref, inner_ref, fill):
+    inside = jnp.where((lat == 1) | (lat == 2), 1.0, 0.0).astype(f32)
+
+    @pl.when(lax.rem(lat, 2) == 1)
+    def _():
+        fill(0, outer_ref, None)
+        fill(7, inner_ref, inside)
+
+    @pl.when(lax.rem(lat, 2) == 0)
+    def _():
+        fill(0, inner_ref, inside)
+        fill(7, outer_ref, None)
 
 
 def picker(rows, cols, group, stride):
@@ -61,9 +78,9 @@
 
 def block_kernel(
     ocean_ref,
-    north_ref,
+    outer_ref,
     own_ref,
-    south_ref,
+    inner_ref,
     cot_ref,
     mask_ref,
     kern_ref,
@@ -124,11 +141,16 @@
             copy.start()
 
     spread = picker(144, 96, 8, 12)
-    for r in range(10):
-        src = north_ref[r] if r < 3 else own_ref[r - 3] if r < 7 else south_ref[r - 7]
-        q = mm(spread, src)
-        for lb in range(4):
-            taps_in[lb, r] = q[:, lb * 128 : lb * 128 + 128].reshape(18, 8, 128)
+
+    def fill(first, source, factor, count=3):
+        for r in range(count):
+            q = mm(spread, source[r])
+            q = q if factor is None else q * factor
+            for lb in range(4):
+                taps_in[lb, first + r] = q[:, lb * 128 : lb * 128 + 128].reshape(18, 8, 128)
+
+    fill(3, own_ref, None, 4)
+    halo_rows(ocean_ref[4], outer_ref, inner_ref, fill)
     order = picker(96, 96, 8, 12)
     for i in range(4):
         gb[i * 96 : i * 96 + 96, :] = mm(order, cot_ref[i]).astype(bf16)
@@ -261,7 +283,7 @@
         send(j, 1024, 64, 12 + j).wait()
 
 
-def block(ocean, north, own, south, cot, mask, kern, gain, wia, woa, wis, wos):
+def block(ocean, outer, own, inner, cot, mask, kern, gain, wia, woa, wis, wos):
     vmem = pl.BlockSpec(memory_space=pltpu.VMEM)
     hbm = pl.BlockSpec(memory_space=pltpu.HBM)
     flops = 2 * 6 * 384 * 512 * 2048
@@ -290,21 +312,38 @@
             *[pltpu.VMEM((1088, 512), bf16)] * 4,
             pltpu.SemaphoreType.DMA((16,)),
         ],
-        compiler_params=pltpu.CompilerParams(vmem_limit_bytes=40 * 1024 * 1024),
+        compiler_params=pltpu.CompilerParams(vmem_limit_bytes=51 * 1024 * 1024),
         cost_estimate=pl.CostEstimate(
             flops=flops, bytes_accessed=12 * 1024 * 1024, transcendentals=384 * 2048
         ),
         name="block_kernel",
-    )(ocean, north, own, south, cot, mask, kern, gain, wia, woa, wis, wos)
+    )(ocean, outer, own, inner, cot, mask, kern, gain, wia, woa, wis, wos)
 
 
 def couple_kernel(
-    north_ref, own_ref, south_ref, gct_ref, cot_ref, kern_ref, scale_ref, out_ref, rows16, acc, gct, taps
+    lat_ref,
+    outer_ref,
+    own_ref,
+    inner_ref,
+    gct_ref,
+    cot_ref,
+    kern_ref,
+    scale_ref,
+    out_ref,
+    rows16,
+    acc,
+    gct,
+    taps,
 ):
     spread = picker(192, 96, 16, 6)
-    for r in range(10):
-        src = north_ref[r] if r < 3 else own_ref[r - 3] if r < 7 else south_ref[r - 7]
-        rows16[r] = mm(spread, src).astype(bf16)
+
+    def fill(first, source, factor, count=3):
+        for r in range(count):
+            q = mm(spread, source[r])
+            rows16[first + r] = (q if factor is None else q * factor).astype(bf16)
+
+    fill(3, own_ref, None, 4)
+    halo_rows(lat_ref[0], outer_ref, inner_ref, fill)
     order = picker(96, 96, 16, 6)
     moved = [mm(order, cot_ref[i]).astype(bf16) for i in range(4)]
     acc[...] = mm(jnp.concatenate(moved, axis=0).T, rows16[3:7, 48:144, :].reshape(384, 512))
@@ -325,12 +364,14 @@
     out_ref[...] = (acc[...] * scale_ref[0]).astype(bf16).T
 
 
-def couple(north, own, south, gct, cot, kern, scale):
+def couple(lat, outer, own, inner, gct, cot, kern, scale):
     vmem = pl.BlockSpec(memory_space=pltpu.VMEM)
     return pl.pallas_call(
         couple_kernel,
         out_shape=jax.ShapeDtypeStruct((512, 512), bf16),
-        in_specs=[vmem] * 6 + [pl.BlockSpec(memory_space=pltpu.SMEM)],
+        in_specs=[pl.BlockSpec(memory_space=pltpu.SMEM)]
+        + [vmem] * 6
+        + [pl.BlockSpec(memory_space=pltpu.SMEM)],
         out_specs=vmem,
         scratch_shapes=[
             pltpu.VMEM((10, 192, 512), bf16),
@@ -343,7 +384,7 @@
             flops=2 * 50 * 384 * 512 * 512, bytes_accessed=4 * 1024 * 1024, transcendentals=0
         ),
         name="couple_kernel",
-    )(north, own, south, gct, cot, kern, scale)
+    )(lat, outer, own, inner, gct, cot, kern, scale)
 
 
 def finish_kernel(place_ref, mine_ref, mine_beside_ref, across_ref, across_beside_ref, *refs):
@@ -402,11 +443,11 @@
     is_ocean = (zh == 1) & (core == 1)
     copies = 3.0
     sea = (1 - land).astype(f32)
-    local = component_snapshots[0]
+    local = lax.optimization_barrier(component_snapshots)[0]
 
     def edge(columns):
-        flags = jnp.broadcast_to(sea[:, columns].astype(bf16)[:, :, None], (4, 3, 128))
-        return jnp.concatenate([local[:, columns], flags], axis=2)
+        flags = jnp.broadcast_to(sea[:, columns].astype(bf16)[None, :, :, None], (1, 4, 3, 128))
+        return jnp.concatenate([component_snapshots[:, :, columns], flags], axis=3)[0]
 
     west = lax.ppermute(edge(slice(87, 90)), LON, ring(16, 1))
     east = lax.ppermute(edge(slice(0, 3)), LON, ring(16, -1))
@@ -446,11 +487,12 @@
     forcing = jnp.where(is_ocean, projected / copies, projected.astype(bf16).astype(f32))
     field = local.astype(f32) + sea_wide[:, :, None] * forcing.reshape(4, 96, 512)
     field = field.astype(bf16)
-    north, south = lat_halo(field)
+    lat = lax.axis_index("lat")
+    outer, inner = lat_halo(field, lat)
     masked = (sea_wide[:, :, None] * partner.astype(f32)).astype(bf16)
-    masked_north, masked_south = lat_halo(masked)
-
-    x, y, lat = (lax.axis_index(axis) for axis in ("x", "y", "lat"))
+    masked_outer, masked_inner = lat_halo(masked, lat)
+
+    x, y = lax.axis_index("x"), lax.axis_index("y")
     result, *parts, grad_conv_t = block(
         jnp.stack(
             [
@@ -458,11 +500,12 @@
                 jnp.where(core == 0, x, y),
                 jnp.where(core == 0, 4, 1),
                 jnp.where(core == 0, 1, 4),
+                lat,
             ]
         ),
-        north,
+        outer,
         field,
-        south,
+        inner,
         grad_branch,
         mask,
         kernel_lanes,
@@ -477,9 +520,10 @@
         parts[k] = lax.ppermute(parts[k], ("core", "x", "y"), cross(k, 0))
 
     grad_couple = couple(
-        masked_north,
+        lat.reshape(1),
+        masked_outer,
         masked,
-        masked_south,
+        masked_inner,
         grad_conv_t,
         grad_branch,
         kernel_rows,

time: 135 us -> 130 us (0.963)
  starting transfers between devices: 67.2 us -> 63.4 us
  waiting for transfers between devices: 19.2 us -> 16.9 us
    ppermute x4, starting transfers between devices: 12.4 us -> 7.2 us  [the longest x2 5.87 us: lat_halo(): outer = lax.ppermute(outer, 'lat', [(0, 1), (1, 0), (2, 3), (3, 2)])]
    ppermute x3, starting transfers between devices: 4.4 us -> 6.87 us  [on_device(): rows[k] = lax.ppermute(rows[k], 'lat', ring(4, k))]
    ppermute x3, waiting for transfers between devices: 5.69 us -> 3.25 us  [on_device(): parts[k] = lax.ppermute(parts[k], ('core', 'x', 'y'), cross(k, 0))]
    ppermute x3, starting transfers between devices: 4.4 us -> 6.79 us  [on_device(): shares[k] = lax.ppermute(shares[k], 'lat', ring(4, k))]
    dynamic_slice x0 -> x2, local copies, waits for them, and re-layouts: none -> 1.57 us  [lat_halo(): inner = lax.dynamic_slice_in_dim(tile, 1 - even, 3, 0)]
    ppermute x1, starting transfers between devices: 7.35 us -> 5.8 us  [on_device(): mine_beside = lax.ppermute(mine, 'core', ring(2, 1))]
    unnamed x26 -> x19, local copies, waits for them, and re-layouts: 3.91 us -> 2.86 us
    another operation x4 -> x3, other arithmetic: 3.46 us -> 3.39 us
  transfers between devices with their start and end apart: 25 -> 25, of which waited for: 9 -> 7; matrix products, arithmetic and copies ran while one was open for 8% -> 9% of each run, Pallas kernels for 22% -> 23%
where the time goes in v4:
time: 130 us
  starting transfers between devices  63.4 us (49%)
  Pallas kernels  30.9 us (24%)
  waiting for transfers between devices  16.9 us (13%)
  other arithmetic  9.98 us (8%)
  local copies, waits for them, and re-layouts  6.82 us (5%)
    pallas_call x1, Pallas kernels, block(): pl.pallas_call(block_kernel, out_shape=(jax.ShapeDtypeStruct((4, 90, 512)...  15.8 us
    pallas_call x1, Pallas kernels, couple(): pl.pallas_call(couple_kernel, out_shape=jax.ShapeDtypeStruct((512, 512),...  13.7 us
    ppermute x3, starting transfers between devices, on_device(): rows[k] = lax.ppermute(rows[k], 'lat', ring(4, k))  6.87 us
    ppermute x3, starting transfers between devices, on_device(): shares[k] = lax.ppermute(shares[k], 'lat', ring(4, k))  6.79 us
    ppermute x2, starting transfers between devices, lat_halo(): outer = lax.ppermute(outer, 'lat', [(0, 1), (1, 0), (2, 3), (3, 2)])  5.87 us
    ppermute x1, starting transfers between devices, on_device(): mine_beside = lax.ppermute(mine, 'core', ring(2, 1))  5.8 us
    ppermute x1, starting transfers between devices, on_device(): got = lax.ppermute(half, 'zh', ring(2, 1))  5.26 us
    ppermute x1, starting transfers between devices, on_device(): across = lax.ppermute(mine, 'zh', ring(2, 1))  5.09 us
  transfers between devices with their start and end apart: 25, of which 7 were waited for; matrix products, arithmetic and copies ran while one was open for 9% of the time, Pallas kernels for 23%

profile of v4, /device:TPU:1, one launch (start us, length us, event | category | flops | bytes accessed | tf_op | source)
XLA Modules:
  0.0 129.6 jit_solution(9557300886899071364)
XLA Ops:
  2.3 2.2 %collective-permute-start = (bf16[4,3,640]{2,1,0:T(4,128)(2,1)S(1)}, bf16[4,3,640]{2,1,0:T(4,128)(2,1)S(1)}, u32[]{:S(2)}, u32[]{:S(2)}) collective-permute-start(bf16[4,3,640]{2,1,0:T(4,128)(2,1)S(1)} %maximum_bitcast_fusion), channel_id=1, source_target_pairs={{0,4},{4,8},{8,12},{12,16},{16,20},{20,24},{24,28},{28,32},{32,36}... | collective-permute-start | bytes 46088 | tf_op jit(solution)/shard_map/ppermute | solution.py:452
  4.6 3.7 %collective-permute-start.1 = (bf16[4,3,640]{2,1,0:T(4,128)(2,1)S(1)}, bf16[4,3,640]{2,1,0:T(4,128)(2,1)S(1)}, u32[]{:S(2)}, u32[]{:S(2)}) collective-permute-start(bf16[4,3,640]{2,1,0:T(4,128)(2,1)S(1)} %maximum_bitcast_fusion.1), channel_id=1, source_target_pairs={{0,60},{4,0},{8,4},{12,8},{16,12},{20,16},{24,20},{28,24},{32,28},... | collective-permute-start | bytes 46088 | tf_op jit(solution)/shard_map/ppermute | solution.py:453
  9.0 1.1 fusion
  11.9 2.9 %collective-permute-start.2 = (bf16[4,96,512]{2,1,0:T(8,128)(2,1)S(1)}, bf16[4,96,512]{2,1,0:T(8,128)(2,1)S(1)}, u32[]{:S(2)}, u32[]{:S(2)}) collective-permute-start(bf16[4,96,512]{2,1,0:T(8,128)(2,1)S(1)} %get-tuple-element.82), channel_id=1, source_target_pairs={{0,64},{64,0},{1,65},{65,1},{2,66},{66,2},{3,67},{67,3},{4,68},{68... | collective-permute-start | bytes 1179656 | tf_op jit(solution)/shard_map/ppermute | solution.py:459
  14.9 1.3 collective-permute-done.2
  16.3 5.3 %collective-permute-start.3 = (bf16[2,96,512]{2,1,0:T(8,128)(2,1)S(1)}, bf16[2,96,512]{2,1,0:T(8,128)(2,1)S(1)}, u32[]{:S(2)}, u32[]{:S(2)}) collective-permute-start(bf16[2,96,512]{2,1,0:T(8,128)(2,1)S(1)} %fusion.8), channel_id=1, source_target_pairs={{0,128},{128,0},{1,129},{129,1},{2,130},{130,2},{3,131},{131,3},{4... | collective-permute-start | bytes 589832 | tf_op jit(solution)/shard_map/ppermute | solution.py:463
  21.7 4.7 %collective-permute-done.3 = bf16[2,96,512]{2,1,0:T(8,128)(2,1)S(1)} collective-permute-done((bf16[2,96,512]{2,1,0:T(8,128)(2,1)S(1)}, bf16[2,96,512]{2,1,0:T(8,128)(2,1)S(1)}, u32[]{:S(2)}, u32[]{:S(2)}) %collective-permute-start.3) | collective-permute-done | bytes 196640 | tf_op jit(solution)/shard_map/ppermute | solution.py:463
  26.5 2.5 %collective-permute-start.4 = (bf16[2,96,512]{2,1,0:T(8,128)(2,1)S(1)}, bf16[2,96,512]{2,1,0:T(8,128)(2,1)S(1)}, u32[]{:S(2)}, u32[]{:S(2)}) collective-permute-start(bf16[2,96,512]{2,1,0:T(8,128)(2,1)S(1)} %collective-permute-done.3), channel_id=1, source_target_pairs={{0,64},{64,0},{1,65},{65,1},{2,66},{66,2},{3,67},{67,3},{4,68},{68... | collective-permute-start | bytes 589832 | tf_op jit(solution)/shard_map/ppermute | solution.py:477
  31.6 3.6 %collective-permute-start.5 = (bf16[3,96,512]{2,1,0:T(8,128)(2,1)}, bf16[3,96,512]{2,1,0:T(8,128)(2,1)S(1)}, u32[]{:S(2)}, u32[]{:S(2)}) collective-permute-start(bf16[3,96,512]{2,1,0:T(8,128)(2,1)} %get-tuple-element.96), channel_id=1, source_target_pairs={{0,1},{1,0},{2,3},{3,2},{4,5},{5,4},{6,7},{7,6},{8,9},{9,8},{10,11... | collective-permute-start | bytes 884744 | tf_op jit(solution)/shard_map/ppermute | solution.py:49
  36.8 2.2 %collective-permute-start.16 = (bf16[3,96,512]{2,1,0:T(8,128)(2,1)}, bf16[3,96,512]{2,1,0:T(8,128)(2,1)S(1)}, u32[]{:S(2)}, u32[]{:S(2)}) collective-permute-start(bf16[3,96,512]{2,1,0:T(8,128)(2,1)} %get-tuple-element.94), channel_id=1, source_target_pairs={{0,1},{1,0},{2,3},{3,2},{4,5},{5,4},{6,7},{7,6},{8,9},{9,8},{10,11... | collective-permute-start | bytes 884744 | tf_op jit(solution)/shard_map/ppermute | solution.py:49
  39.7 2.8 %collective-permute-done.5.outer_ref = bf16[3,96,512]{2,1,0:T(8,128)(2,1)S(1)} collective-permute-done((bf16[3,96,512]{2,1,0:T(8,128)(2,1)}, bf16[3,96,512]{2,1,0:T(8,128)(2,1)S(1)}, u32[]{:S(2)}, u32[]{:S(2)}) %collective-permute-start.5) | collective-permute-done | bytes 294944 | tf_op jit(solution)/shard_map/ppermute | solution.py:49
  42.5 15.8 %block_kernel.1 = (bf16[4,90,512]{2,1,0:T(8,128)(2,1)S(1)}, bf16[1088,512]{1,0:T(8,128)(2,1)}, bf16[1088,512]{1,0:T(8,128)(2,1)}, bf16[1088,512]{1,0:T(8,128)(2,...) custom-call(s32[5]{0:T(128)S(1)} %stack.36.ocean_ref, ...), custom_call_target="tpu_custom_call" | custom-call | flops 4831838208 | bytes 12582912 | tf_op jit(solution)/shard_map/block_kernel/pallas_call | solution.py:290
  59.1 1.6 %collective-permute-start.8 = (bf16[1088,512]{1,0:T(8,128)(2,1)}, bf16[1088,512]{1,0:T(8,128)(2,1)}, u32[]{:S(2)}, u32[]{:S(2)}) collective-permute-start(bf16[1088,512]{1,0:T(8,128)(2,1)} %get-tuple-element.43), channel_id=1, source_target_pairs={{0,16},{4,20},{8,24},{12,28},{16,32},{20,36},{24,40},{28,44},{32,4... | collective-permute-start | bytes 3342344 | tf_op jit(solution)/shard_map/ppermute | solution.py:520
  60.7 1.0 collective-permute-start.9
  62.8 13.7 %couple_kernel.1 = bf16[512,512]{1,0:T(8,128)(2,1)S(1)} custom-call(s32[1]{0:T(128)} %bitcast.4.lat_ref, bf16[3,96,512]{2,1,0:T(8,128)(2,1)S(1)} %collective-permute-done.16.outer_ref, bf16[4,96,512]{2,1,0:T(8,128)(2,1)S(1)} %get-tuple-element.79.own_ref, bf16[3,96,512]{2,1,0:T(8,128)(2,1)S(1)} %collective-permute-done.17.inner_ref, ...), custom_call_target="tpu_custom_call" | custom-call | flops 10066329600 | bytes 4194304 | tf_op jit(solution)/shard_map/couple_kernel/pallas_call | solution.py:369
  77.2 3.5 %collective-permute-start.18 = (bf16[16,8,512]{2,1,0:T(8,128)(2,1)S(1)}, bf16[16,8,512]{2,1,0:T(8,128)(2,1)S(1)}, u32[]{:S(2)}, u32[]{:S(2)}) collective-permute-start(bf16[16,8,512]{2,1,0:T(8,128)(2,1)S(1)} %get-tuple-element.87), channel_id=1, source_target_pairs={{0,2},{1,3},{2,0},{3,1},{4,6},{5,7},{6,4},{7,5},{8,10},{9,11},{10,... | collective-permute-start | bytes 393224 | tf_op jit(solution)/shard_map/ppermute | solution.py:546
  80.7 3.3 %collective-permute-start.20 = (bf16[16,8,512]{2,1,0:T(8,128)(2,1)S(1)}, bf16[16,8,512]{2,1,0:T(8,128)(2,1)}, u32[]{:S(2)}, u32[]{:S(2)}) collective-permute-start(bf16[16,8,512]{2,1,0:T(8,128)(2,1)S(1)} %get-tuple-element.88), channel_id=1, source_target_pairs={{0,3},{1,0},{2,1},{3,2},{4,7},{5,4},{6,5},{7,6},{8,11},{9,8},{10,9... | collective-permute-start | bytes 393224 | tf_op jit(solution)/shard_map/ppermute | solution.py:546
  84.0 3.2 %collective-permute-done.8 = bf16[1088,512]{1,0:T(8,128)(2,1)} collective-permute-done((bf16[1088,512]{1,0:T(8,128)(2,1)}, bf16[1088,512]{1,0:T(8,128)(2,1)}, u32[]{:S(2)}, u32[]{:S(2)}) %collective-permute-start.8) | collective-permute-done | bytes 1114144 | tf_op jit(solution)/shard_map/ppermute | solution.py:520
  88.1 2.4 %add_convert_fusion.5 = (bf16[256,512]{1,0:T(8,128)(2,1)S(1)}, bf16[256,512]{1,0:T(8,128)(2,1)S(1)}, bf16[256,512]{1,0:T(8,128)(2,1)S(1)}, bf16[256,512]{1,0:T(8,128)(2,1)S(1)}) fusion(bf16[1088,512]{1,0:T(8,128)(2,1)} %collective-permute-done.9, s32[]{:T(128)S(6)} %select_n.161, bf16[1088,512]{1,0:T(8,128)(2,1)} %collective-permute-done.8, ...), kind=kLoop, calls=%fused_computation.14 | loop fusion | flops 4194304 | bytes 5242896 | tf_op jit(solution)/shard_map/convert.23
  90.6 1.7 %collective-permute-start.10 = (bf16[312,512]{1,0:T(8,128)(2,1)S(1)}, bf16[312,512]{1,0:T(8,128)(2,1)S(1)}, u32[]{:S(2)}, u32[]{:S(2)}) collective-permute-start(bf16[312,512]{1,0:T(8,128)(2,1)S(1)} %get-tuple-element.101), channel_id=1, source_target_pairs={{0,8},{4,12},{8,0},{12,4},{16,24},{20,28},{24,16},{28,20},{32,40},... | collective-permute-start | bytes 958472 | tf_op jit(solution)/shard_map/ppermute | solution.py:540
  93.0 2.0 %collective-permute-start.12 = (bf16[312,512]{1,0:T(8,128)(2,1)S(1)}, bf16[312,512]{1,0:T(8,128)(2,1)S(1)}, u32[]{:S(2)}, u32[]{:S(2)}) collective-permute-start(bf16[312,512]{1,0:T(8,128)(2,1)S(1)} %get-tuple-element.103), channel_id=1, source_target_pairs={{0,12},{4,0},{8,4},{12,8},{16,28},{20,16},{24,20},{28,24},{32,44},... | collective-permute-start | bytes 958472 | tf_op jit(solution)/shard_map/ppermute | solution.py:540
  95.0 1.7 %fusion.5 = bf16[16,8,512]{2,1,0:T(8,128)(2,1)} fusion(bf16[16,8,512]{2,1,0:T(8,128)(2,1)} %collective-permute-done.20, bf16[16,8,512]{2,1,0:T(8,128)(2,1)} %collective-permute-done.19, bf16[16,8,512]{2,1,0:T(8,128)(2,1)S(1)} %collective-permute-done.18, bf16[16,4,8,512]{3,2,1,0:T(8,128)(2,1)S(1)} %bitcast.59, s32[]{:T(128)S(6)} %select_n.165), kind=kLoop, calls=%fused_computation.26 | loop fusion | flops 524288 | bytes 655364 | tf_op jit(solution)/shard_map/convert_element_type | solution.py:547
  96.6 3.5 %all-to-all-start = ((bf16[16,8,512]{2,1,0:T(8,128)(2,1)}), bf16[16,8,512]{2,1,0:T(8,128)(2,1)S(1)}, u32[]{:S(2)}, u32[]{:S(2)}) async-start(bf16[16,8,512]{2,1,0:T(8,128)(2,1)} %fusion.5), calls=%async_computation | async-start | bytes 262144 | tf_op jit(solution)/shard_map/all_to_all | solution.py:547
  100.2 1.6 %collective-permute-done.11 = bf16[312,512]{1,0:T(8,128)(2,1)S(1)} collective-permute-done((bf16[312,512]{1,0:T(8,128)(2,1)S(1)}, bf16[312,512]{1,0:T(8,128)(2,1)S(1)}, u32[]{:S(2)}, u32[]{:S(2)}) %collective-permute-start.11) | collective-permute-done | bytes 319520 | tf_op jit(solution)/shard_map/ppermute | solution.py:540
  102.1 3.6 %collective-permute-start.13 = (bf16[120,512]{1,0:T(8,128)(2,1)S(1)}, bf16[120,512]{1,0:T(8,128)(2,1)S(1)}, u32[]{:S(2)}, u32[]{:S(2)}) collective-permute-start(bf16[120,512]{1,0:T(8,128)(2,1)S(1)} %get-tuple-element.90), channel_id=1, source_target_pairs={{0,2},{1,3},{2,0},{3,1},{4,6},{5,7},{6,4},{7,5},{8,10},{9,11},{10,... | collective-permute-start | bytes 368648 | tf_op jit(solution)/shard_map/ppermute | solution.py:561
  105.7 3.3 %collective-permute-start.15 = (bf16[120,512]{1,0:T(8,128)(2,1)S(1)}, bf16[120,512]{1,0:T(8,128)(2,1)S(1)}, u32[]{:S(2)}, u32[]{:S(2)}) collective-permute-start(bf16[120,512]{1,0:T(8,128)(2,1)S(1)} %get-tuple-element.91), channel_id=1, source_target_pairs={{0,3},{1,0},{2,1},{3,2},{4,7},{5,4},{6,5},{7,6},{8,11},{9,8},{10,9... | collective-permute-start | bytes 368648 | tf_op jit(solution)/shard_map/ppermute | solution.py:561
  109.0 2.3 %collective-permute-done.14 = bf16[120,512]{1,0:T(8,128)(2,1)S(1)} collective-permute-done((bf16[120,512]{1,0:T(8,128)(2,1)S(1)}, bf16[120,512]{1,0:T(8,128)(2,1)S(1)}, u32[]{:S(2)}, u32[]{:S(2)}) %collective-permute-start.14) | collective-permute-done | bytes 122912 | tf_op jit(solution)/shard_map/ppermute | solution.py:561
  111.4 5.1 %collective-permute-start.22 = (bf16[128,512]{1,0:T(8,128)(2,1)S(1)}, bf16[128,512]{1,0:T(8,128)(2,1)S(1)}, u32[]{:S(2)}, u32[]{:S(2)}) collective-permute-start(bf16[128,512]{1,0:T(8,128)(2,1)S(1)} %pad_maximum_fusion.6.mine_ref), channel_id=1, source_target_pairs={{0,128},{128,0},{1,129},{129,1},{2,130},{130,2},{3,131},{131,3},{4... | collective-permute-start | bytes 393224 | tf_op jit(solution)/shard_map/ppermute | solution.py:564
  116.5 5.8 %collective-permute-start.21 = (bf16[128,512]{1,0:T(8,128)(2,1)S(1)}, bf16[128,512]{1,0:T(8,128)(2,1)S(1)}, u32[]{:S(2)}, u32[]{:S(2)}) collective-permute-start(bf16[128,512]{1,0:T(8,128)(2,1)S(1)} %pad_maximum_fusion.6.mine_ref), channel_id=1, source_target_pairs={{0,64},{64,0},{1,65},{65,1},{2,66},{66,2},{3,67},{67,3},{4,68},{68... | collective-permute-start | bytes 393224 | tf_op jit(solution)/shard_map/ppermute | solution.py:563
  122.3 4.6 %collective-permute-start.23 = (bf16[128,512]{1,0:T(8,128)(2,1)S(1)}, bf16[128,512]{1,0:T(8,128)(2,1)S(1)}, u32[]{:S(2)}, u32[]{:S(2)}) collective-permute-start(bf16[128,512]{1,0:T(8,128)(2,1)S(1)} %collective-permute-done.22.across_ref), channel_id=1, source_target_pairs={{0,64},{64,0},{1,65},{65,1},{2,66},{66,2},{3,67},{67,3},{4,68},{68... | collective-permute-start | bytes 393224 | tf_op jit(solution)/shard_map/ppermute | solution.py:565
  127.0 1.0 copy.37
  128.0 1.5 %finish_kernel.1 = (f32[49,512]{1,0:T(8,128)}, f32[1,512]{1,0:T(1,128)}, f32[8,2048]{1,0:T(8,128)}, f32[32,512]{1,0:T(8,128)}, f32[49,512]{1,0:T(8,128)}, /*inde...) custom-call(s32[2]{0:T(128)S(1)} %pad_add_fusion.place_ref, ...), custom_call_target="tpu_custom_call" | custom-call | tf_op jit(solution)/shard_map/finish_kernel/pallas_call | solution.py:416
  (93 shorter events, 13.9 us)
Async XLA Ops:
  0.6 10.5 %copy-start.5 = (bf16[1,4,90,512]{3,1,2,0:T(4,128)(2,1)S(1)}, bf16[1,4,90,512]{3,1,2,0:T(4,128)(2,1)}, u32[]{:S(2)}) copy-start(bf16[1,4,90,512]{3,1,2,0:T(4,128)(2,1)} %param.13) | copy-start | bytes 1105924
  2.3 9.4 %collective-permute-start = (bf16[4,3,640]{2,1,0:T(4,128)(2,1)S(1)}, bf16[4,3,640]{2,1,0:T(4,128)(2,1)S(1)}, u32[]{:S(2)}, u32[]{:S(2)}) collective-permute-start(bf16[4,3,640]{2,1,0:T(4,128)(2,1)S(1)} %maximum_bitcast_fusion), channel_id=1, source_target_pairs={{0,4},{4,8},{8,12},{12,16},{16,20},{20,24},{24,28},{28,32},{32,36}... | collective-permute-start | bytes 46088 | tf_op jit(solution)/shard_map/ppermute | solution.py:452
  4.6 7.1 %collective-permute-start.1 = (bf16[4,3,640]{2,1,0:T(4,128)(2,1)S(1)}, bf16[4,3,640]{2,1,0:T(4,128)(2,1)S(1)}, u32[]{:S(2)}, u32[]{:S(2)}) collective-permute-start(bf16[4,3,640]{2,1,0:T(4,128)(2,1)S(1)} %maximum_bitcast_fusion.1), channel_id=1, source_target_pairs={{0,60},{4,0},{8,4},{12,8},{16,12},{20,16},{24,20},{28,24},{32,28},... | collective-permute-start | bytes 46088 | tf_op jit(solution)/shard_map/ppermute | solution.py:453
  11.6 3.2 %copy-start.6 = (f32[512]{0:T(512)S(1)}, f32[512]{0:T(512)}, u32[]{:S(2)}) copy-start(f32[512]{0:T(512)} %param.21) | copy-start | bytes 6148
  11.6 3.2 %copy-start.7 = (f32[512]{0:T(512)S(1)}, f32[512]{0:T(512)}, u32[]{:S(2)}) copy-start(f32[512]{0:T(512)} %param.17) | copy-start | bytes 6148
  11.6 3.2 %copy-start.3 = (bf16[512,512]{1,0:T(8,128)(2,1)S(1)}, bf16[512,512]{1,0:T(8,128)(2,1)}, u32[]{:S(2)}) copy-start(bf16[512,512]{1,0:T(8,128)(2,1)} %param.25) | copy-start | bytes 1572868
  11.6 3.2 %copy-start.4 = (bf16[512,512]{1,0:T(8,128)(2,1)S(1)}, bf16[512,512]{1,0:T(8,128)(2,1)}, u32[]{:S(2)}) copy-start(bf16[512,512]{1,0:T(8,128)(2,1)} %param.24) | copy-start | bytes 1572868
  11.9 4.2 %collective-permute-start.2 = (bf16[4,96,512]{2,1,0:T(8,128)(2,1)S(1)}, bf16[4,96,512]{2,1,0:T(8,128)(2,1)S(1)}, u32[]{:S(2)}, u32[]{:S(2)}) collective-permute-start(bf16[4,96,512]{2,1,0:T(8,128)(2,1)S(1)} %get-tuple-element.82), channel_id=1, source_target_pairs={{0,64},{64,0},{1,65},{65,1},{2,66},{66,2},{3,67},{67,3},{4,68},{68... | collective-permute-start | bytes 1179656 | tf_op jit(solution)/shard_map/ppermute | solution.py:459
  16.3 10.1 %collective-permute-start.3 = (bf16[2,96,512]{2,1,0:T(8,128)(2,1)S(1)}, bf16[2,96,512]{2,1,0:T(8,128)(2,1)S(1)}, u32[]{:S(2)}, u32[]{:S(2)}) collective-permute-start(bf16[2,96,512]{2,1,0:T(8,128)(2,1)S(1)} %fusion.8), channel_id=1, source_target_pairs={{0,128},{128,0},{1,129},{129,1},{2,130},{130,2},{3,131},{131,3},{4... | collective-permute-start | bytes 589832 | tf_op jit(solution)/shard_map/ppermute | solution.py:463
  26.5 3.5 %collective-permute-start.4 = (bf16[2,96,512]{2,1,0:T(8,128)(2,1)S(1)}, bf16[2,96,512]{2,1,0:T(8,128)(2,1)S(1)}, u32[]{:S(2)}, u32[]{:S(2)}) collective-permute-start(bf16[2,96,512]{2,1,0:T(8,128)(2,1)S(1)} %collective-permute-done.3), channel_id=1, source_target_pairs={{0,64},{64,0},{1,65},{65,1},{2,66},{66,2},{3,67},{67,3},{4,68},{68... | collective-permute-start | bytes 589832 | tf_op jit(solution)/shard_map/ppermute | solution.py:477
  31.6 10.9 %collective-permute-start.5 = (bf16[3,96,512]{2,1,0:T(8,128)(2,1)}, bf16[3,96,512]{2,1,0:T(8,128)(2,1)S(1)}, u32[]{:S(2)}, u32[]{:S(2)}) collective-permute-start(bf16[3,96,512]{2,1,0:T(8,128)(2,1)} %get-tuple-element.96), channel_id=1, source_target_pairs={{0,1},{1,0},{2,3},{3,2},{4,5},{5,4},{6,7},{7,6},{8,9},{9,8},{10,11... | collective-permute-start | bytes 884744 | tf_op jit(solution)/shard_map/ppermute | solution.py:49
  35.2 7.3 %collective-permute-start.6 = (bf16[3,96,512]{2,1,0:T(8,128)(2,1)S(1)}, bf16[3,96,512]{2,1,0:T(8,128)(2,1)S(1)}, u32[]{:S(2)}, u32[]{:S(2)}) collective-permute-start(bf16[3,96,512]{2,1,0:T(8,128)(2,1)S(1)} %get-tuple-element.95), channel_id=1, source_target_pairs={{0,0},{1,2},{2,1},{3,3},{4,4},{5,6},{6,5},{7,7},{8,8},{9,10},{10,9... | collective-permute-start | bytes 884744 | tf_op jit(solution)/shard_map/ppermute | solution.py:50
  36.8 25.0 %collective-permute-start.16 = (bf16[3,96,512]{2,1,0:T(8,128)(2,1)}, bf16[3,96,512]{2,1,0:T(8,128)(2,1)S(1)}, u32[]{:S(2)}, u32[]{:S(2)}) collective-permute-start(bf16[3,96,512]{2,1,0:T(8,128)(2,1)} %get-tuple-element.94), channel_id=1, source_target_pairs={{0,1},{1,0},{2,3},{3,2},{4,5},{5,4},{6,7},{7,6},{8,9},{9,8},{10,11... | collective-permute-start | bytes 884744 | tf_op jit(solution)/shard_map/ppermute | solution.py:49
  39.0 22.7 %collective-permute-start.17 = (bf16[3,96,512]{2,1,0:T(8,128)(2,1)S(1)}, bf16[3,96,512]{2,1,0:T(8,128)(2,1)S(1)}, u32[]{:S(2)}, u32[]{:S(2)}) collective-permute-start(bf16[3,96,512]{2,1,0:T(8,128)(2,1)S(1)} %get-tuple-element.93), channel_id=1, source_target_pairs={{0,0},{1,2},{2,1},{3,3},{4,4},{5,6},{6,5},{7,7},{8,8},{9,10},{10,9... | collective-permute-start | bytes 884744 | tf_op jit(solution)/shard_map/ppermute | solution.py:50
  59.1 21.6 %collective-permute-start.7 = (bf16[1088,512]{1,0:T(8,128)(2,1)}, bf16[1088,512]{1,0:T(8,128)(2,1)}, u32[]{:S(2)}, u32[]{:S(2)}) collective-permute-start(bf16[1088,512]{1,0:T(8,128)(2,1)} %get-tuple-element.42), channel_id=1, source_target_pairs={{0,32},{4,36},{8,40},{12,44},{16,48},{20,52},{24,56},{28,60},{32,0... | collective-permute-start | bytes 3342344 | tf_op jit(solution)/shard_map/ppermute | solution.py:520
  59.1 28.1 %collective-permute-start.8 = (bf16[1088,512]{1,0:T(8,128)(2,1)}, bf16[1088,512]{1,0:T(8,128)(2,1)}, u32[]{:S(2)}, u32[]{:S(2)}) collective-permute-start(bf16[1088,512]{1,0:T(8,128)(2,1)} %get-tuple-element.43), channel_id=1, source_target_pairs={{0,16},{4,20},{8,24},{12,28},{16,32},{20,36},{24,40},{28,44},{32,4... | collective-permute-start | bytes 3342344 | tf_op jit(solution)/shard_map/ppermute | solution.py:520
  60.7 26.5 %collective-permute-start.9 = (bf16[1088,512]{1,0:T(8,128)(2,1)}, bf16[1088,512]{1,0:T(8,128)(2,1)}, u32[]{:S(2)}, u32[]{:S(2)}) collective-permute-start(bf16[1088,512]{1,0:T(8,128)(2,1)} %get-tuple-element.44), channel_id=1, source_target_pairs={{0,48},{4,52},{8,56},{12,60},{16,0},{20,4},{24,8},{28,12},{32,16},... | collective-permute-start | bytes 3342344 | tf_op jit(solution)/shard_map/ppermute | solution.py:520
  61.8 1.0 copy-start.1
  62.8 24.4 %copy-start.2 = (bf16[1088,512]{1,0:T(8,128)(2,1)S(1)}, bf16[1088,512]{1,0:T(8,128)(2,1)}, u32[]{:S(2)}) copy-start(bf16[1088,512]{1,0:T(8,128)(2,1)} %get-tuple-element.41) | copy-start | bytes 3342340
  77.2 15.8 %collective-permute-start.18 = (bf16[16,8,512]{2,1,0:T(8,128)(2,1)S(1)}, bf16[16,8,512]{2,1,0:T(8,128)(2,1)S(1)}, u32[]{:S(2)}, u32[]{:S(2)}) collective-permute-start(bf16[16,8,512]{2,1,0:T(8,128)(2,1)S(1)} %get-tuple-element.87), channel_id=1, source_target_pairs={{0,2},{1,3},{2,0},{3,1},{4,6},{5,7},{6,4},{7,5},{8,10},{9,11},{10,... | collective-permute-start | bytes 393224 | tf_op jit(solution)/shard_map/ppermute | solution.py:546
  80.7 14.3 %collective-permute-start.19 = (bf16[16,8,512]{2,1,0:T(8,128)(2,1)}, bf16[16,8,512]{2,1,0:T(8,128)(2,1)}, u32[]{:S(2)}, u32[]{:S(2)}) collective-permute-start(bf16[16,8,512]{2,1,0:T(8,128)(2,1)} %get-tuple-element.89), channel_id=1, source_target_pairs={{0,1},{1,2},{2,3},{3,0},{4,5},{5,6},{6,7},{7,4},{8,9},{9,10},{10,1... | collective-permute-start | bytes 393224 | tf_op jit(solution)/shard_map/ppermute | solution.py:546
  80.7 14.3 %collective-permute-start.20 = (bf16[16,8,512]{2,1,0:T(8,128)(2,1)S(1)}, bf16[16,8,512]{2,1,0:T(8,128)(2,1)}, u32[]{:S(2)}, u32[]{:S(2)}) collective-permute-start(bf16[16,8,512]{2,1,0:T(8,128)(2,1)S(1)} %get-tuple-element.88), channel_id=1, source_target_pairs={{0,3},{1,0},{2,1},{3,2},{4,7},{5,4},{6,5},{7,6},{8,11},{9,8},{10,9... | collective-permute-start | bytes 393224 | tf_op jit(solution)/shard_map/ppermute | solution.py:546
  90.6 9.6 %collective-permute-start.10 = (bf16[312,512]{1,0:T(8,128)(2,1)S(1)}, bf16[312,512]{1,0:T(8,128)(2,1)S(1)}, u32[]{:S(2)}, u32[]{:S(2)}) collective-permute-start(bf16[312,512]{1,0:T(8,128)(2,1)S(1)} %get-tuple-element.101), channel_id=1, source_target_pairs={{0,8},{4,12},{8,0},{12,4},{16,24},{20,28},{24,16},{28,20},{32,40},... | collective-permute-start | bytes 958472 | tf_op jit(solution)/shard_map/ppermute | solution.py:540
  92.3 9.5 %collective-permute-start.11 = (bf16[312,512]{1,0:T(8,128)(2,1)S(1)}, bf16[312,512]{1,0:T(8,128)(2,1)S(1)}, u32[]{:S(2)}, u32[]{:S(2)}) collective-permute-start(bf16[312,512]{1,0:T(8,128)(2,1)S(1)} %get-tuple-element.102), channel_id=1, source_target_pairs={{0,4},{4,8},{8,12},{12,0},{16,20},{20,24},{24,28},{28,16},{32,36},... | collective-permute-start | bytes 958472 | tf_op jit(solution)/shard_map/ppermute | solution.py:540
  93.0 8.8 %collective-permute-start.12 = (bf16[312,512]{1,0:T(8,128)(2,1)S(1)}, bf16[312,512]{1,0:T(8,128)(2,1)S(1)}, u32[]{:S(2)}, u32[]{:S(2)}) collective-permute-start(bf16[312,512]{1,0:T(8,128)(2,1)S(1)} %get-tuple-element.103), channel_id=1, source_target_pairs={{0,12},{4,0},{8,4},{12,8},{16,28},{20,16},{24,20},{28,24},{32,44},... | collective-permute-start | bytes 958472 | tf_op jit(solution)/shard_map/ppermute | solution.py:540
  96.6 12.3 %all-to-all-start = ((bf16[16,8,512]{2,1,0:T(8,128)(2,1)}), bf16[16,8,512]{2,1,0:T(8,128)(2,1)S(1)}, u32[]{:S(2)}, u32[]{:S(2)}) async-start(bf16[16,8,512]{2,1,0:T(8,128)(2,1)} %fusion.5), calls=%async_computation | async-start | bytes 262144 | tf_op jit(solution)/shard_map/all_to_all | solution.py:547
  102.1 6.9 %collective-permute-start.13 = (bf16[120,512]{1,0:T(8,128)(2,1)S(1)}, bf16[120,512]{1,0:T(8,128)(2,1)S(1)}, u32[]{:S(2)}, u32[]{:S(2)}) collective-permute-start(bf16[120,512]{1,0:T(8,128)(2,1)S(1)} %get-tuple-element.90), channel_id=1, source_target_pairs={{0,2},{1,3},{2,0},{3,1},{4,6},{5,7},{6,4},{7,5},{8,10},{9,11},{10,... | collective-permute-start | bytes 368648 | tf_op jit(solution)/shard_map/ppermute | solution.py:561
  105.7 5.6 %collective-permute-start.14 = (bf16[120,512]{1,0:T(8,128)(2,1)S(1)}, bf16[120,512]{1,0:T(8,128)(2,1)S(1)}, u32[]{:S(2)}, u32[]{:S(2)}) collective-permute-start(bf16[120,512]{1,0:T(8,128)(2,1)S(1)} %get-tuple-element.92), channel_id=1, source_target_pairs={{0,1},{1,2},{2,3},{3,0},{4,5},{5,6},{6,7},{7,4},{8,9},{9,10},{10,1... | collective-permute-start | bytes 368648 | tf_op jit(solution)/shard_map/ppermute | solution.py:561
  105.7 5.6 %collective-permute-start.15 = (bf16[120,512]{1,0:T(8,128)(2,1)S(1)}, bf16[120,512]{1,0:T(8,128)(2,1)S(1)}, u32[]{:S(2)}, u32[]{:S(2)}) collective-permute-start(bf16[120,512]{1,0:T(8,128)(2,1)S(1)} %get-tuple-element.91), channel_id=1, source_target_pairs={{0,3},{1,0},{2,1},{3,2},{4,7},{5,4},{6,5},{7,6},{8,11},{9,8},{10,9... | collective-permute-start | bytes 368648 | tf_op jit(solution)/shard_map/ppermute | solution.py:561
  111.4 10.9 %collective-permute-start.22 = (bf16[128,512]{1,0:T(8,128)(2,1)S(1)}, bf16[128,512]{1,0:T(8,128)(2,1)S(1)}, u32[]{:S(2)}, u32[]{:S(2)}) collective-permute-start(bf16[128,512]{1,0:T(8,128)(2,1)S(1)} %pad_maximum_fusion.6.mine_ref), channel_id=1, source_target_pairs={{0,128},{128,0},{1,129},{129,1},{2,130},{130,2},{3,131},{131,3},{4... | collective-permute-start | bytes 393224 | tf_op jit(solution)/shard_map/ppermute | solution.py:564
  116.5 11.5 %collective-permute-start.21 = (bf16[128,512]{1,0:T(8,128)(2,1)S(1)}, bf16[128,512]{1,0:T(8,128)(2,1)S(1)}, u32[]{:S(2)}, u32[]{:S(2)}) collective-permute-start(bf16[128,512]{1,0:T(8,128)(2,1)S(1)} %pad_maximum_fusion.6.mine_ref), channel_id=1, source_target_pairs={{0,64},{64,0},{1,65},{65,1},{2,66},{66,2},{3,67},{67,3},{4,68},{68... | collective-permute-start | bytes 393224 | tf_op jit(solution)/shard_map/ppermute | solution.py:563
  122.3 5.7 %collective-permute-start.23 = (bf16[128,512]{1,0:T(8,128)(2,1)S(1)}, bf16[128,512]{1,0:T(8,128)(2,1)S(1)}, u32[]{:S(2)}, u32[]{:S(2)}) collective-permute-start(bf16[128,512]{1,0:T(8,128)(2,1)S(1)} %collective-permute-done.22.across_ref), channel_id=1, source_target_pairs={{0,64},{64,0},{1,65},{65,1},{2,66},{66,2},{3,67},{67,3},{4,68},{68... | collective-permute-start | bytes 393224 | tf_op jit(solution)/shard_map/ppermute | solution.py:565
  (1 other events, 0.8 us)

commit v5 on v4

--- a/solution.py
+++ b/solution.py
@@ -407,7 +407,7 @@
         for cb in range(4):
             expand_ref[:, cb * 512 : cb * 512 + 512] = total[n, cb * 8 : cb * 8 + 8, :]
         contract_ref[...] = total[n, 32:64, :]
-        outs[8 + n][...] = total[n, 120:128, :]
+        outs[8 + n][...] = total[n, 114:122, :]
 
 
 def finish(here, mine, mine_beside, across, across_beside):
@@ -418,7 +418,7 @@
         out_shape=[jax.ShapeDtypeStruct(shape, f32) for shape in shapes],
         in_specs=[pl.BlockSpec(memory_space=pltpu.SMEM)] + [vmem] * 4,
         out_specs=[vmem] * 10,
-        scratch_shapes=[pltpu.VMEM((2, 128, 512), f32)],
+        scratch_shapes=[pltpu.VMEM((2, 122, 512), f32)],
         compiler_params=pltpu.CompilerParams(vmem_limit_bytes=8 * 1024 * 1024),
         name="finish_kernel",
     )(here, mine, mine_beside, across, across_beside)
@@ -529,7 +529,7 @@
         kernel_rows,
         jnp.where(is_ocean, 1.0 / copies, 1.0).astype(f32).reshape(1),
     )
-    small = total_of([part[1024:1080] for part in parts])
+    small = total_of([part[1024:1074] for part in parts])
     near = jnp.where(core == 0, y, x)
     messages = []
     for k in range(4):
@@ -552,7 +552,7 @@
         [
             table[:128].reshape(4, 4, 8, 512).transpose(1, 0, 2, 3).reshape(4, 32, 512),
             table[128:256].reshape(4, 32, 512),
-            jnp.broadcast_to(table[256:][None], (4, 56, 512)),
+            jnp.broadcast_to(table[256:][None], (4, 50, 512)),
         ],
         axis=1,
     ).astype(bf16)

time: 130 us -> 130 us (level)
  no operation moved by 1% of the time
where the time goes in v5:
time: 130 us
  starting transfers between devices  63.4 us (49%)
  Pallas kernels  30.9 us (24%)
  waiting for transfers between devices  16.9 us (13%)
  other arithmetic  9.99 us (8%)
  local copies, waits for them, and re-layouts  6.82 us (5%)
    pallas_call x1, Pallas kernels, block(): pl.pallas_call(block_kernel, out_shape=(jax.ShapeDtypeStruct((4, 90, 512)...  15.8 us
    pallas_call x1, Pallas kernels, couple(): pl.pallas_call(couple_kernel, out_shape=jax.ShapeDtypeStruct((512, 512),...  13.7 us
    ppermute x3, starting transfers between devices, on_device(): rows[k] = lax.ppermute(rows[k], 'lat', ring(4, k))  6.87 us
    ppermute x3, starting transfers between devices, on_device(): shares[k] = lax.ppermute(shares[k], 'lat', ring(4, k))  6.79 us
    ppermute x2, starting transfers between devices, lat_halo(): outer = lax.ppermute(outer, 'lat', [(0, 1), (1, 0), (2, 3), (3, 2)])  5.87 us
    ppermute x1, starting transfers between devices, on_device(): mine_beside = lax.ppermute(mine, 'core', ring(2, 1))  5.8 us
    ppermute x1, starting transfers between devices, on_device(): got = lax.ppermute(half, 'zh', ring(2, 1))  5.26 us
    ppermute x1, starting transfers between devices, on_device(): across = lax.ppermute(mine, 'zh', ring(2, 1))  5.09 us
  transfers between devices with their start and end apart: 25, of which 7 were waited for; matrix products, arithmetic and copies ran while one was open for 9% of the time, Pallas kernels for 23%

profile of v5, /device:TPU:1, one launch (start us, length us, event | category | flops | bytes accessed | tf_op | source)
XLA Modules:
  0.0 129.6 jit_solution(14167896872264092665)
XLA Ops:
  2.3 2.2 %collective-permute-start = (bf16[4,3,640]{2,1,0:T(4,128)(2,1)S(1)}, bf16[4,3,640]{2,1,0:T(4,128)(2,1)S(1)}, u32[]{:S(2)}, u32[]{:S(2)}) collective-permute-start(bf16[4,3,640]{2,1,0:T(4,128)(2,1)S(1)} %maximum_bitcast_fusion), channel_id=1, source_target_pairs={{0,4},{4,8},{8,12},{12,16},{16,20},{20,24},{24,28},{28,32},{32,36}... | collective-permute-start | bytes 46088 | tf_op jit(solution)/shard_map/ppermute | solution.py:452
  4.6 3.7 %collective-permute-start.1 = (bf16[4,3,640]{2,1,0:T(4,128)(2,1)S(1)}, bf16[4,3,640]{2,1,0:T(4,128)(2,1)S(1)}, u32[]{:S(2)}, u32[]{:S(2)}) collective-permute-start(bf16[4,3,640]{2,1,0:T(4,128)(2,1)S(1)} %maximum_bitcast_fusion.1), channel_id=1, source_target_pairs={{0,60},{4,0},{8,4},{12,8},{16,12},{20,16},{24,20},{28,24},{32,28},... | collective-permute-start | bytes 46088 | tf_op jit(solution)/shard_map/ppermute | solution.py:453
  9.0 1.1 fusion
  11.9 2.9 %collective-permute-start.2 = (bf16[4,96,512]{2,1,0:T(8,128)(2,1)S(1)}, bf16[4,96,512]{2,1,0:T(8,128)(2,1)S(1)}, u32[]{:S(2)}, u32[]{:S(2)}) collective-permute-start(bf16[4,96,512]{2,1,0:T(8,128)(2,1)S(1)} %get-tuple-element.82), channel_id=1, source_target_pairs={{0,64},{64,0},{1,65},{65,1},{2,66},{66,2},{3,67},{67,3},{4,68},{68... | collective-permute-start | bytes 1179656 | tf_op jit(solution)/shard_map/ppermute | solution.py:459
  14.9 1.3 collective-permute-done.2
  16.3 5.3 %collective-permute-start.3 = (bf16[2,96,512]{2,1,0:T(8,128)(2,1)S(1)}, bf16[2,96,512]{2,1,0:T(8,128)(2,1)S(1)}, u32[]{:S(2)}, u32[]{:S(2)}) collective-permute-start(bf16[2,96,512]{2,1,0:T(8,128)(2,1)S(1)} %fusion.8), channel_id=1, source_target_pairs={{0,128},{128,0},{1,129},{129,1},{2,130},{130,2},{3,131},{131,3},{4... | collective-permute-start | bytes 589832 | tf_op jit(solution)/shard_map/ppermute | solution.py:463
  21.7 4.7 %collective-permute-done.3 = bf16[2,96,512]{2,1,0:T(8,128)(2,1)S(1)} collective-permute-done((bf16[2,96,512]{2,1,0:T(8,128)(2,1)S(1)}, bf16[2,96,512]{2,1,0:T(8,128)(2,1)S(1)}, u32[]{:S(2)}, u32[]{:S(2)}) %collective-permute-start.3) | collective-permute-done | bytes 196640 | tf_op jit(solution)/shard_map/ppermute | solution.py:463
  26.5 2.5 %collective-permute-start.4 = (bf16[2,96,512]{2,1,0:T(8,128)(2,1)S(1)}, bf16[2,96,512]{2,1,0:T(8,128)(2,1)S(1)}, u32[]{:S(2)}, u32[]{:S(2)}) collective-permute-start(bf16[2,96,512]{2,1,0:T(8,128)(2,1)S(1)} %collective-permute-done.3), channel_id=1, source_target_pairs={{0,64},{64,0},{1,65},{65,1},{2,66},{66,2},{3,67},{67,3},{4,68},{68... | collective-permute-start | bytes 589832 | tf_op jit(solution)/shard_map/ppermute | solution.py:477
  31.6 3.6 %collective-permute-start.5 = (bf16[3,96,512]{2,1,0:T(8,128)(2,1)}, bf16[3,96,512]{2,1,0:T(8,128)(2,1)S(1)}, u32[]{:S(2)}, u32[]{:S(2)}) collective-permute-start(bf16[3,96,512]{2,1,0:T(8,128)(2,1)} %get-tuple-element.96), channel_id=1, source_target_pairs={{0,1},{1,0},{2,3},{3,2},{4,5},{5,4},{6,7},{7,6},{8,9},{9,8},{10,11... | collective-permute-start | bytes 884744 | tf_op jit(solution)/shard_map/ppermute | solution.py:49
  36.8 2.2 %collective-permute-start.16 = (bf16[3,96,512]{2,1,0:T(8,128)(2,1)}, bf16[3,96,512]{2,1,0:T(8,128)(2,1)S(1)}, u32[]{:S(2)}, u32[]{:S(2)}) collective-permute-start(bf16[3,96,512]{2,1,0:T(8,128)(2,1)} %get-tuple-element.94), channel_id=1, source_target_pairs={{0,1},{1,0},{2,3},{3,2},{4,5},{5,4},{6,7},{7,6},{8,9},{9,8},{10,11... | collective-permute-start | bytes 884744 | tf_op jit(solution)/shard_map/ppermute | solution.py:49
  39.7 2.8 %collective-permute-done.5.outer_ref = bf16[3,96,512]{2,1,0:T(8,128)(2,1)S(1)} collective-permute-done((bf16[3,96,512]{2,1,0:T(8,128)(2,1)}, bf16[3,96,512]{2,1,0:T(8,128)(2,1)S(1)}, u32[]{:S(2)}, u32[]{:S(2)}) %collective-permute-start.5) | collective-permute-done | bytes 294944 | tf_op jit(solution)/shard_map/ppermute | solution.py:49
  42.5 15.8 %block_kernel.1 = (bf16[4,90,512]{2,1,0:T(8,128)(2,1)S(1)}, bf16[1088,512]{1,0:T(8,128)(2,1)}, bf16[1088,512]{1,0:T(8,128)(2,1)}, bf16[1088,512]{1,0:T(8,128)(2,...) custom-call(s32[5]{0:T(128)S(1)} %stack.36.ocean_ref, ...), custom_call_target="tpu_custom_call" | custom-call | flops 4831838208 | bytes 12582912 | tf_op jit(solution)/shard_map/block_kernel/pallas_call | solution.py:290
  59.1 1.6 %collective-permute-start.8 = (bf16[1088,512]{1,0:T(8,128)(2,1)}, bf16[1088,512]{1,0:T(8,128)(2,1)}, u32[]{:S(2)}, u32[]{:S(2)}) collective-permute-start(bf16[1088,512]{1,0:T(8,128)(2,1)} %get-tuple-element.43), channel_id=1, source_target_pairs={{0,16},{4,20},{8,24},{12,28},{16,32},{20,36},{24,40},{28,44},{32,4... | collective-permute-start | bytes 3342344 | tf_op jit(solution)/shard_map/ppermute | solution.py:520
  60.7 1.0 collective-permute-start.9
  62.8 13.7 %couple_kernel.1 = bf16[512,512]{1,0:T(8,128)(2,1)S(1)} custom-call(s32[1]{0:T(128)} %bitcast.4.lat_ref, bf16[3,96,512]{2,1,0:T(8,128)(2,1)S(1)} %collective-permute-done.16.outer_ref, bf16[4,96,512]{2,1,0:T(8,128)(2,1)S(1)} %get-tuple-element.79.own_ref, bf16[3,96,512]{2,1,0:T(8,128)(2,1)S(1)} %collective-permute-done.17.inner_ref, ...), custom_call_target="tpu_custom_call" | custom-call | flops 10066329600 | bytes 4194304 | tf_op jit(solution)/shard_map/couple_kernel/pallas_call | solution.py:369
  77.2 3.5 %collective-permute-start.18 = (bf16[16,8,512]{2,1,0:T(8,128)(2,1)S(1)}, bf16[16,8,512]{2,1,0:T(8,128)(2,1)S(1)}, u32[]{:S(2)}, u32[]{:S(2)}) collective-permute-start(bf16[16,8,512]{2,1,0:T(8,128)(2,1)S(1)} %get-tuple-element.87), channel_id=1, source_target_pairs={{0,2},{1,3},{2,0},{3,1},{4,6},{5,7},{6,4},{7,5},{8,10},{9,11},{10,... | collective-permute-start | bytes 393224 | tf_op jit(solution)/shard_map/ppermute | solution.py:546
  80.7 3.3 %collective-permute-start.20 = (bf16[16,8,512]{2,1,0:T(8,128)(2,1)S(1)}, bf16[16,8,512]{2,1,0:T(8,128)(2,1)}, u32[]{:S(2)}, u32[]{:S(2)}) collective-permute-start(bf16[16,8,512]{2,1,0:T(8,128)(2,1)S(1)} %get-tuple-element.88), channel_id=1, source_target_pairs={{0,3},{1,0},{2,1},{3,2},{4,7},{5,4},{6,5},{7,6},{8,11},{9,8},{10,9... | collective-permute-start | bytes 393224 | tf_op jit(solution)/shard_map/ppermute | solution.py:546
  84.0 3.2 %collective-permute-done.8 = bf16[1088,512]{1,0:T(8,128)(2,1)} collective-permute-done((bf16[1088,512]{1,0:T(8,128)(2,1)}, bf16[1088,512]{1,0:T(8,128)(2,1)}, u32[]{:S(2)}, u32[]{:S(2)}) %collective-permute-start.8) | collective-permute-done | bytes 1114144 | tf_op jit(solution)/shard_map/ppermute | solution.py:520
  88.1 2.4 %add_convert_fusion.5 = (bf16[256,512]{1,0:T(8,128)(2,1)S(1)}, bf16[256,512]{1,0:T(8,128)(2,1)S(1)}, bf16[256,512]{1,0:T(8,128)(2,1)S(1)}, bf16[256,512]{1,0:T(8,128)(2,1)S(1)}) fusion(bf16[1088,512]{1,0:T(8,128)(2,1)} %collective-permute-done.9, s32[]{:T(128)S(6)} %select_n.161, bf16[1088,512]{1,0:T(8,128)(2,1)} %collective-permute-done.8, ...), kind=kLoop, calls=%fused_computation.14 | loop fusion | flops 4194304 | bytes 5242896 | tf_op jit(solution)/shard_map/convert.23
  90.6 1.7 %collective-permute-start.10 = (bf16[306,512]{1,0:T(8,128)(2,1)S(1)}, bf16[306,512]{1,0:T(8,128)(2,1)S(1)}, u32[]{:S(2)}, u32[]{:S(2)}) collective-permute-start(bf16[306,512]{1,0:T(8,128)(2,1)S(1)} %get-tuple-element.101), channel_id=1, source_target_pairs={{0,8},{4,12},{8,0},{12,4},{16,24},{20,28},{24,16},{28,20},{32,40},... | collective-permute-start | bytes 940040 | tf_op jit(solution)/shard_map/ppermute | solution.py:540
  93.0 2.0 %collective-permute-start.12 = (bf16[306,512]{1,0:T(8,128)(2,1)S(1)}, bf16[306,512]{1,0:T(8,128)(2,1)S(1)}, u32[]{:S(2)}, u32[]{:S(2)}) collective-permute-start(bf16[306,512]{1,0:T(8,128)(2,1)S(1)} %get-tuple-element.103), channel_id=1, source_target_pairs={{0,12},{4,0},{8,4},{12,8},{16,28},{20,16},{24,20},{28,24},{32,44},... | collective-permute-start | bytes 940040 | tf_op jit(solution)/shard_map/ppermute | solution.py:540
  95.0 1.7 %fusion.5 = bf16[16,8,512]{2,1,0:T(8,128)(2,1)} fusion(bf16[16,8,512]{2,1,0:T(8,128)(2,1)} %collective-permute-done.20, bf16[16,8,512]{2,1,0:T(8,128)(2,1)} %collective-permute-done.19, bf16[16,8,512]{2,1,0:T(8,128)(2,1)S(1)} %collective-permute-done.18, bf16[16,4,8,512]{3,2,1,0:T(8,128)(2,1)S(1)} %bitcast.59, s32[]{:T(128)S(6)} %select_n.165), kind=kLoop, calls=%fused_computation.26 | loop fusion | flops 524288 | bytes 655364 | tf_op jit(solution)/shard_map/convert_element_type | solution.py:547
  96.6 3.5 %all-to-all-start = ((bf16[16,8,512]{2,1,0:T(8,128)(2,1)}), bf16[16,8,512]{2,1,0:T(8,128)(2,1)S(1)}, u32[]{:S(2)}, u32[]{:S(2)}) async-start(bf16[16,8,512]{2,1,0:T(8,128)(2,1)} %fusion.5), calls=%async_computation | async-start | bytes 262144 | tf_op jit(solution)/shard_map/all_to_all | solution.py:547
  100.2 1.6 %collective-permute-done.11 = bf16[306,512]{1,0:T(8,128)(2,1)S(1)} collective-permute-done((bf16[306,512]{1,0:T(8,128)(2,1)S(1)}, bf16[306,512]{1,0:T(8,128)(2,1)S(1)}, u32[]{:S(2)}, u32[]{:S(2)}) %collective-permute-start.11) | collective-permute-done | bytes 313376 | tf_op jit(solution)/shard_map/ppermute | solution.py:540
  102.1 3.6 %collective-permute-start.13 = (bf16[114,512]{1,0:T(8,128)(2,1)S(1)}, bf16[114,512]{1,0:T(8,128)(2,1)S(1)}, u32[]{:S(2)}, u32[]{:S(2)}) collective-permute-start(bf16[114,512]{1,0:T(8,128)(2,1)S(1)} %get-tuple-element.90), channel_id=1, source_target_pairs={{0,2},{1,3},{2,0},{3,1},{4,6},{5,7},{6,4},{7,5},{8,10},{9,11},{10,... | collective-permute-start | bytes 350216 | tf_op jit(solution)/shard_map/ppermute | solution.py:561
  105.7 3.3 %collective-permute-start.15 = (bf16[114,512]{1,0:T(8,128)(2,1)S(1)}, bf16[114,512]{1,0:T(8,128)(2,1)S(1)}, u32[]{:S(2)}, u32[]{:S(2)}) collective-permute-start(bf16[114,512]{1,0:T(8,128)(2,1)S(1)} %get-tuple-element.91), channel_id=1, source_target_pairs={{0,3},{1,0},{2,1},{3,2},{4,7},{5,4},{6,5},{7,6},{8,11},{9,8},{10,9... | collective-permute-start | bytes 350216 | tf_op jit(solution)/shard_map/ppermute | solution.py:561
  109.0 2.3 %collective-permute-done.14 = bf16[114,512]{1,0:T(8,128)(2,1)S(1)} collective-permute-done((bf16[114,512]{1,0:T(8,128)(2,1)S(1)}, bf16[114,512]{1,0:T(8,128)(2,1)S(1)}, u32[]{:S(2)}, u32[]{:S(2)}) %collective-permute-start.14) | collective-permute-done | bytes 116768 | tf_op jit(solution)/shard_map/ppermute | solution.py:561
  111.5 5.1 %collective-permute-start.22 = (bf16[122,512]{1,0:T(8,128)(2,1)S(1)}, bf16[122,512]{1,0:T(8,128)(2,1)S(1)}, u32[]{:S(2)}, u32[]{:S(2)}) collective-permute-start(bf16[122,512]{1,0:T(8,128)(2,1)S(1)} %pad_maximum_fusion.6.mine_ref), channel_id=1, source_target_pairs={{0,128},{128,0},{1,129},{129,1},{2,130},{130,2},{3,131},{131,3},{4... | collective-permute-start | bytes 374792 | tf_op jit(solution)/shard_map/ppermute | solution.py:564
  116.5 5.8 %collective-permute-start.21 = (bf16[122,512]{1,0:T(8,128)(2,1)S(1)}, bf16[122,512]{1,0:T(8,128)(2,1)S(1)}, u32[]{:S(2)}, u32[]{:S(2)}) collective-permute-start(bf16[122,512]{1,0:T(8,128)(2,1)S(1)} %pad_maximum_fusion.6.mine_ref), channel_id=1, source_target_pairs={{0,64},{64,0},{1,65},{65,1},{2,66},{66,2},{3,67},{67,3},{4,68},{68... | collective-permute-start | bytes 374792 | tf_op jit(solution)/shard_map/ppermute | solution.py:563
  122.3 4.6 %collective-permute-start.23 = (bf16[122,512]{1,0:T(8,128)(2,1)S(1)}, bf16[122,512]{1,0:T(8,128)(2,1)S(1)}, u32[]{:S(2)}, u32[]{:S(2)}) collective-permute-start(bf16[122,512]{1,0:T(8,128)(2,1)S(1)} %collective-permute-done.22.across_ref), channel_id=1, source_target_pairs={{0,64},{64,0},{1,65},{65,1},{2,66},{66,2},{3,67},{67,3},{4,68},{68... | collective-permute-start | bytes 374792 | tf_op jit(solution)/shard_map/ppermute | solution.py:565
  127.0 1.0 copy.37
  128.1 1.4 %finish_kernel.1 = (f32[49,512]{1,0:T(8,128)}, f32[1,512]{1,0:T(1,128)}, f32[8,2048]{1,0:T(8,128)}, f32[32,512]{1,0:T(8,128)}, f32[49,512]{1,0:T(8,128)}, /*inde...) custom-call(s32[2]{0:T(128)S(1)} %pad_add_fusion.place_ref, ...), custom_call_target="tpu_custom_call" | custom-call | tf_op jit(solution)/shard_map/finish_kernel/pallas_call | solution.py:416
  (93 shorter events, 13.9 us)
Async XLA Ops:
  0.6 10.5 %copy-start.5 = (bf16[1,4,90,512]{3,1,2,0:T(4,128)(2,1)S(1)}, bf16[1,4,90,512]{3,1,2,0:T(4,128)(2,1)}, u32[]{:S(2)}) copy-start(bf16[1,4,90,512]{3,1,2,0:T(4,128)(2,1)} %param.13) | copy-start | bytes 1105924
  2.3 9.4 %collective-permute-start = (bf16[4,3,640]{2,1,0:T(4,128)(2,1)S(1)}, bf16[4,3,640]{2,1,0:T(4,128)(2,1)S(1)}, u32[]{:S(2)}, u32[]{:S(2)}) collective-permute-start(bf16[4,3,640]{2,1,0:T(4,128)(2,1)S(1)} %maximum_bitcast_fusion), channel_id=1, source_target_pairs={{0,4},{4,8},{8,12},{12,16},{16,20},{20,24},{24,28},{28,32},{32,36}... | collective-permute-start | bytes 46088 | tf_op jit(solution)/shard_map/ppermute | solution.py:452
  4.6 7.1 %collective-permute-start.1 = (bf16[4,3,640]{2,1,0:T(4,128)(2,1)S(1)}, bf16[4,3,640]{2,1,0:T(4,128)(2,1)S(1)}, u32[]{:S(2)}, u32[]{:S(2)}) collective-permute-start(bf16[4,3,640]{2,1,0:T(4,128)(2,1)S(1)} %maximum_bitcast_fusion.1), channel_id=1, source_target_pairs={{0,60},{4,0},{8,4},{12,8},{16,12},{20,16},{24,20},{28,24},{32,28},... | collective-permute-start | bytes 46088 | tf_op jit(solution)/shard_map/ppermute | solution.py:453
  11.6 3.2 %copy-start.6 = (f32[512]{0:T(512)S(1)}, f32[512]{0:T(512)}, u32[]{:S(2)}) copy-start(f32[512]{0:T(512)} %param.21) | copy-start | bytes 6148
  11.6 3.2 %copy-start.7 = (f32[512]{0:T(512)S(1)}, f32[512]{0:T(512)}, u32[]{:S(2)}) copy-start(f32[512]{0:T(512)} %param.17) | copy-start | bytes 6148
  11.6 3.2 %copy-start.3 = (bf16[512,512]{1,0:T(8,128)(2,1)S(1)}, bf16[512,512]{1,0:T(8,128)(2,1)}, u32[]{:S(2)}) copy-start(bf16[512,512]{1,0:T(8,128)(2,1)} %param.25) | copy-start | bytes 1572868
  11.6 3.2 %copy-start.4 = (bf16[512,512]{1,0:T(8,128)(2,1)S(1)}, bf16[512,512]{1,0:T(8,128)(2,1)}, u32[]{:S(2)}) copy-start(bf16[512,512]{1,0:T(8,128)(2,1)} %param.24) | copy-start | bytes 1572868
  11.9 4.2 %collective-permute-start.2 = (bf16[4,96,512]{2,1,0:T(8,128)(2,1)S(1)}, bf16[4,96,512]{2,1,0:T(8,128)(2,1)S(1)}, u32[]{:S(2)}, u32[]{:S(2)}) collective-permute-start(bf16[4,96,512]{2,1,0:T(8,128)(2,1)S(1)} %get-tuple-element.82), channel_id=1, source_target_pairs={{0,64},{64,0},{1,65},{65,1},{2,66},{66,2},{3,67},{67,3},{4,68},{68... | collective-permute-start | bytes 1179656 | tf_op jit(solution)/shard_map/ppermute | solution.py:459
  16.3 10.1 %collective-permute-start.3 = (bf16[2,96,512]{2,1,0:T(8,128)(2,1)S(1)}, bf16[2,96,512]{2,1,0:T(8,128)(2,1)S(1)}, u32[]{:S(2)}, u32[]{:S(2)}) collective-permute-start(bf16[2,96,512]{2,1,0:T(8,128)(2,1)S(1)} %fusion.8), channel_id=1, source_target_pairs={{0,128},{128,0},{1,129},{129,1},{2,130},{130,2},{3,131},{131,3},{4... | collective-permute-start | bytes 589832 | tf_op jit(solution)/shard_map/ppermute | solution.py:463
  26.5 3.5 %collective-permute-start.4 = (bf16[2,96,512]{2,1,0:T(8,128)(2,1)S(1)}, bf16[2,96,512]{2,1,0:T(8,128)(2,1)S(1)}, u32[]{:S(2)}, u32[]{:S(2)}) collective-permute-start(bf16[2,96,512]{2,1,0:T(8,128)(2,1)S(1)} %collective-permute-done.3), channel_id=1, source_target_pairs={{0,64},{64,0},{1,65},{65,1},{2,66},{66,2},{3,67},{67,3},{4,68},{68... | collective-permute-start | bytes 589832 | tf_op jit(solution)/shard_map/ppermute | solution.py:477
  31.6 10.9 %collective-permute-start.5 = (bf16[3,96,512]{2,1,0:T(8,128)(2,1)}, bf16[3,96,512]{2,1,0:T(8,128)(2,1)S(1)}, u32[]{:S(2)}, u32[]{:S(2)}) collective-permute-start(bf16[3,96,512]{2,1,0:T(8,128)(2,1)} %get-tuple-element.96), channel_id=1, source_target_pairs={{0,1},{1,0},{2,3},{3,2},{4,5},{5,4},{6,7},{7,6},{8,9},{9,8},{10,11... | collective-permute-start | bytes 884744 | tf_op jit(solution)/shard_map/ppermute | solution.py:49
  35.2 7.3 %collective-permute-start.6 = (bf16[3,96,512]{2,1,0:T(8,128)(2,1)S(1)}, bf16[3,96,512]{2,1,0:T(8,128)(2,1)S(1)}, u32[]{:S(2)}, u32[]{:S(2)}) collective-permute-start(bf16[3,96,512]{2,1,0:T(8,128)(2,1)S(1)} %get-tuple-element.95), channel_id=1, source_target_pairs={{0,0},{1,2},{2,1},{3,3},{4,4},{5,6},{6,5},{7,7},{8,8},{9,10},{10,9... | collective-permute-start | bytes 884744 | tf_op jit(solution)/shard_map/ppermute | solution.py:50
  36.8 25.0 %collective-permute-start.16 = (bf16[3,96,512]{2,1,0:T(8,128)(2,1)}, bf16[3,96,512]{2,1,0:T(8,128)(2,1)S(1)}, u32[]{:S(2)}, u32[]{:S(2)}) collective-permute-start(bf16[3,96,512]{2,1,0:T(8,128)(2,1)} %get-tuple-element.94), channel_id=1, source_target_pairs={{0,1},{1,0},{2,3},{3,2},{4,5},{5,4},{6,7},{7,6},{8,9},{9,8},{10,11... | collective-permute-start | bytes 884744 | tf_op jit(solution)/shard_map/ppermute | solution.py:49
  39.0 22.7 %collective-permute-start.17 = (bf16[3,96,512]{2,1,0:T(8,128)(2,1)S(1)}, bf16[3,96,512]{2,1,0:T(8,128)(2,1)S(1)}, u32[]{:S(2)}, u32[]{:S(2)}) collective-permute-start(bf16[3,96,512]{2,1,0:T(8,128)(2,1)S(1)} %get-tuple-element.93), channel_id=1, source_target_pairs={{0,0},{1,2},{2,1},{3,3},{4,4},{5,6},{6,5},{7,7},{8,8},{9,10},{10,9... | collective-permute-start | bytes 884744 | tf_op jit(solution)/shard_map/ppermute | solution.py:50
  59.1 21.6 %collective-permute-start.7 = (bf16[1088,512]{1,0:T(8,128)(2,1)}, bf16[1088,512]{1,0:T(8,128)(2,1)}, u32[]{:S(2)}, u32[]{:S(2)}) collective-permute-start(bf16[1088,512]{1,0:T(8,128)(2,1)} %get-tuple-element.42), channel_id=1, source_target_pairs={{0,32},{4,36},{8,40},{12,44},{16,48},{20,52},{24,56},{28,60},{32,0... | collective-permute-start | bytes 3342344 | tf_op jit(solution)/shard_map/ppermute | solution.py:520
  59.1 28.1 %collective-permute-start.8 = (bf16[1088,512]{1,0:T(8,128)(2,1)}, bf16[1088,512]{1,0:T(8,128)(2,1)}, u32[]{:S(2)}, u32[]{:S(2)}) collective-permute-start(bf16[1088,512]{1,0:T(8,128)(2,1)} %get-tuple-element.43), channel_id=1, source_target_pairs={{0,16},{4,20},{8,24},{12,28},{16,32},{20,36},{24,40},{28,44},{32,4... | collective-permute-start | bytes 3342344 | tf_op jit(solution)/shard_map/ppermute | solution.py:520
  60.7 26.5 %collective-permute-start.9 = (bf16[1088,512]{1,0:T(8,128)(2,1)}, bf16[1088,512]{1,0:T(8,128)(2,1)}, u32[]{:S(2)}, u32[]{:S(2)}) collective-permute-start(bf16[1088,512]{1,0:T(8,128)(2,1)} %get-tuple-element.44), channel_id=1, source_target_pairs={{0,48},{4,52},{8,56},{12,60},{16,0},{20,4},{24,8},{28,12},{32,16},... | collective-permute-start | bytes 3342344 | tf_op jit(solution)/shard_map/ppermute | solution.py:520
  61.8 1.0 copy-start.1
  62.8 24.4 %copy-start.2 = (bf16[1088,512]{1,0:T(8,128)(2,1)S(1)}, bf16[1088,512]{1,0:T(8,128)(2,1)}, u32[]{:S(2)}) copy-start(bf16[1088,512]{1,0:T(8,128)(2,1)} %get-tuple-element.41) | copy-start | bytes 3342340
  77.2 15.8 %collective-permute-start.18 = (bf16[16,8,512]{2,1,0:T(8,128)(2,1)S(1)}, bf16[16,8,512]{2,1,0:T(8,128)(2,1)S(1)}, u32[]{:S(2)}, u32[]{:S(2)}) collective-permute-start(bf16[16,8,512]{2,1,0:T(8,128)(2,1)S(1)} %get-tuple-element.87), channel_id=1, source_target_pairs={{0,2},{1,3},{2,0},{3,1},{4,6},{5,7},{6,4},{7,5},{8,10},{9,11},{10,... | collective-permute-start | bytes 393224 | tf_op jit(solution)/shard_map/ppermute | solution.py:546
  80.7 14.3 %collective-permute-start.19 = (bf16[16,8,512]{2,1,0:T(8,128)(2,1)}, bf16[16,8,512]{2,1,0:T(8,128)(2,1)}, u32[]{:S(2)}, u32[]{:S(2)}) collective-permute-start(bf16[16,8,512]{2,1,0:T(8,128)(2,1)} %get-tuple-element.89), channel_id=1, source_target_pairs={{0,1},{1,2},{2,3},{3,0},{4,5},{5,6},{6,7},{7,4},{8,9},{9,10},{10,1... | collective-permute-start | bytes 393224 | tf_op jit(solution)/shard_map/ppermute | solution.py:546
  80.7 14.3 %collective-permute-start.20 = (bf16[16,8,512]{2,1,0:T(8,128)(2,1)S(1)}, bf16[16,8,512]{2,1,0:T(8,128)(2,1)}, u32[]{:S(2)}, u32[]{:S(2)}) collective-permute-start(bf16[16,8,512]{2,1,0:T(8,128)(2,1)S(1)} %get-tuple-element.88), channel_id=1, source_target_pairs={{0,3},{1,0},{2,1},{3,2},{4,7},{5,4},{6,5},{7,6},{8,11},{9,8},{10,9... | collective-permute-start | bytes 393224 | tf_op jit(solution)/shard_map/ppermute | solution.py:546
  90.6 9.6 %collective-permute-start.10 = (bf16[306,512]{1,0:T(8,128)(2,1)S(1)}, bf16[306,512]{1,0:T(8,128)(2,1)S(1)}, u32[]{:S(2)}, u32[]{:S(2)}) collective-permute-start(bf16[306,512]{1,0:T(8,128)(2,1)S(1)} %get-tuple-element.101), channel_id=1, source_target_pairs={{0,8},{4,12},{8,0},{12,4},{16,24},{20,28},{24,16},{28,20},{32,40},... | collective-permute-start | bytes 940040 | tf_op jit(solution)/shard_map/ppermute | solution.py:540
  92.3 9.5 %collective-permute-start.11 = (bf16[306,512]{1,0:T(8,128)(2,1)S(1)}, bf16[306,512]{1,0:T(8,128)(2,1)S(1)}, u32[]{:S(2)}, u32[]{:S(2)}) collective-permute-start(bf16[306,512]{1,0:T(8,128)(2,1)S(1)} %get-tuple-element.102), channel_id=1, source_target_pairs={{0,4},{4,8},{8,12},{12,0},{16,20},{20,24},{24,28},{28,16},{32,36},... | collective-permute-start | bytes 940040 | tf_op jit(solution)/shard_map/ppermute | solution.py:540
  93.0 8.8 %collective-permute-start.12 = (bf16[306,512]{1,0:T(8,128)(2,1)S(1)}, bf16[306,512]{1,0:T(8,128)(2,1)S(1)}, u32[]{:S(2)}, u32[]{:S(2)}) collective-permute-start(bf16[306,512]{1,0:T(8,128)(2,1)S(1)} %get-tuple-element.103), channel_id=1, source_target_pairs={{0,12},{4,0},{8,4},{12,8},{16,28},{20,16},{24,20},{28,24},{32,44},... | collective-permute-start | bytes 940040 | tf_op jit(solution)/shard_map/ppermute | solution.py:540
  96.6 12.3 %all-to-all-start = ((bf16[16,8,512]{2,1,0:T(8,128)(2,1)}), bf16[16,8,512]{2,1,0:T(8,128)(2,1)S(1)}, u32[]{:S(2)}, u32[]{:S(2)}) async-start(bf16[16,8,512]{2,1,0:T(8,128)(2,1)} %fusion.5), calls=%async_computation | async-start | bytes 262144 | tf_op jit(solution)/shard_map/all_to_all | solution.py:547
  102.1 6.9 %collective-permute-start.13 = (bf16[114,512]{1,0:T(8,128)(2,1)S(1)}, bf16[114,512]{1,0:T(8,128)(2,1)S(1)}, u32[]{:S(2)}, u32[]{:S(2)}) collective-permute-start(bf16[114,512]{1,0:T(8,128)(2,1)S(1)} %get-tuple-element.90), channel_id=1, source_target_pairs={{0,2},{1,3},{2,0},{3,1},{4,6},{5,7},{6,4},{7,5},{8,10},{9,11},{10,... | collective-permute-start | bytes 350216 | tf_op jit(solution)/shard_map/ppermute | solution.py:561
  105.7 5.6 %collective-permute-start.14 = (bf16[114,512]{1,0:T(8,128)(2,1)S(1)}, bf16[114,512]{1,0:T(8,128)(2,1)S(1)}, u32[]{:S(2)}, u32[]{:S(2)}) collective-permute-start(bf16[114,512]{1,0:T(8,128)(2,1)S(1)} %get-tuple-element.92), channel_id=1, source_target_pairs={{0,1},{1,2},{2,3},{3,0},{4,5},{5,6},{6,7},{7,4},{8,9},{9,10},{10,1... | collective-permute-start | bytes 350216 | tf_op jit(solution)/shard_map/ppermute | solution.py:561
  105.7 5.6 %collective-permute-start.15 = (bf16[114,512]{1,0:T(8,128)(2,1)S(1)}, bf16[114,512]{1,0:T(8,128)(2,1)S(1)}, u32[]{:S(2)}, u32[]{:S(2)}) collective-permute-start(bf16[114,512]{1,0:T(8,128)(2,1)S(1)} %get-tuple-element.91), channel_id=1, source_target_pairs={{0,3},{1,0},{2,1},{3,2},{4,7},{5,4},{6,5},{7,6},{8,11},{9,8},{10,9... | collective-permute-start | bytes 350216 | tf_op jit(solution)/shard_map/ppermute | solution.py:561
  111.5 10.9 %collective-permute-start.22 = (bf16[122,512]{1,0:T(8,128)(2,1)S(1)}, bf16[122,512]{1,0:T(8,128)(2,1)S(1)}, u32[]{:S(2)}, u32[]{:S(2)}) collective-permute-start(bf16[122,512]{1,0:T(8,128)(2,1)S(1)} %pad_maximum_fusion.6.mine_ref), channel_id=1, source_target_pairs={{0,128},{128,0},{1,129},{129,1},{2,130},{130,2},{3,131},{131,3},{4... | collective-permute-start | bytes 374792 | tf_op jit(solution)/shard_map/ppermute | solution.py:564
  116.5 11.5 %collective-permute-start.21 = (bf16[122,512]{1,0:T(8,128)(2,1)S(1)}, bf16[122,512]{1,0:T(8,128)(2,1)S(1)}, u32[]{:S(2)}, u32[]{:S(2)}) collective-permute-start(bf16[122,512]{1,0:T(8,128)(2,1)S(1)} %pad_maximum_fusion.6.mine_ref), channel_id=1, source_target_pairs={{0,64},{64,0},{1,65},{65,1},{2,66},{66,2},{3,67},{67,3},{4,68},{68... | collective-permute-start | bytes 374792 | tf_op jit(solution)/shard_map/ppermute | solution.py:563
  122.3 5.7 %collective-permute-start.23 = (bf16[122,512]{1,0:T(8,128)(2,1)S(1)}, bf16[122,512]{1,0:T(8,128)(2,1)S(1)}, u32[]{:S(2)}, u32[]{:S(2)}) collective-permute-start(bf16[122,512]{1,0:T(8,128)(2,1)S(1)} %collective-permute-done.22.across_ref), channel_id=1, source_target_pairs={{0,64},{64,0},{1,65},{65,1},{2,66},{66,2},{3,67},{67,3},{4,68},{68... | collective-permute-start | bytes 374792 | tf_op jit(solution)/shard_map/ppermute | solution.py:565
  (1 other events, 0.8 us)
